TPU v7x, 256 devices: a whole 4x4x8 slice. The times are simulated.
256 devices in a mesh: lon: 16 (over z, y_lo), lat: 4 (over y_hi, core), ch: 4 (over x).
Axes of the slice: x: 4, y: 4 (y_hi: 2, y_lo: 2; y = y_hi * 2 + y_lo), z: 8, core: 2. Of those that a mesh axis runs over, the one named last changes fastest.
Arguments:
- features: bfloat16 [96, 384, 2048], P('lat', 'lon', 'ch'), may hold values from -8 to 8
- depth_kernel: float32 [3, 9, 2048], P(None, None, 'ch'), may hold values from -2 to 2
- branch_weight: bfloat16 [5, 2048, 256], P(None, 'ch'), may hold values from -0.1875 to 0.1875
- proj_weight: bfloat16 [5, 256, 256], P(None, 'ch'), may hold values from -0.25 to 0.25
- cotangent: bfloat16 [96, 384, 256], P('lat', 'lon', 'ch'), may hold values from -6 to 6
Outputs:
- mixed: bfloat16 [96, 384, 256], P('lat', 'lon', 'ch')
- grad_features: bfloat16 [96, 384, 2048], P('lat', 'lon', 'ch')
- grad_branch: float32 [5, 2048, 256], P(None, 'ch')
- grad_proj: float32 [5, 256, 256], P(None, 'ch')
- grad_depth: float32 [3, 9, 2048], P(None, None, 'ch')
All inputs are finite; a program needn't handle non-finite values.
Results may differ from a plain program's by a relative error of at most 0.01.
Values may be sent and summed in bfloat16 or wider, within the bound.
No kernel may reach another device: no remote copies, remote signals or barrier semaphores. Data moves between devices by JAX's collectives and lax.ppermute only.
A program may use at most 128 MiB of HBM per device.

v0:
```python
import math

import jax
import jax.numpy as jnp
from jax import lax
from jax.experimental import pallas as pl
from jax.experimental.pallas import tpu as pltpu
from jax.sharding import PartitionSpec as P

dilations = (6, 12, 18)
margin = 18
lead = 24
f32, bf16 = jnp.float32, jnp.bfloat16
GRID = ("lon", "lat")


MIB = 1024 * 1024


def params(size):
    return pltpu.CompilerParams(vmem_limit_bytes=size * MIB)


def smem():
    return pl.BlockSpec(memory_space=pltpu.SMEM)


def vmem():
    return pl.BlockSpec(memory_space=pltpu.VMEM)


def anywhere():
    return pl.BlockSpec(memory_space=pl.ANY)


def stay(value):
    return pltpu.with_memory_space_constraint(value, pltpu.HBM)


def remote():
    return pl.BlockSpec(memory_space=pltpu.HBM)


def by_lanes(*shape, lanes=128):
    return pl.BlockSpec(shape + (lanes,), lambda i: (0,) * len(shape) + (i,))


def whole(*shape):
    return pl.BlockSpec(shape, lambda i: (0,) * len(shape))


def shaped(dtype, *shape):
    return jax.ShapeDtypeStruct(shape, dtype)


def far(dtype, *shape):
    return pltpu.HBM(shape, dtype)


def cost(flops, moved, hard=0):
    return pl.CostEstimate(flops=flops, bytes_accessed=moved, transcendentals=hard)


def window_of(spacing, step_lon):
    base = lead + step_lon * spacing
    return base // 8, base % 8


def roll_rows(value, shift, count):
    if shift:
        value = pltpu.roll(value, value.shape[0] - shift, 0)
    return value[:count]


def pick(value, scalar):
    return pl.multiple_of(value, scalar)


def split_lanes(line):
    return [line[:, 128 * n : 128 * (n + 1)] for n in range(line.shape[1] // 128)]


def edges_body(tile_ref, right_ref, left_ref, sum_ref, packed):
    rows, cols, chan = tile_ref.shape

    def row_step(row, carry):
        line = tile_ref[row].astype(f32)
        for number, block in enumerate(split_lanes(line)):
            place = slice(margin * number, margin * (number + 1))
            packed[0, row, place, :] = block[:margin]
            packed[1, row, place, :] = roll_rows(block, cols - margin, margin)
        return carry + line

    total = lax.fori_loop(0, rows, row_step, jnp.zeros((cols, chan), f32))
    left_ref[...] = packed[0].astype(bf16)
    right_ref[...] = packed[1].astype(bf16)

    @pl.when(pl.program_id(0) == 0)
    def _():
        sum_ref[...] = jnp.zeros_like(sum_ref)

    sum_ref[...] += jnp.sum(total, axis=0, keepdims=True)


def edges(tile):
    rows, cols, chan = tile.shape
    wide = margin * chan // 128
    block = rows // 3
    by_rows = lambda *shape: pl.BlockSpec((block,) + shape, lambda i: (i, 0, 0))
    return pl.pallas_call(
        edges_body,
        grid=(3,),
        in_specs=[by_rows(cols, chan)],
        out_specs=[by_rows(wide, 128), by_rows(wide, 128), whole(1, chan)],
        out_shape=[
            shaped(bf16, rows, wide, 128),
            shaped(bf16, rows, wide, 128),
            shaped(f32, 1, chan),
        ],
        scratch_shapes=[pltpu.VMEM((2, block, wide, 128), f32)],
        compiler_params=params(8),
        cost_estimate=cost(rows * cols * chan, 2_000_000),
        name="edges",
    )(stay(tile))


def corners_body(id_ref, left_ref, right_ref, sum_ref, *refs):
    chip_ref, cross_ref, out_ref = refs[-3:]
    rows = left_ref.shape[0]
    upper = id_ref[1]
    for number, ref in enumerate((left_ref, right_ref)):
        place = slice(margin * number, margin * (number + 1))
        chip_ref[place] = ref[pl.ds((rows - margin) * (1 - upper), margin)]
        cross_ref[place] = ref[pl.ds((rows - margin) * upper, margin)]
    out_ref[...] = sum_ref[...]


def corners(ids, left, right, running, before):
    _, wide, lanes = left.shape
    return pl.pallas_call(
        corners_body,
        in_specs=[smem()] + [vmem()] * 3 + [anywhere()] * len(before),
        out_specs=[vmem()] * 3,
        out_shape=[shaped(bf16, 2 * margin, wide, lanes)] * 2 + [shaped(f32, *running.shape)],
        compiler_params=params(8),
        cost_estimate=cost(1000, 3_000_000),
        name="corners",
    )(ids, left, right, running, *before)


def fill_extended(ext, halos, blocks, upper):
    tile, left, right, chip, cross, chip_corner, cross_corner = halos
    rows, cols, _ = tile.shape
    off, after = lead - margin, lead + cols

    def put(at, row, middle, before, behind, skip=0):
        before, behind = before[row].astype(f32), behind[row + skip].astype(f32)
        for number, block in blocks:
            place = slice(margin * number, margin * (number + 1))
            line = ext(block, at)
            line[lead:after, :] = middle[row, :, 128 * block : 128 * (block + 1)].astype(f32)
            line[off:lead, :] = before[place]
            line[after : after + margin, :] = behind[place]

    def tile_row(row, carry):
        put(margin + row, row, tile, left, right)
        return carry

    chip_first = (margin + rows) * (1 - upper)
    cross_first = (margin + rows) * upper

    def strip_row(row, carry):
        put(chip_first + row, row, chip, chip_corner, chip_corner, margin)
        put(cross_first + row, row, cross, cross_corner, cross_corner, margin)
        return carry

    lax.fori_loop(0, rows, tile_row, 0)
    lax.fori_loop(0, margin, strip_row, 0)


def halo_specs(halos, lanes):
    return [
        by_lanes(*halo.shape[:2], lanes=lanes) if number in (0, 3, 4) else whole(*halo.shape)
        for number, halo in enumerate(halos)
    ]


def fill_taps(taps, kernel_ref):
    for member in range(3):
        for tap in range(9):
            taps[9 * member + tap] = jnp.broadcast_to(
                kernel_ref[member, tap : tap + 1, :], taps.shape[1:]
            )


def pack(row_ref, value, vector):
    size, part = value.shape
    row_ref[...] = jnp.zeros_like(row_ref)
    for number in range(size // 16):
        row_ref[:, part * number : part * (number + 1)] = value[16 * number : 16 * (number + 1)]
    row_ref[0:1, 640 : 640 + vector.shape[1]] = vector
    return row_ref[...].astype(bf16)


def unpack(message, put, part, size, fan):
    for number in range(size // 16):
        put(number, message[:, part * number : part * (number + 1)])
    return message[0:1, 640 : 640 + fan]


def conv_body(
    id_ref, tile_ref, left_ref, right_ref, top_ref, bottom_ref, up_ref, down_ref, kernel_ref,
    weight_ref, pooled_ref, cot_ref,
    inputs_ref, own_ref, one_ref, two_ref, three_ref, own_cot_ref, own_pool_ref,
    ext, cells, taps, total, pool, rows_ref,
):
    step = pl.program_id(0)
    halos = (tile_ref, left_ref, right_ref, top_ref, bottom_ref, up_ref, down_ref)
    rows, cols, _ = tile_ref.shape
    blocks, lanes = 2, 128
    fan = weight_ref.shape[2]

    @pl.when(step == 0)
    def _():
        total[...] = jnp.zeros_like(total)
        pool[...] = jnp.zeros_like(pool)

    fill_taps(taps, kernel_ref)

    for number in range(2):

        @pl.when(step == number)
        def _(number=number):
            fill_extended(
                lambda block, row: ext.at[block, row],
                halos,
                [(blocks * number + block, block) for block in range(blocks)],
                id_ref[1],
            )

    for block in range(blocks):
        across = slice(lanes * block, lanes * (block + 1))

        def conv_rows(pair, carry, block=block, across=across):
            at = (2 * pair, 2 * pair + 1)
            places = [pl.ds(pl.multiple_of(row * cols, 8), cols) for row in at]
            for row, place in zip(at, places):
                cells[0, place, across] = ext[block, margin + row, lead : lead + cols, :]
            for member, spacing in enumerate(dilations):
                summed = [None, None]
                for step_lon in (-1, 0, 1):
                    group, shift = window_of(spacing, step_lon)
                    count = cols // 8 + (shift != 0)
                    part = [None, None]
                    for step_lat in (-1, 0, 1):
                        tap = taps[9 * member + 3 * (step_lat + 1) + step_lon + 1, :, across]
                        for n in (0, 1):
                            window = ext[
                                block,
                                at[n] + margin + step_lat * spacing,
                                8 * group : 8 * (group + count),
                                :,
                            ].reshape(count, 8, lanes)
                            term = window * tap
                            part[n] = term if part[n] is None else part[n] + term
                    for n in (0, 1):
                        piece = roll_rows(part[n].reshape(8 * count, lanes), shift, cols)
                        summed[n] = piece if summed[n] is None else summed[n] + piece
                for n in (0, 1):
                    cells[member + 1, places[n], across] = summed[n]
            return carry

        lax.fori_loop(0, rows // 2, conv_rows, 0)
    for member in range(4):
        block = cells[member].astype(bf16)
        inputs_ref[member] = block
        total[:, fan * member : fan * (member + 1)] += jnp.dot(
            block, weight_ref[member], preferred_element_type=f32
        )
    pool[...] += jnp.dot(
        jnp.broadcast_to(pooled_ref[...], (8, blocks * lanes)),
        weight_ref[4].astype(f32),
        precision=lax.Precision.HIGHEST,
        preferred_element_type=f32,
    )

    @pl.when(step == pl.num_programs(0) - 1)
    def _():
        size = own_ref.shape[0]
        me = id_ref[0]
        band = rows // 4
        part = cot_ref.shape[2]

        def chunk(ahead):
            return total[pl.ds(pl.multiple_of(lax.rem(me + ahead, 4) * size, 16), size), :]

        def cot_chunk(ahead):
            picked = cot_ref[pl.ds(lax.rem(me + ahead, 4) * band, band)]
            return picked.astype(f32).reshape(size, part)

        own_ref[...] = chunk(0)
        own_cot_ref[...] = cot_chunk(0)
        own_pool_ref[...] = pool[0:1, :]
        for ahead, ref in enumerate((one_ref, two_ref, three_ref), 1):
            ref[:size, :] = chunk(ahead).astype(bf16)
            ref[size:, :] = pack(rows_ref, cot_chunk(ahead), pool[0:1, :])


def conv_forward(ids, halos, kernel, weight, pooled, cotangent):
    rows, cols, chan = halos[0].shape
    tall, wide = rows + 2 * margin, cols + 2 * lead
    fan = weight.shape[2]
    lanes = 256
    size = rows * cols // 4
    cells = rows * cols
    part = cotangent.shape[2]
    return pl.pallas_call(
        conv_body,
        grid=(chan // lanes,),
        in_specs=[smem()]
        + halo_specs(halos, lanes)
        + [
            by_lanes(3, 9, lanes=lanes),
            pl.BlockSpec((5, lanes, fan), lambda i: (0, i, 0)),
            by_lanes(1, lanes=lanes),
            whole(*cotangent.shape),
        ],
        out_specs=[by_lanes(4, cells, lanes=lanes), whole(size, 4 * fan)]
        + [whole(size + 16, 4 * fan)] * 3
        + [whole(size, part), whole(1, fan)],
        out_shape=[
            far(bf16, 4, cells, chan),
            far(f32, size, 4 * fan),
        ]
        + [shaped(bf16, size + 16, 4 * fan)] * 3
        + [shaped(f32, size, part), shaped(f32, 1, fan)],
        scratch_shapes=[
            pltpu.VMEM((lanes // 128, tall, wide, 128), f32),
            pltpu.VMEM((4, cells, lanes), f32),
            pltpu.VMEM((27, 8, lanes), f32),
            pltpu.VMEM((cells, 4 * fan), f32),
            pltpu.VMEM((8, fan), f32),
            pltpu.VMEM((16, 4 * fan), f32),
        ],
        compiler_params=params(58),
        cost_estimate=cost(2 * cells * chan * (4 * fan + 27), 20_000_000),
        name="conv_forward",
    )(ids, stay(halos[0]), *halos[1:], kernel, weight, pooled, cotangent)


def slope(value, sig):
    return sig * (1.0 + value * (1.0 - sig))


def proj_body(
    id_ref, own_ref, one_ref, two_ref, three_ref, own_cot_ref, own_pool_ref,
    weight_own, weight_one, weight_two, weight_three, _, last_ref, dpre_ref, send_one_ref, send_two_ref, send_three_ref,
    grad_own_ref, own_mixed_ref, own_sum_ref, pool_ref,
    pre, grads, weights, pieces, cot, rows_ref,
):
    size, part = own_cot_ref.shape
    fan = 4 * part
    me = id_ref[0]
    pre[...] = own_ref[...]
    pool = own_pool_ref[...]
    pieces[me] = own_cot_ref[...]
    for behind, ref in enumerate((one_ref, two_ref, three_ref), 1):
        pre[...] += ref[:size, :].astype(f32)
        origin = lax.rem(me + 4 - behind, 4)

        def put(number, value, origin=origin):
            pieces[origin, 16 * number : 16 * (number + 1), :] = value

        pool = pool + unpack(ref[size:, :].astype(f32), put, part, size, fan)
    for origin in range(4):
        cot[:, part * origin : part * (origin + 1)] = pieces[origin]
    for behind, ref in enumerate((weight_own, weight_one, weight_two, weight_three)):
        first = pl.multiple_of(lax.rem(me + 4 - behind, 4) * part, 16)
        weights[:, pl.ds(first, part), :] = ref[...]
    last_ref[...] = weights[4]

    pool_ref[...] = pool
    pool = jnp.broadcast_to(pool, (8, fan))
    pool_branch = (pool * jax.nn.sigmoid(pool)).astype(bf16)
    proj = jnp.dot(pool_branch, weights[4], preferred_element_type=f32)[0:1, :]
    for member in range(4):
        value = pre[:, fan * member : fan * (member + 1)]
        branch = (value * jax.nn.sigmoid(value)).astype(bf16)
        proj = proj + jnp.dot(branch, weights[member], preferred_element_type=f32)
    sig = jax.nn.sigmoid(proj)
    mixed = (proj * sig).astype(bf16).astype(f32)
    back = (cot[...] * slope(proj, sig)).astype(bf16)
    back_sum = jnp.sum(back.astype(f32), axis=0, keepdims=True)
    own_sum_ref[...] = back_sum
    for target in range(4):
        pieces[target] = mixed[:, part * target : part * (target + 1)]
    own_mixed_ref[...] = pieces[me]
    for member in range(4):
        lanes = slice(fan * member, fan * (member + 1))
        value = pre[:, lanes]
        sig = jax.nn.sigmoid(value)
        branch = (value * sig).astype(bf16)
        grads[member] = lax.dot_general(
            branch, back, (((0,), (0,)), ((), ())), preferred_element_type=f32
        )
        dbranch = lax.dot_general(
            back, weights[member], (((1,), (1,)), ((), ())), preferred_element_type=f32
        )
        dpre = (dbranch * slope(value, sig)).astype(bf16)
        for ref in (dpre_ref, send_one_ref, send_two_ref, send_three_ref):
            ref[:size, lanes] = dpre
        grad_own_ref[member] = grads[member, pl.ds(pl.multiple_of(me * part, 16), part), :]
        for ahead, ref in enumerate((send_one_ref, send_two_ref, send_three_ref), 1):
            first = pl.multiple_of(lax.rem(me + ahead, 4) * part, 16)
            ref[size + 16 :, lanes] = grads[member, pl.ds(first, part), :].astype(bf16)
    for ahead, ref in enumerate((send_one_ref, send_two_ref, send_three_ref), 1):
        ref[size : size + 16, :] = pack(rows_ref, pieces[lax.rem(me + ahead, 4)], back_sum)


def project(ids, own, others, own_cot, own_pool, weights, before):
    size, wide = own.shape
    fan = wide // 4
    part = fan // 4
    return pl.pallas_call(
        proj_body,
        in_specs=[smem()] + [vmem()] * 10 + [anywhere()],
        out_specs=[vmem()] * 9,
        out_shape=[shaped(bf16, fan, fan), shaped(bf16, size, wide)]
        + [shaped(bf16, size + 16 + part, wide)] * 3
        + [shaped(f32, 4, part, fan)]
        + [shaped(f32, size, part), shaped(f32, 1, fan), shaped(f32, 1, fan)],
        scratch_shapes=[
            pltpu.VMEM((size, wide), f32),
            pltpu.VMEM((4, fan, fan), f32),
            pltpu.VMEM((5, fan, fan), bf16),
            pltpu.VMEM((4, size, part), f32),
            pltpu.VMEM((size, fan), f32),
            pltpu.VMEM((16, wide), f32),
        ],
        compiler_params=params(16),
        cost_estimate=cost(6 * size * wide * fan, 4_000_000, 2 * size * wide),
        name="project",
    )(ids, stay(own), *others, own_cot, own_pool, *weights, before)


def weight_body(
    id_ref, own_ref, gp_ref, own_sum_ref, one_ref, two_ref, three_ref, inputs_ref,
    keep_ref, give_ref, full_ref, total_ref, sum_ref,
):
    size = own_ref.shape[0]
    fan = keep_ref.shape[2]
    me, upper = id_ref[0], id_ref[1]
    others = (one_ref, two_ref, three_ref)
    full_ref[pl.ds(pl.multiple_of(me * size, 16), size), :] = own_ref[...]
    for behind, ref in enumerate(others, 1):
        first = pl.multiple_of(lax.rem(me + 4 - behind, 4) * size, 16)
        full_ref[pl.ds(first, size), :] = ref[:size, :]

    def grad(member):
        lanes = pl.ds(pl.multiple_of(member * fan, 256), fan)
        return lax.dot_general(
            inputs_ref[member],
            full_ref[:, lanes],
            (((0,), (0,)), ((), ())),
            preferred_element_type=f32,
        )

    for number in range(2):
        give_ref[number] = grad(2 * (1 - upper) + number).astype(bf16)
        keep_ref[number] = grad(2 * upper + number)
    for member in range(4):
        value = gp_ref[member]
        for ref in others:
            value = value + ref[size + 16 :, fan * member : fan * (member + 1)].astype(f32)
        total_ref[member] = value
    total = own_sum_ref[...]
    for ref in others:
        total = total + ref[size : size + 16, 640 : 640 + fan].astype(f32)[0:1]
    sum_ref[...] = total


def weight_grads(ids, own, gp_own, own_sum, others, inputs):
    size, wide = own.shape
    fan = wide // 4
    part = fan // 4
    _, cells, chan = inputs.shape
    return pl.pallas_call(
        weight_body,
        in_specs=[smem()] + [vmem()] * 7,
        out_specs=[vmem()] * 5,
        out_shape=[
            shaped(f32, 2, chan, fan),
            shaped(bf16, 2, chan, fan),
            shaped(bf16, cells, wide),
            shaped(f32, 4, part, fan),
            shaped(f32, 1, fan),
        ],
        compiler_params=params(20),
        cost_estimate=cost(2 * cells * chan * wide, 6_000_000),
        name="weight_grads",
    )(ids, own, gp_own, own_sum, *others, stay(inputs))


def unpack_body(id_ref, own_mixed_ref, one_ref, two_ref, three_ref, mixed_ref, pieces):
    size, part = own_mixed_ref.shape
    me = id_ref[0]
    pieces[me] = own_mixed_ref[...]
    for behind, ref in enumerate((one_ref, two_ref, three_ref), 1):
        origin = lax.rem(me + 4 - behind, 4)

        def put(number, value, origin=origin):
            pieces[origin, 16 * number : 16 * (number + 1), :] = value

        unpack(ref[...].astype(f32), put, part, size, 4 * part)
    mixed_ref[...] = pieces[...].astype(bf16)


def unpack_mixed(ids, own_mixed, others):
    size, part = own_mixed.shape
    rows = pl.BlockSpec((16, others[0].shape[1]), lambda i: (size // 16, 0))
    return pl.pallas_call(
        unpack_body,
        grid=(1,),
        in_specs=[smem(), whole(size, part)] + [rows] * 3,
        out_specs=whole(4, size, part),
        out_shape=shaped(bf16, 4, size, part),
        scratch_shapes=[pltpu.VMEM((4, size, part), f32)],
        compiler_params=params(8),
        cost_estimate=cost(100_000, 500_000),
        name="unpack_mixed",
    )(ids, own_mixed, *[stay(value) for value in others])


placed = {}
for _member in range(3):
    for _step in (-1, 0, 1):
        _key = (_member, window_of(dilations[_member], _step)[1])
        placed.setdefault(_key, len(placed))


def shift_rows(shifted, source, rows, cols, lanes):
    def row_step(row, carry):
        place = pl.ds(pl.multiple_of(row * cols, 8), cols)
        for member in range(3):
            value = source(member, place)
            wide = jnp.concatenate([value, jnp.zeros((8, lanes), f32)], axis=0)
            for (owner, shift), number in placed.items():
                if owner != member:
                    continue
                shifted[number, row] = pltpu.roll(wide, shift, 0) if shift else wide
        return carry

    lax.fori_loop(0, rows, row_step, 0)


def scatter_body(
    id_ref, dpre_ref, weight_ref, kernel_ref, _,
    grad_ref, center_ref, left_ref, right_ref, chip_ref, cross_corner, cross_center, token_ref,
    taps, first, grads, shifted, strips,
):
    rows, cols, across_all = center_ref.shape
    lanes = 128
    fan = weight_ref.shape[2]
    wide = cols + 2 * margin
    groups = (cols + 2 * lead) // 8
    off = lead - margin
    fill_taps(taps, kernel_ref)
    token_ref[...] = jnp.zeros_like(token_ref)
    for member in range(4):
        piece = lax.dot_general(
            dpre_ref[:, fan * member : fan * (member + 1)],
            weight_ref[member],
            (((1,), (1,)), ((), ())),
            preferred_element_type=f32,
        )
        if member == 0:
            first[...] = piece
        else:
            piece = piece.astype(bf16)
            grad_ref[member - 1] = piece
            grads[member - 1] = piece.astype(f32)

    for block in range(across_all // lanes):
        across = slice(lanes * block, lanes * (block + 1))
        shift_rows(
            shifted,
            lambda member, place, across=across: grads[member, place, across],
            rows,
            cols,
            lanes,
        )
        for begin in range(0, rows + 2 * margin, 6):
            active = [
                (member, step_lat)
                for member, spacing in enumerate(dilations)
                for step_lat in (-1, 0, 1)
                if margin + step_lat * spacing <= begin < margin + rows + step_lat * spacing
            ]
            inside = margin <= begin < margin + rows

            def ext_rows(at, begin=begin, active=active, inside=inside, across=across):
                sums = [[None] * groups, [None] * groups]
                for n in (0, 1):
                    if inside:
                        value = first[pl.ds(pl.multiple_of((at[n] - margin) * cols, 8), cols), across]
                        for number in range(cols // 8):
                            sums[n][lead // 8 + number] = value[8 * number : 8 * (number + 1)]
                for member, step_lat in active:
                    spacing = dilations[member]
                    for step_lon in (-1, 0, 1):
                        group, shift = window_of(spacing, step_lon)
                        count = cols // 8 + (shift != 0)
                        weight = taps[9 * member + 3 * (step_lat + 1) + step_lon + 1, :, across]
                        for n in (0, 1):
                            grad = shifted[
                                placed[member, shift],
                                at[n] - margin - step_lat * spacing,
                                : 8 * count,
                                :,
                            ]
                            for number in range(count):
                                term = grad[8 * number : 8 * (number + 1)] * weight
                                old = sums[n][group + number]
                                sums[n][group + number] = term if old is None else old + term
                for n in (0, 1):
                    parts = [jnp.zeros((8, lanes), f32) if s is None else s for s in sums[n]]
                    center = jnp.concatenate(parts[lead // 8 : (lead + cols) // 8], axis=0)
                    left = roll_rows(jnp.concatenate(parts[: lead // 8], axis=0), off, margin)
                    right = jnp.concatenate(parts[(lead + cols) // 8 :], axis=0)[:margin]
                    if inside:
                        row = at[n] - margin
                        center_ref[row, :, across] = center.astype(bf16)
                        left_ref[row, :, across] = left.astype(bf16)
                        right_ref[row, :, across] = right.astype(bf16)
                    else:
                        side = int(begin >= margin)
                        row = at[n] - side * (margin + rows)
                        strips[side, row, :cols, across] = center
                        strips[side, row, cols : cols + margin, across] = left
                        strips[side, row, cols + margin : wide, across] = right

            if inside:

                def step_rows(step, carry, begin=begin, ext_rows=ext_rows):
                    ext_rows((begin + 2 * step, begin + 2 * step + 1))
                    return carry

                lax.fori_loop(0, 3, step_rows, 0)
            else:
                for step in range(3):
                    ext_rows((begin + 2 * step, begin + 2 * step + 1))

    for upper in (0, 1):

        @pl.when(id_ref[1] == upper)
        def _(upper=upper):
            for row in range(margin):
                chip_ref[row] = strips[1 - upper, row, :wide, :].astype(bf16)
                cross_corner[row] = strips[upper, row, cols:wide, :].astype(bf16)
                cross_center[row] = strips[upper, row, :cols, :].astype(bf16)


def scatter_grads(ids, dpre, weight, kernel, rows, cols, before):
    cells, wide_fan = dpre.shape
    fan = wide_fan // 4
    chan = weight.shape[1]
    wide = cols + 2 * margin
    lanes = 256
    return pl.pallas_call(
        scatter_body,
        grid=(chan // lanes,),
        in_specs=[
            smem(),
            whole(cells, wide_fan),
            pl.BlockSpec((4, lanes, fan), lambda i: (0, i, 0)),
            by_lanes(3, 9, lanes=lanes),
            anywhere(),
        ],
        out_specs=[
            by_lanes(3, cells, lanes=lanes),
            by_lanes(rows, cols, lanes=lanes),
            by_lanes(rows, margin, lanes=lanes),
            by_lanes(rows, margin, lanes=lanes),
        ]
        + [by_lanes(margin, wide, lanes=lanes)]
        + [by_lanes(margin, 2 * margin, lanes=lanes), by_lanes(margin, cols, lanes=lanes)]
        + [whole(8, 128)],
        out_shape=[
            far(bf16, 3, cells, chan),
            far(bf16, rows, cols, chan),
            far(bf16, rows, margin, chan),
            far(bf16, rows, margin, chan),
        ]
        + [shaped(bf16, margin, wide, chan)]
        + [shaped(bf16, margin, 2 * margin, chan), shaped(bf16, margin, cols, chan)]
        + [shaped(f32, 8, 128)],
        scratch_shapes=[
            pltpu.VMEM((27, 8, lanes), f32),
            pltpu.VMEM((cells, lanes), f32),
            pltpu.VMEM((3, cells, lanes), f32),
            pltpu.VMEM((len(placed), rows, cols + 8, 128), f32),
            pltpu.VMEM((2, margin, cols + 2 * lead - 8, lanes), f32),
        ],
        compiler_params=params(24),
        cost_estimate=cost(2 * cells * chan * (wide_fan + 27), 15_000_000),
        name="scatter_grads",
    )(ids, dpre, weight, kernel, before)


def extend_body(
    id_ref, tile_ref, left_ref, right_ref, top_ref, bottom_ref, up_ref, down_ref, _, ext_ref, token_ref, ext
):
    halos = (tile_ref, left_ref, right_ref, top_ref, bottom_ref, up_ref, down_ref)
    ext[...] = jnp.zeros_like(ext)
    token_ref[...] = jnp.zeros_like(token_ref)
    blocks = ext.shape[0]
    fill_extended(
        lambda block, row: ext.at[block, row],
        halos,
        [(block, block) for block in range(blocks)],
        id_ref[1],
    )

    def copy_rows(row, carry):
        for block in range(blocks):
            ext_ref[row, :, 128 * block : 128 * (block + 1)] = ext[block, row].astype(bf16)
        return carry

    lax.fori_loop(0, ext.shape[1], copy_rows, 0)


def extend(ids, halos, before):
    rows, cols, chan = halos[0].shape
    tall, wide = rows + 2 * margin, cols + 2 * lead + 8
    return pl.pallas_call(
        extend_body,
        in_specs=[smem()] + [vmem()] * 7 + [anywhere()],
        out_specs=[vmem()] * 2,
        out_shape=[far(bf16, tall, wide, chan), shaped(f32, 8, 128)],
        scratch_shapes=[pltpu.VMEM((chan // 128, tall, wide, 128), f32)],
        compiler_params=params(36),
        cost_estimate=cost(1_000_000, 10_000_000),
        name="extend",
    )(ids, *[stay(halo) for halo in halos], before)


def taps_body(grad_ref, ext_ref, sum_ref, tap_ref, ext, grads, shifted):
    step = pl.program_id(0)
    tall, wide, lanes = ext_ref.shape
    rows, cols = tall - 2 * margin, wide - 2 * lead - 8
    per = sum_ref.shape[1] // lanes
    first = 32 * (step // per)
    place = pl.ds(pl.multiple_of(lanes * lax.rem(step, per), 128), lanes)

    def widen_row(row, carry):
        ext[row] = ext_ref[row].astype(f32)
        return carry

    lax.fori_loop(0, tall, widen_row, 0, unroll=4)
    grads[...] = grad_ref[...].astype(f32)
    shift_rows(shifted, lambda member, place: grads[member, place, :], rows, cols, lanes)

    def tap_row(row, carry):
        sums = list(carry)
        for member, spacing in enumerate(dilations):
            for step_lon in (-1, 0, 1):
                group, shift = window_of(spacing, step_lon)
                count = cols // 8 + (shift != 0)
                grad = shifted[placed[member, shift], row, : 8 * count, :].reshape(count, 8, lanes)
                for step_lat in (-1, 0, 1):
                    window = ext[
                        row + margin + step_lat * spacing, 8 * group : 8 * (group + count), :
                    ].reshape(count, 8, lanes)
                    tap = 9 * member + 3 * (step_lat + 1) + step_lon + 1
                    sums[tap] = sums[tap] + jnp.sum(grad * window, axis=0)
        return tuple(sums)

    sums = lax.fori_loop(0, rows, tap_row, (jnp.zeros((8, lanes), f32),) * 27)
    rows_of = [jnp.sum(value, axis=0, keepdims=True) for value in sums]
    rows_of.append(sum_ref[:, place])
    rows_of += [jnp.zeros((1, lanes), f32)] * 4
    tap_ref[pl.ds(pl.multiple_of(first, 32), 32), place] = jnp.concatenate(rows_of, axis=0)


def tap_sums(grads, extended, back_sum):
    tall, wide, chan = extended.shape
    _, cells, _ = grads.shape
    rows, cols = tall - 2 * margin, wide - 2 * lead - 8
    lanes = 128
    shape = (32 * chan // back_sum.shape[1], back_sum.shape[1])
    return pl.pallas_call(
        taps_body,
        grid=(chan // lanes,),
        in_specs=[by_lanes(3, cells), by_lanes(tall, wide), whole(*back_sum.shape)],
        out_specs=whole(*shape),
        out_shape=shaped(f32, *shape),
        scratch_shapes=[
            pltpu.VMEM((tall, wide, lanes), f32),
            pltpu.VMEM((3, cells, lanes), f32),
            pltpu.VMEM((len(placed), rows, cols + 8, lanes), f32),
        ],
        compiler_params=params(20),
        cost_estimate=cost(2 * cells * chan * 27, 15_000_000),
        name="tap_sums",
    )(stay(grads), stay(extended), back_sum)


def home_body(
    id_ref, left_ref, right_ref, chip_ref, corner_ref, left_out, right_out, packed, line
):
    rows, _, _ = left_ref.shape
    wide = chip_ref.shape[1]
    cols = wide - 2 * margin
    shifted = rows - margin

    def one_row(row, refs):
        left, right = left_ref[row].astype(f32), right_ref[row].astype(f32)
        for ref, first, number in refs:
            line[number, cols - ref.shape[1] + 2 * margin :, :] = ref[row - first].astype(f32)
            left = left + line[number, cols : cols + margin, :]
            right = right + line[number, cols + margin :, :]
        for number, (one, two) in enumerate(zip(split_lanes(left), split_lanes(right))):
            place = slice(margin * number, margin * (number + 1))
            packed[0, row, place, :] = one
            packed[1, row, place, :] = two

    for upper in (0, 1):
        pieces = [(chip_ref, shifted * (1 - upper), 0), (corner_ref, shifted * upper, 1)]
        cuts = sorted({0, rows} | {at for _, first, _ in pieces for at in (first, first + margin)})

        @pl.when(id_ref[1] == upper)
        def _(pieces=pieces, cuts=cuts):
            for first, last in zip(cuts, cuts[1:]):
                refs = [piece for piece in pieces if piece[1] <= first < piece[1] + margin]

                def step(number, carry, first=first, refs=refs):
                    one_row(first + number, refs)
                    return carry

                lax.fori_loop(0, last - first, step, 0)

    left_out[...] = packed[0].astype(bf16)
    right_out[...] = packed[1].astype(bf16)


def home(ids, left, right, chip, corner):
    rows, _, chan = left.shape
    wide = margin * chan // 128
    return pl.pallas_call(
        home_body,
        in_specs=[smem()] + [vmem()] * 4,
        out_specs=[vmem()] * 2,
        out_shape=[shaped(bf16, rows, wide, 128)] * 2,
        scratch_shapes=[
            pltpu.VMEM((2, rows, wide, 128), f32),
            pltpu.VMEM((2, chip.shape[1], chan), f32),
        ],
        compiler_params=params(16),
        cost_estimate=cost(rows * margin * chan, 5_000_000),
        name="home",
    )(ids, stay(left), stay(right), chip, corner)


def middle_body(id_ref, center_ref, chip_ref, cross_ref, out_ref):
    rows, cols, _ = center_ref.shape
    shifted = rows - margin
    upper = id_ref[1]

    def copy_row(row, carry):
        out_ref[row] = center_ref[row].astype(f32)
        return carry

    def chip_row(row, carry):
        out_ref[shifted * (1 - upper) + row] += chip_ref[row].astype(f32)[:cols]
        return carry

    def cross_row(row, carry):
        out_ref[shifted * upper + row] += cross_ref[row].astype(f32)
        return carry

    lax.fori_loop(0, rows, copy_row, 0)
    lax.fori_loop(0, margin, chip_row, 0)
    lax.fori_loop(0, margin, cross_row, 0)


def middle(ids, center, chip, cross):
    rows, cols, chan = center.shape
    return pl.pallas_call(
        middle_body,
        grid=(chan // 128,),
        in_specs=[
            smem(),
            by_lanes(rows, cols),
            by_lanes(*chip.shape[:2]),
            by_lanes(*cross.shape[:2]),
        ],
        out_specs=by_lanes(rows, cols),
        out_shape=shaped(f32, rows, cols, chan),
        compiler_params=params(12),
        cost_estimate=cost(rows * cols * chan, 4_000_000),
        name="middle",
    )(ids, stay(center), stay(chip), stay(cross))


def finish_body(center_ref, left_ref, right_ref, pooled_ref, out_ref, pads):
    rows, cols, chan = center_ref.shape
    base = pooled_ref[...]

    @pl.when(pl.program_id(0) == 0)
    def _():
        pads[...] = jnp.zeros_like(pads)

    def row_step(row, carry):
        left, right = left_ref[row].astype(f32), right_ref[row].astype(f32)
        for number in range(chan // 128):
            place = slice(margin * number, margin * (number + 1))
            across = slice(128 * number, 128 * (number + 1))
            pads[0, row, :margin, across] = left[place]
            pads[1, row, cols - margin :, across] = right[place]
        return carry

    lax.fori_loop(0, rows, row_step, 0)

    def add_row(row, carry):
        out_ref[row] = (center_ref[row] + pads[0, row] + pads[1, row] + base).astype(bf16)
        return carry

    lax.fori_loop(0, rows, add_row, 0)


def finish(center, left, right, pooled):
    rows, cols, chan = center.shape
    wide = margin * chan // 128
    block = rows // 3
    by_rows = lambda *shape: pl.BlockSpec((block,) + shape, lambda i: (i, 0, 0))
    return pl.pallas_call(
        finish_body,
        grid=(3,),
        in_specs=[by_rows(cols, chan), by_rows(wide, 128), by_rows(wide, 128), whole(1, chan)],
        out_specs=by_rows(cols, chan),
        out_shape=shaped(bf16, rows, cols, chan),
        scratch_shapes=[pltpu.VMEM((2, block, cols, chan), f32)],
        compiler_params=params(10),
        cost_estimate=cost(rows * cols * chan, 4_000_000),
        name="finish",
    )(center, left, right, pooled)


def core_body(id_ref, keep_ref, got_ref, gp_ref, own_ref, one_ref, two_ref, three_ref, token_ref):
    token_ref[...] = jnp.zeros_like(token_ref)
    fan = keep_ref.shape[1]
    rows = own_ref.shape[0] - gp_ref.shape[1]
    here = id_ref[2]
    for code, ref in enumerate((own_ref, one_ref, two_ref, three_ref)):
        target = here ^ code
        place = pl.ds(pl.multiple_of(target * rows, 16), rows)
        ref[:rows, :] = (keep_ref[place, :] + got_ref[place, :].astype(f32)).astype(ref.dtype)
        ref[rows:, :] = gp_ref[target].astype(ref.dtype)


def core_stage(ids, keep, got, gp):
    rows, fan = keep.shape
    part = gp.shape[1]
    size = rows // 4 + part
    return pl.pallas_call(
        core_body,
        in_specs=[smem()] + [vmem()] * 3,
        out_specs=[vmem()] * 5,
        out_shape=[shaped(f32, size, fan)] + [shaped(bf16, size, fan)] * 3 + [shaped(f32, 8, 128)],
        compiler_params=params(12),
        cost_estimate=cost(rows * fan, 3_000_000),
        name="core_stage",
    )(ids, keep, got, gp)


def y_body(id_ref, own_ref, one_ref, two_ref, three_ref, _, keep_ref, give_ref, total):
    half, _ = keep_ref.shape
    upper = id_ref[3]
    total[...] = (
        own_ref[...] + one_ref[...].astype(f32) + two_ref[...].astype(f32) + three_ref[...].astype(f32)
    )
    keep_ref[...] = total[pl.ds(pl.multiple_of(upper * half, 16), half), :]
    give_ref[...] = total[pl.ds(pl.multiple_of((1 - upper) * half, 16), half), :].astype(bf16)


def y_stage(ids, own, others, before):
    size, fan = own.shape
    return pl.pallas_call(
        y_body,
        in_specs=[smem()] + [vmem()] * 4 + [anywhere()],
        out_specs=[vmem()] * 2,
        out_shape=[shaped(f32, size // 2, fan), shaped(bf16, size // 2, fan)],
        scratch_shapes=[pltpu.VMEM((size, fan), f32)],
        compiler_params=params(8),
        cost_estimate=cost(size * fan, 1_000_000),
        name="y_stage",
    )(ids, own, *others, before)


def gather_body(id_ref, own_ref, extra_ref, one_ref, two_ref, three_ref, out_ref, sum_ref):
    size = own_ref.shape[0]
    here = id_ref[2]
    total = extra_ref[...]
    out_ref[pl.ds(pl.multiple_of(here * size, 16), size), :] = own_ref[...]
    for code, ref in enumerate((one_ref, two_ref, three_ref), 1):
        place = pl.ds(pl.multiple_of((here ^ code) * size, 16), size)
        out_ref[place, :] = ref[:size, :]
        total = total + ref[size:, :].astype(f32)
    out_ref[4 * size :, :] = total.astype(bf16)
    sum_ref[...] = total


def y_gather(ids, own, extra, others):
    size, fan = own.shape
    count = extra.shape[0]
    return pl.pallas_call(
        gather_body,
        in_specs=[smem()] + [vmem()] * 5,
        out_specs=[vmem()] * 2,
        out_shape=[shaped(bf16, 4 * size + count, fan), shaped(f32, count, fan)],
        compiler_params=params(8),
        cost_estimate=cost(size * fan, 2_000_000),
        name="y_gather",
    )(ids, own, extra, *others)


def last_body(
    id_ref, own_ref, got_ref, own_extra_ref, got_extra_ref, weight_ref, proj_ref, pool_ref, pooled_ref,
    branch_ref, grad_proj_ref, depth_ref, dpooled_ref, dpool, column, *, cells,
):
    highest = lax.Precision.HIGHEST
    _, chan, lanes = branch_ref.shape
    part = grad_proj_ref.shape[1]
    fan = 4 * part
    scale = 1.0 / math.sqrt(cells)
    me, upper = id_ref[0], id_ref[1]
    step = pl.program_id(0)
    size = chan // 2 + part
    top = lax.broadcasted_iota(jnp.int32, (8, lanes), 0) == 0

    def outer(column_of, row_of):
        return lax.dot_general(
            column_of,
            jnp.where(top, row_of, 0.0),
            (((0,), (0,)), ((), ())),
            precision=highest,
            preferred_element_type=f32,
        )

    @pl.when(step == 0)
    def _():
        extra = own_extra_ref[...] + got_extra_ref[4 * size :, :].astype(f32)
        for number in range(chan // fan):
            for tap in range(27):
                row = 32 * number + tap
                depth_ref[tap // 9, tap % 9 : tap % 9 + 1, fan * number : fan * (number + 1)] = (
                    extra[row : row + 1] * scale
                )
        back_sum = jnp.broadcast_to(extra[27:28], (8, fan))
        pool = jnp.broadcast_to(pool_ref[...], (8, fan))
        sig = jax.nn.sigmoid(pool)
        full = slope(pool, sig) * lax.dot_general(
            back_sum,
            proj_ref[...].astype(f32),
            (((1,), (1,)), ((), ())),
            precision=highest,
            preferred_element_type=f32,
        )
        dpooled = lax.dot_general(
            full,
            weight_ref[0].astype(f32),
            (((1,), (1,)), ((), ())),
            precision=highest,
            preferred_element_type=f32,
        )
        dpooled_ref[...] = dpooled[0:1] * (1.0 / cells)
        pool_branch = (pool * sig).astype(bf16).astype(f32)
        for number in range(fan // lanes):
            dpool[0, number] = full[:, lanes * number : lanes * (number + 1)]
            dpool[1, number] = back_sum[:, lanes * number : lanes * (number + 1)]
        for origin in range(4):
            column[origin] = pool_branch[:, part * origin : part * (origin + 1)]

    for number in range(4):
        first = size * number
        rows = slice(chan // 2 * (number % 2), chan // 2 * (number % 2 + 1))
        for ref, half in ((own_ref, upper), (got_ref, 1 - upper)):
            branch_ref[2 * half + number // 2, rows, :] = (
                ref[first : first + chan // 2, :].astype(f32) * scale
            )
        both = own_ref[first + chan // 2 : first + size, :].astype(f32)
        both = both + got_ref[first + chan // 2 : first + size, :].astype(f32)
        grad_proj_ref[number] = both * scale
    branch_ref[4] = outer(jnp.broadcast_to(pooled_ref[...], (8, chan)), dpool[0, step]) * scale
    grad_proj_ref[4] = outer(column[me], dpool[1, step]) * scale


def last_stage(ids, own, got, extra, weight, proj, pool_pre, pooled, cells):
    _, chan, fan = weight.shape
    part = fan // 4
    return pl.pallas_call(
        lambda *refs: last_body(*refs, cells=cells),
        grid=(fan // 128,),
        in_specs=[
            smem(),
            by_lanes(own.shape[0]),
            by_lanes(got.shape[0]),
            whole(*extra.shape),
            whole(*got.shape),
            pl.BlockSpec((1, chan, fan), lambda i: (4, 0, 0)),
            whole(*proj.shape),
            whole(*pool_pre.shape),
            whole(*pooled.shape),
        ],
        out_specs=[by_lanes(5, chan), by_lanes(5, part), whole(3, 9, chan), whole(1, chan)],
        out_shape=[
            shaped(f32, 5, chan, fan),
            shaped(f32, 5, part, fan),
            shaped(f32, 3, 9, chan),
            shaped(f32, 1, chan),
        ],
        scratch_shapes=[
            pltpu.VMEM((2, fan // 128, 8, 128), f32),
            pltpu.VMEM((4, 8, part), f32),
        ],
        compiler_params=params(18),
        cost_estimate=cost(8 * chan * fan, 5_000_000),
        name="last_stage",
    )(ids, own, got, extra, got, weight, proj, pool_pre, pooled)


def shift(value, axis, ahead, closed=True):
    count = lax.axis_size(axis)
    pairs = [
        (i, (i + ahead) % count) for i in range(count) if closed or 0 <= i + ahead < count
    ]
    return lax.ppermute(value, axis, pairs)


def to_partner(value):
    count = lax.axis_size("lat")
    return lax.ppermute(value, "lat", [(i, i ^ 1) for i in range(count)])


def to_other_chip(value):
    count = lax.axis_size("lat")
    pairs = [(i, i + 1) for i in range(1, count - 1, 2)]
    return lax.ppermute(value, "lat", pairs + [(j, i) for i, j in pairs])


def place_in_grid():
    return lax.axis_index("lon") * lax.axis_size("lat") + lax.axis_index("lat")


def swap(value, mask):
    count = lax.axis_size("lon") * lax.axis_size("lat")
    return lax.ppermute(value, GRID, [(i, i ^ mask) for i in range(count)])


def has(mask):
    return (place_in_grid() & mask) != 0


def number_in(bits):
    return sum(has(bit).astype(jnp.int32) << at for at, bit in enumerate(bits))


def mask_of(bits, code):
    return sum(bit for at, bit in enumerate(bits) if (code >> at) & 1)


def grid_sum(value):
    mask = 1
    while mask < lax.axis_size("lon") * lax.axis_size("lat"):
        value = value + swap(value, mask)
        mask *= 2
    return value


core_bit, y_bits = 1, (4, 2)


def z_bits():
    bits, mask = [], 8
    while mask < lax.axis_size("lon") * lax.axis_size("lat"):
        bits.append(mask)
        mask *= 2
    return bits


def per_device(features, depth_kernel, branch_weight, proj_weight, cotangent):
    rows, cols, chan = features.shape
    fan = branch_weight.shape[2]
    part = proj_weight.shape[1]
    cell_count = rows * cols * lax.axis_size("lat") * lax.axis_size("lon")
    me = lax.axis_index("ch")
    flag = lambda mask: has(mask).astype(jnp.int32)
    ids = jnp.stack(
        [me.astype(jnp.int32), flag(core_bit), number_in(y_bits), flag(z_bits()[0])]
    )
    tie = lax.optimization_barrier

    to_right, to_left, colsum = edges(features)
    left = shift(to_right, "lon", 1)
    right = shift(to_left, "lon", -1)

    proj_others = [shift(proj_weight, "ch", d) for d in (1, 2, 3)]
    pooled = colsum.reshape(chan // 128, 128)
    bits = z_bits()
    pooled = pooled + swap(pooled, core_bit)
    pooled, tile = tie((pooled, features))
    rest = rows - margin
    first = jnp.where(has(core_bit), rest, 0)
    cross = to_other_chip(lax.dynamic_slice_in_dim(tile, first, margin))
    chip = to_partner(lax.dynamic_slice_in_dim(tile, rest - first, margin))
    for mask in [bits[0], bits[2], y_bits[0]]:
        pooled = pooled + swap(pooled, mask)
    chip_corner, cross_corner, pooled = corners(ids, left, right, pooled, (chip, cross))
    cross_corner = to_other_chip(cross_corner)
    chip_corner = to_partner(chip_corner)
    for mask in [bits[1], y_bits[1]]:
        pooled = pooled + swap(pooled, mask)
    pooled = pooled.reshape(1, chan) / cell_count

    halos = (features, left, right, chip, cross, chip_corner, cross_corner)
    inputs, own, *ahead, own_cot, own_pool = conv_forward(
        ids, halos, depth_kernel, branch_weight, pooled, cotangent
    )
    ahead, proj_others = tie((ahead, proj_others))
    extended, token = extend(ids, halos, own_pool)
    others = [shift(value, "ch", d) for d, value in enumerate(ahead, 1)]
    proj_last, dpre, *sent, gp_own, own_mixed, own_sum, pool_pre = project(
        ids, own, others, own_cot, own_pool, [proj_weight, *proj_others], token
    )
    others = [shift(value, "ch", d) for d, value in enumerate(sent, 1)]
    keep, give, dpre_full, gp, back_sum = weight_grads(ids, dpre, gp_own, own_sum, others, inputs)
    mixed = unpack_mixed(ids, own_mixed, others)

    got = swap(give.reshape(2 * chan, fan), core_bit)
    big, *send, token = core_stage(ids, keep.reshape(2 * chan, fan), got, gp)
    taken = [swap(value, mask_of(y_bits, code)) for code, value in enumerate(send, 1)]
    grads, center, mid_left, mid_right, *strips, token = scatter_grads(
        ids, dpre_full, branch_weight, depth_kernel, rows, cols, token
    )
    big, give = y_stage(ids, big, taken, token)
    strips, give = tie((strips, give))
    strips = [to_partner(strips[0])] + [to_other_chip(value) for value in strips[1:]]
    extra = tap_sums(grads, extended, back_sum)
    to_left, to_right = home(ids, mid_left, mid_right, *strips[:2])
    center = middle(ids, center, strips[0], strips[2])
    for number, mask in enumerate(bits):
        got = swap(give, mask).astype(f32)
        big = big + got
        if number + 1 < len(bits):
            upper = has(bits[number + 1])
            half = big.shape[0] // 2
            give = jnp.where(upper, big[:half], big[half:]).astype(bf16)
            big = jnp.where(upper, big[half:], big[:half])
        if number == 1:
            give, to_left, to_right = tie((give, to_left, to_right))

    from_left = shift(to_right, "lon", 1)
    from_right = shift(to_left, "lon", -1)
    big, from_left, from_right, center, mixed = tie((big, from_left, from_right, center, mixed))

    sent = jnp.concatenate([big, extra]).astype(bf16)
    for number, mask in enumerate(bits[::-1]):
        got = swap(sent, mask)
        size = got.shape[0] - extra.shape[0]
        extra = extra + got[size:].astype(f32)
        big = sent[:size]
        big = jnp.where(
            has(mask),
            jnp.concatenate([got[:size], big]),
            jnp.concatenate([big, got[:size]]),
        )
        sent = jnp.concatenate([big, extra.astype(bf16)])
    taken = [swap(sent, mask_of(y_bits, code)) for code in (1, 2, 3)]
    half, extra = y_gather(ids, big, extra, taken)
    got = swap(half, core_bit)
    grad_branch, grad_proj, grad_depth, dpooled = last_stage(
        ids, half, got, extra, branch_weight, proj_last, pool_pre, pooled, cell_count
    )
    grad_features = finish(center, from_left, from_right, dpooled)
    return (mixed.reshape(rows, cols, part), grad_features, grad_branch, grad_proj, grad_depth)


def solution(mesh):
    return jax.shard_map(
        per_device,
        mesh=mesh,
        in_specs=(
            P("lat", "lon", "ch"),
            P(None, None, "ch"),
            P(None, "ch", None),
            P(None, "ch", None),
            P("lat", "lon", "ch"),
        ),
        out_specs=(
            P("lat", "lon", "ch"),
            P("lat", "lon", "ch"),
            P(None, "ch", None),
            P(None, "ch", None),
            P(None, None, "ch"),
        ),
        check_vma=False,
    )
```

profile of v0, /device:TPU:1, one launch (start us, length us, event | category | flops | bytes accessed | tf_op | source)
XLA Modules:
  0.0 208.9 jit_solution(17653613742666308590)
XLA Ops:
  0.6 2.2 %edges.1 = (bf16[24,72,128]{2,1,0:T(8,128)(2,1)S(1)}, bf16[24,72,128]{2,1,0:T(8,128)(2,1)S(1)}, f32[1,512]{1,0:T(1,128)S(1)}) custom-call(bf16[24,24,512]{2,1,0:T(8,128)(2,1)} %tile_ref.5), custom_call_target="tpu_custom_call" | custom-call | flops 294912 | bytes 2000000 | tf_op jit(solution)/shard_map/edges/pallas_call | solution.py:110
  2.8 3.3 %collective-permute-start.2 = (f32[4,128]{1,0:T(4,128)S(1)}, f32[4,128]{1,0:T(4,128)S(1)}, u32[]{:S(2)}, u32[]{:S(2)}) collective-permute-start(f32[4,128]{1,0:T(4,128)S(1)} %bitcast.12), channel_id=1, source_target_pairs={{0,4},{4,0},{8,12},{12,8},{16,20},{20,16},{24,28},{28,24},{32,36},... | collective-permute-start | bytes 6152 | tf_op jit(solution)/shard_map/ppermute | solution.py:1157
  6.1 4.9 %collective-permute-start.1 = (bf16[24,72,128]{2,1,0:T(8,128)(2,1)S(1)}, bf16[24,72,128]{2,1,0:T(8,128)(2,1)S(1)}, u32[]{:S(2)}, u32[]{:S(2)}) collective-permute-start(bf16[24,72,128]{2,1,0:T(8,128)(2,1)S(1)} %get-tuple-element.78), channel_id=1, source_target_pairs={{0,240},{16,0},{32,16},{48,32},{64,48},{80,64},{96,80},{112,96},{1... | collective-permute-start | bytes 1327112 | tf_op jit(solution)/shard_map/ppermute | solution.py:1137
  11.0 2.0 constant_dynamic-slice_fusion
  13.0 5.0 %collective-permute-start.4 = (bf16[18,24,512]{2,1,0:T(8,128)(2,1)}, bf16[18,24,512]{2,1,0:T(8,128)(2,1)S(1)}, u32[]{:S(2)}, u32[]{:S(2)}) collective-permute-start(bf16[18,24,512]{2,1,0:T(8,128)(2,1)} %get-tuple-element.156), channel_id=1, source_target_pairs={{4,8},{8,4},{5,9},{9,5},{6,10},{10,6},{7,11},{11,7},{20,24},{24,20... | collective-permute-start | bytes 1327112 | tf_op jit(solution)/shard_map/ppermute | solution.py:1148
  18.2 2.7 %collective-permute-done.5 = f32[4,128]{1,0:T(4,128)S(1)} collective-permute-done((f32[4,128]{1,0:T(4,128)S(1)}, f32[4,128]{1,0:T(4,128)S(1)}, u32[]{:S(2)}, u32[]{:S(2)}) %collective-permute-start.5) | collective-permute-done | bytes 2080 | tf_op jit(solution)/shard_map/ppermute | solution.py:1157
  20.9 4.4 %collective-permute-start.6 = (f32[4,128]{1,0:T(4,128)S(1)}, f32[4,128]{1,0:T(4,128)S(1)}, u32[]{:S(2)}, u32[]{:S(2)}) collective-permute-start(f32[4,128]{1,0:T(4,128)S(1)} %add.60), channel_id=1, source_target_pairs={{0,128},{4,132},{8,136},{12,140},{16,144},{20,148},{24,152},{28,15... | collective-permute-start | bytes 6152 | tf_op jit(solution)/shard_map/ppermute | solution.py:1157
  25.3 2.0 collective-permute-done.6
  27.3 4.9 %collective-permute-done.7 = f32[4,128]{1,0:T(4,128)S(1)} collective-permute-done((f32[4,128]{1,0:T(4,128)S(1)}, f32[4,128]{1,0:T(4,128)S(1)}, u32[]{:S(2)}, u32[]{:S(2)}) %collective-permute-start.7) | collective-permute-done | bytes 2080 | tf_op jit(solution)/shard_map/ppermute | solution.py:1157
  34.0 4.1 %collective-permute-start.9 = (bf16[36,72,128]{2,1,0:T(8,128)(2,1)S(1)}, bf16[36,72,128]{2,1,0:T(8,128)(2,1)S(1)}, u32[]{:S(2)}, u32[]{:S(2)}) collective-permute-start(bf16[36,72,128]{2,1,0:T(8,128)(2,1)S(1)} %get-tuple-element.83), channel_id=1, source_target_pairs={{4,8},{8,4},{5,9},{9,5},{6,10},{10,6},{7,11},{11,7},{20,24},{24,20... | collective-permute-start | bytes 1990664 | tf_op jit(solution)/shard_map/ppermute | solution.py:1148
  38.1 2.6 %collective-permute-start.10 = (f32[4,128]{1,0:T(4,128)S(1)}, f32[4,128]{1,0:T(4,128)S(1)}, u32[]{:S(2)}, u32[]{:S(2)}) collective-permute-start(f32[4,128]{1,0:T(4,128)S(1)} %get-tuple-element.84), channel_id=1, source_target_pairs={{0,64},{4,68},{8,72},{12,76},{16,80},{20,84},{24,88},{28,92},{32,9... | collective-permute-start | bytes 6152 | tf_op jit(solution)/shard_map/ppermute | solution.py:1157
  41.7 2.8 %collective-permute-start.13 = (bf16[5,64,256]{2,1,0:T(8,128)(2,1)S(1)}, bf16[5,64,256]{2,1,0:T(8,128)(2,1)S(1)}, u32[]{:S(2)}, u32[]{:S(2)}) collective-permute-start(bf16[5,64,256]{2,1,0:T(8,128)(2,1)S(1)} %copy-done.10), channel_id=1, source_target_pairs={{0,2},{1,3},{2,0},{3,1},{4,6},{5,7},{6,4},{7,5},{8,10},{9,11},{10,... | collective-permute-start | bytes 491528 | tf_op jit(solution)/shard_map/ppermute | solution.py:1137
  45.8 2.5 %collective-permute-start.14 = (bf16[5,64,256]{2,1,0:T(8,128)(2,1)S(1)}, bf16[5,64,256]{2,1,0:T(8,128)(2,1)S(1)}, u32[]{:S(2)}, u32[]{:S(2)}) collective-permute-start(bf16[5,64,256]{2,1,0:T(8,128)(2,1)S(1)} %copy-done.10), channel_id=1, source_target_pairs={{0,3},{1,0},{2,1},{3,2},{4,7},{5,4},{6,5},{7,6},{8,11},{9,8},{10,9... | collective-permute-start | bytes 491528 | tf_op jit(solution)/shard_map/ppermute | solution.py:1137
  49.9 9.5 %conv_forward.1 = (bf16[4,576,512]{2,1,0:T(8,128)(2,1)}, f32[144,1024]{1,0:T(8,128)}, bf16[160,1024]{1,0:T(8,128)(2,1)}, bf16[160,1024]{1,0:T(8,128)(2,1)}, bf16...) custom-call(s32[4]{0:T(128)} %copy-done.11, bf16[24,24,512]{2,1,0:T(8,128)(2,1)} %tile_ref.5, ...), custom_call_target="tpu_custom_call" | custom-call | flops 619905024 | bytes 20000000 | tf_op jit(solution)/shard_map/conv_forward/pallas_call | solution.py:317
  59.5 2.1 %collective-permute-start.16 = (bf16[160,1024]{1,0:T(8,128)(2,1)}, bf16[160,1024]{1,0:T(8,128)(2,1)S(1)}, u32[]{:S(2)}, u32[]{:S(2)}) collective-permute-start(bf16[160,1024]{1,0:T(8,128)(2,1)} %get-tuple-element.90), channel_id=1, source_target_pairs={{0,2},{1,3},{2,0},{3,1},{4,6},{5,7},{6,4},{7,5},{8,10},{9,11},{10,... | collective-permute-start | bytes 983048 | tf_op jit(solution)/shard_map/ppermute | solution.py:1137
  64.2 6.6 %extend.1 = (bf16[60,80,512]{2,1,0:T(8,128)(2,1)}, f32[8,128]{1,0:T(8,128)S(1)}) custom-call(s32[4]{0:T(128)S(1)} %copy-done.12, bf16[24,24,512]{2,1,0:T(8,128)(2,1)} %tile_ref.5, bf16[24,72,128]{2,1,0:T(8,128)(2,1)} %copy-done.2, bf16[24,72,128]{2,1,0:T(8,128)(2,1)} %copy-done.3, bf16[18,24,512]{2,1,0:T(8,128)(2,1)} %copy-done.5, ...), custom_call_target="tpu_custom_call" | custom-call | flops 1000000 | bytes 10000000 | tf_op jit(solution)/shard_map/extend/pallas_call | solution.py:735
  70.8 3.6 %collective-permute-done.16.two_ref = bf16[160,1024]{1,0:T(8,128)(2,1)S(1)} collective-permute-done((bf16[160,1024]{1,0:T(8,128)(2,1)}, bf16[160,1024]{1,0:T(8,128)(2,1)S(1)}, u32[]{:S(2)}, u32[]{:S(2)}) %collective-permute-start.16) | collective-permute-done | bytes 327712 | tf_op jit(solution)/shard_map/ppermute | solution.py:1137
  74.4 2.9 %collective-permute-done.17.three_ref = bf16[160,1024]{1,0:T(8,128)(2,1)S(1)} collective-permute-done((bf16[160,1024]{1,0:T(8,128)(2,1)}, bf16[160,1024]{1,0:T(8,128)(2,1)S(1)}, u32[]{:S(2)}, u32[]{:S(2)}) %collective-permute-start.17) | collective-permute-done | bytes 327712 | tf_op jit(solution)/shard_map/ppermute | solution.py:1137
  77.3 2.1 %project.1 = (bf16[256,256]{1,0:T(8,128)(2,1)S(1)}, bf16[144,1024]{1,0:T(8,128)(2,1)S(1)}, bf16[224,1024]{1,0:T(8,128)(2,1)S(1)}, bf16[224,1024]{1,0:T(8,128)(2,...) custom-call(s32[4]{0:T(128)S(1)} %copy-done.12, ...), custom_call_target="tpu_custom_call" | custom-call | flops 226492416 | bytes 4000000 | tf_op jit(solution)/shard_map/project/pallas_call | solution.py:424
  80.1 1.4 collective-permute-start.18
  81.5 3.1 %collective-permute-start.19 = (bf16[224,1024]{1,0:T(8,128)(2,1)S(1)}, bf16[224,1024]{1,0:T(8,128)(2,1)S(1)}, u32[]{:S(2)}, u32[]{:S(2)}) collective-permute-start(bf16[224,1024]{1,0:T(8,128)(2,1)S(1)} %get-tuple-element.102), channel_id=1, source_target_pairs={{0,2},{1,3},{2,0},{3,1},{4,6},{5,7},{6,4},{7,5},{8,10},{9,11},{10,... | collective-permute-start | bytes 1376264 | tf_op jit(solution)/shard_map/ppermute | solution.py:1137
  84.5 8.6 %collective-permute-done.18.one_ref = bf16[224,1024]{1,0:T(8,128)(2,1)S(1)} collective-permute-done((bf16[224,1024]{1,0:T(8,128)(2,1)S(1)}, bf16[224,1024]{1,0:T(8,128)(2,1)S(1)}, u32[]{:S(2)}, u32[]{:S(2)}) %collective-permute-start.18) | collective-permute-done | bytes 458784 | tf_op jit(solution)/shard_map/ppermute | solution.py:1137
  93.1 11.4 %collective-permute-done.19.two_ref = bf16[224,1024]{1,0:T(8,128)(2,1)S(1)} collective-permute-done((bf16[224,1024]{1,0:T(8,128)(2,1)S(1)}, bf16[224,1024]{1,0:T(8,128)(2,1)S(1)}, u32[]{:S(2)}, u32[]{:S(2)}) %collective-permute-start.19) | collective-permute-done | bytes 458784 | tf_op jit(solution)/shard_map/ppermute | solution.py:1137
  104.5 3.1 %weight_grads.1 = (f32[2,512,256]{2,1,0:T(8,128)S(1)}, bf16[2,512,256]{2,1,0:T(8,128)(2,1)S(1)}, bf16[576,1024]{1,0:T(8,128)(2,1)S(1)}, f32[4,64,256]{2,1,0:T(8,128)S(1)}, f32[1,256]{1,0:T(1,128)S(1)}) custom-call(s32[4]{0:T(128)S(1)} %copy-done.12, bf16[144,1024]{1,0:T(8,128)(2,1)S(1)} %get-tuple-element.98.own_ref, ...), custom_call_target="tpu_custom_call" | custom-call | flops 603979776 | bytes 6000000 | tf_op jit(solution)/shard_map/weight_grads/pallas_call | solution.py:487
  107.7 1.4 collective-permute-start.21
  109.1 1.5 collective-permute-done.21.got_ref
  111.4 3.5 %collective-permute-start.23 = (bf16[320,256]{1,0:T(8,128)(2,1)S(1)}, bf16[320,256]{1,0:T(8,128)(2,1)S(1)}, u32[]{:S(2)}, u32[]{:S(2)}) collective-permute-start(bf16[320,256]{1,0:T(8,128)(2,1)S(1)} %get-tuple-element.110), channel_id=1, source_target_pairs={{0,8},{4,12},{8,0},{12,4},{16,24},{20,28},{24,16},{28,20},{32,40},... | collective-permute-start | bytes 491528 | tf_op jit(solution)/shard_map/ppermute | solution.py:1157
  115.3 8.1 %scatter_grads.1 = (bf16[3,576,512]{2,1,0:T(8,128)(2,1)}, bf16[24,24,512]{2,1,0:T(8,128)(2,1)}, bf16[24,18,512]{2,1,0:T(8,128)(2,1)}, bf16[24,18,512]{2,1,0:T(8,...) custom-call(s32[4]{0:T(128)S(1)} %copy-done.12, ...), custom_call_target="tpu_custom_call" | custom-call | flops 619905024 | bytes 15000000 | tf_op jit(solution)/shard_map/scatter_grads/pallas_call | solution.py:669
  128.8 3.1 %collective-permute-start.28 = (bf16[18,36,512]{2,1,0:T(8,128)(2,1)}, bf16[18,36,512]{2,1,0:T(8,128)(2,1)S(1)}, u32[]{:S(2)}, u32[]{:S(2)}) collective-permute-start(bf16[18,36,512]{2,1,0:T(8,128)(2,1)} %copy-done.19), channel_id=1, source_target_pairs={{4,8},{8,4},{5,9},{9,5},{6,10},{10,6},{7,11},{11,7},{20,24},{24,20... | collective-permute-start | bytes 1990664 | tf_op jit(solution)/shard_map/ppermute | solution.py:1148
  133.6 3.0 %collective-permute-start.26 = (bf16[80,256]{1,0:T(8,128)(2,1)S(1)}, bf16[80,256]{1,0:T(8,128)(2,1)S(1)}, u32[]{:S(2)}, u32[]{:S(2)}) collective-permute-start(bf16[80,256]{1,0:T(8,128)(2,1)S(1)} %select_convert_fusion), channel_id=1, source_target_pairs={{0,64},{4,68},{8,72},{12,76},{16,80},{20,84},{24,88},{28,92},{32,9... | collective-permute-start | bytes 122888 | tf_op jit(solution)/shard_map/ppermute | solution.py:1157
  136.6 4.2 %collective-permute-start.32 = (bf16[18,24,512]{2,1,0:T(8,128)(2,1)}, bf16[18,24,512]{2,1,0:T(8,128)(2,1)S(1)}, u32[]{:S(2)}, u32[]{:S(2)}) collective-permute-start(bf16[18,24,512]{2,1,0:T(8,128)(2,1)} %copy-done.20), channel_id=1, source_target_pairs={{4,8},{8,4},{5,9},{9,5},{6,10},{10,6},{7,11},{11,7},{20,24},{24,20... | collective-permute-start | bytes 1327112 | tf_op jit(solution)/shard_map/ppermute | solution.py:1148
  141.8 1.5 collective-permute-done.28.corner_ref
  143.3 2.4 %home.1 = (bf16[24,72,128]{2,1,0:T(8,128)(2,1)S(1)}, bf16[24,72,128]{2,1,0:T(8,128)(2,1)S(1)}) custom-call(s32[4]{0:T(128)S(1)} %copy-done.13, bf16[24,18,512]{2,1,0:T(8,128)(2,1)} %get-tuple-element.121.left_ref, bf16[24,18,512]{2,1,0:T(8,128)(2,1)} %get-tuple-element.122.right_ref, bf16[18,60,512]{2,1,0:T(8,128)(2,1)S(1)} %collective-permute-done.27.chip_ref, ...), custom_call_target="tpu_custom_call" | custom-call | flops 221184 | bytes 5000000 | tf_op jit(solution)/shard_map/home/pallas_call | solution.py:849
  145.8 3.9 %collective-permute-start.31 = (bf16[24,72,128]{2,1,0:T(8,128)(2,1)S(1)}, bf16[24,72,128]{2,1,0:T(8,128)(2,1)S(1)}, u32[]{:S(2)}, u32[]{:S(2)}) collective-permute-start(bf16[24,72,128]{2,1,0:T(8,128)(2,1)S(1)} %get-tuple-element.129), channel_id=1, source_target_pairs={{0,240},{16,0},{32,16},{48,32},{64,48},{80,64},{96,80},{112,96},{1... | collective-permute-start | bytes 1327112 | tf_op jit(solution)/shard_map/ppermute | solution.py:1137
  149.7 5.7 %collective-permute-start.29 = (bf16[40,256]{1,0:T(8,128)(2,1)S(1)}, bf16[40,256]{1,0:T(8,128)(2,1)S(1)}, u32[]{:S(2)}, u32[]{:S(2)}) collective-permute-start(bf16[40,256]{1,0:T(8,128)(2,1)S(1)} %select_convert_fusion.1), channel_id=1, source_target_pairs={{0,128},{4,132},{8,136},{12,140},{16,144},{20,148},{24,152},{28,15... | collective-permute-start | bytes 61448 | tf_op jit(solution)/shard_map/ppermute | solution.py:1157
  155.4 1.6 unpack_mixed.1
  156.9 7.5 %tap_sums.1 = f32[64,256]{1,0:T(8,128)S(1)} custom-call(bf16[3,576,512]{2,1,0:T(8,128)(2,1)} %get-tuple-element.138.grad_ref, bf16[60,80,512]{2,1,0:T(8,128)(2,1)} %get-tuple-element.139.ext_ref, f32[1,256]{1,0:T(1,128)S(1)} %get-tuple-element.140.sum_ref), custom_call_target="tpu_custom_call" | custom-call | flops 15925248 | bytes 15000000 | tf_op jit(solution)/shard_map/tap_sums/pallas_call | solution.py:791
  165.2 3.6 %middle.1.center_ref = f32[24,24,512]{2,1,0:T(8,128)S(1)} custom-call(s32[4]{0:T(128)S(1)} %copy-done.13, bf16[24,24,512]{2,1,0:T(8,128)(2,1)} %get-tuple-element.130.center_ref, bf16[18,60,512]{2,1,0:T(8,128)(2,1)} %copy-done.1, bf16[18,24,512]{2,1,0:T(8,128)(2,1)} %copy-done.24), custom_call_target="tpu_custom_call" | custom-call | flops 294912 | bytes 4000000 | tf_op jit(solution)/shard_map/middle/pallas_call | solution.py:888
  168.9 3.5 %collective-permute-start.33 = (bf16[104,256]{1,0:T(8,128)(2,1)S(1)}, bf16[104,256]{1,0:T(8,128)(2,1)S(1)}, u32[]{:S(2)}, u32[]{:S(2)}) collective-permute-start(bf16[104,256]{1,0:T(8,128)(2,1)S(1)} %pad_maximum_fusion.3), channel_id=1, source_target_pairs={{0,128},{4,132},{8,136},{12,140},{16,144},{20,148},{24,152},{28,15... | collective-permute-start | bytes 159752 | tf_op jit(solution)/shard_map/ppermute | solution.py:1157
  172.3 3.8 %collective-permute-done.33 = bf16[104,256]{1,0:T(8,128)(2,1)S(1)} collective-permute-done((bf16[104,256]{1,0:T(8,128)(2,1)S(1)}, bf16[104,256]{1,0:T(8,128)(2,1)S(1)}, u32[]{:S(2)}, u32[]{:S(2)}) %collective-permute-start.33) | collective-permute-done | bytes 53280 | tf_op jit(solution)/shard_map/ppermute | solution.py:1157
  176.3 6.3 %collective-permute-done.34 = bf16[144,256]{1,0:T(8,128)(2,1)S(1)} collective-permute-done((bf16[144,256]{1,0:T(8,128)(2,1)S(1)}, bf16[144,256]{1,0:T(8,128)(2,1)S(1)}, u32[]{:S(2)}, u32[]{:S(2)}) %collective-permute-start.34) | collective-permute-done | bytes 73760 | tf_op jit(solution)/shard_map/ppermute | solution.py:1157
  182.7 4.2 %collective-permute-done.35 = bf16[224,256]{1,0:T(8,128)(2,1)S(1)} collective-permute-done((bf16[224,256]{1,0:T(8,128)(2,1)S(1)}, bf16[224,256]{1,0:T(8,128)(2,1)S(1)}, u32[]{:S(2)}, u32[]{:S(2)}) %collective-permute-start.35) | collective-permute-done | bytes 114720 | tf_op jit(solution)/shard_map/ppermute | solution.py:1157
  188.2 2.2 %collective-permute-start.36 = (bf16[384,256]{1,0:T(8,128)(2,1)S(1)}, bf16[384,256]{1,0:T(8,128)(2,1)S(1)}, u32[]{:S(2)}, u32[]{:S(2)}) collective-permute-start(bf16[384,256]{1,0:T(8,128)(2,1)S(1)} %pad_maximum_fusion), channel_id=1, source_target_pairs={{0,16},{4,20},{8,24},{12,28},{16,0},{20,4},{24,8},{28,12},{32,48},... | collective-permute-start | bytes 589832 | tf_op jit(solution)/shard_map/ppermute | solution.py:1157
  190.4 8.5 %collective-permute-done.38.three_ref = bf16[384,256]{1,0:T(8,128)(2,1)S(1)} collective-permute-done((bf16[384,256]{1,0:T(8,128)(2,1)S(1)}, bf16[384,256]{1,0:T(8,128)(2,1)S(1)}, u32[]{:S(2)}, u32[]{:S(2)}) %collective-permute-start.38) | collective-permute-done | bytes 196640 | tf_op jit(solution)/shard_map/ppermute | solution.py:1157
  199.5 1.7 collective-permute-start.39
  201.2 1.8 collective-permute-done.39.refs_2_.refs_4_
  203.0 3.5 %last_stage.1 = (f32[5,512,256]{2,1,0:T(8,128)}, f32[5,64,256]{2,1,0:T(8,128)}, f32[3,9,512]{2,1,0:T(8,128)S(1)}, f32[1,512]{1,0:T(1,128)S(1)}) custom-call(s32[4]{0:T(128)S(1)} %copy-done.13, bf16[1344,256]{1,0:T(8,128)(2,1)S(1)} %get-tuple-element.141.refs_1_, bf16[1344,256]{1,0:T(8,128)(2,1)S(1)} %collective-permute-done.39.refs_2_.refs_4_, ...), custom_call_target="tpu_custom_call" | custom-call | flops 1048576 | bytes 5000000 | tf_op jit(solution)/shard_map/last_stage/pallas_call | solution.py:1101
  207.1 1.8 finish.1
  (129 shorter events, 21.7 us)
Async XLA Ops:
  2.8 8.2 %collective-permute-start.2 = (f32[4,128]{1,0:T(4,128)S(1)}, f32[4,128]{1,0:T(4,128)S(1)}, u32[]{:S(2)}, u32[]{:S(2)}) collective-permute-start(f32[4,128]{1,0:T(4,128)S(1)} %bitcast.12), channel_id=1, source_target_pairs={{0,4},{4,0},{8,12},{12,8},{16,20},{20,16},{24,28},{28,24},{32,36},... | collective-permute-start | bytes 6152 | tf_op jit(solution)/shard_map/ppermute | solution.py:1157
  6.1 26.1 %collective-permute-start = (bf16[24,72,128]{2,1,0:T(8,128)(2,1)S(1)}, bf16[24,72,128]{2,1,0:T(8,128)(2,1)S(1)}, u32[]{:S(2)}, u32[]{:S(2)}) collective-permute-start(bf16[24,72,128]{2,1,0:T(8,128)(2,1)S(1)} %get-tuple-element.77), channel_id=1, source_target_pairs={{0,16},{16,32},{32,48},{48,64},{64,80},{80,96},{96,112},{112,128},... | collective-permute-start | bytes 1327112 | tf_op jit(solution)/shard_map/ppermute | solution.py:1137
  6.1 26.1 %collective-permute-start.1 = (bf16[24,72,128]{2,1,0:T(8,128)(2,1)S(1)}, bf16[24,72,128]{2,1,0:T(8,128)(2,1)S(1)}, u32[]{:S(2)}, u32[]{:S(2)}) collective-permute-start(bf16[24,72,128]{2,1,0:T(8,128)(2,1)S(1)} %get-tuple-element.78), channel_id=1, source_target_pairs={{0,240},{16,0},{32,16},{48,32},{64,48},{80,64},{96,80},{112,96},{1... | collective-permute-start | bytes 1327112 | tf_op jit(solution)/shard_map/ppermute | solution.py:1137
  13.0 28.8 %copy-start.10 = (bf16[5,64,256]{2,1,0:T(8,128)(2,1)S(1)}, bf16[5,64,256]{2,1,0:T(8,128)(2,1)}, u32[]{:S(2)}) copy-start(bf16[5,64,256]{2,1,0:T(8,128)(2,1)} %weight_own.1) | copy-start | bytes 491524
  13.0 31.9 %copy-start.25 = (f32[3,9,512]{2,0,1:T(4,128)S(1)}, f32[3,9,512]{2,0,1:T(4,128)}, u32[]{:S(2)}) copy-start(f32[3,9,512]{2,0,1:T(4,128)} %param.6) | copy-start | bytes 165892
  13.0 20.0 %collective-permute-start.4 = (bf16[18,24,512]{2,1,0:T(8,128)(2,1)}, bf16[18,24,512]{2,1,0:T(8,128)(2,1)S(1)}, u32[]{:S(2)}, u32[]{:S(2)}) collective-permute-start(bf16[18,24,512]{2,1,0:T(8,128)(2,1)} %get-tuple-element.156), channel_id=1, source_target_pairs={{4,8},{8,4},{5,9},{9,5},{6,10},{10,6},{7,11},{11,7},{20,24},{24,20... | collective-permute-start | bytes 1327112 | tf_op jit(solution)/shard_map/ppermute | solution.py:1148
  18.0 15.0 %collective-permute-start.3 = (bf16[18,24,512]{2,1,0:T(8,128)(2,1)S(1)}, bf16[18,24,512]{2,1,0:T(8,128)(2,1)S(1)}, u32[]{:S(2)}, u32[]{:S(2)}) collective-permute-start(bf16[18,24,512]{2,1,0:T(8,128)(2,1)S(1)} %get-tuple-element.157), channel_id=1, source_target_pairs={{0,4},{4,0},{8,12},{12,8},{1,5},{5,1},{9,13},{13,9},{2,6},{6,2},{1... | collective-permute-start | bytes 1327112 | tf_op jit(solution)/shard_map/ppermute | solution.py:1142
  18.1 2.8 %collective-permute-start.5 = (f32[4,128]{1,0:T(4,128)S(1)}, f32[4,128]{1,0:T(4,128)S(1)}, u32[]{:S(2)}, u32[]{:S(2)}) collective-permute-start(f32[4,128]{1,0:T(4,128)S(1)} %add.58), channel_id=1, source_target_pairs={{0,32},{4,36},{8,40},{12,44},{16,48},{20,52},{24,56},{28,60},{32,0... | collective-permute-start | bytes 6152 | tf_op jit(solution)/shard_map/ppermute | solution.py:1157
  20.9 6.3 %collective-permute-start.6 = (f32[4,128]{1,0:T(4,128)S(1)}, f32[4,128]{1,0:T(4,128)S(1)}, u32[]{:S(2)}, u32[]{:S(2)}) collective-permute-start(f32[4,128]{1,0:T(4,128)S(1)} %add.60), channel_id=1, source_target_pairs={{0,128},{4,132},{8,136},{12,140},{16,144},{20,148},{24,152},{28,15... | collective-permute-start | bytes 6152 | tf_op jit(solution)/shard_map/ppermute | solution.py:1157
  27.2 5.0 %collective-permute-start.7 = (f32[4,128]{1,0:T(4,128)S(1)}, f32[4,128]{1,0:T(4,128)S(1)}, u32[]{:S(2)}, u32[]{:S(2)}) collective-permute-start(f32[4,128]{1,0:T(4,128)S(1)} %add.61), channel_id=1, source_target_pairs={{0,16},{4,20},{8,24},{12,28},{16,0},{20,4},{24,8},{28,12},{32,48},... | collective-permute-start | bytes 6152 | tf_op jit(solution)/shard_map/ppermute | solution.py:1157
  27.3 21.5 %copy-start.11 = (s32[4]{0:T(128)}, s32[4]{0:T(128)S(1)}, u32[]{:S(2)}) copy-start(s32[4]{0:T(128)S(1)} %pad_add_fusion.id_ref.refs_0_) | copy-start | bytes 52
  32.3 16.6 %copy-start.2 = (bf16[24,72,128]{2,1,0:T(8,128)(2,1)}, bf16[24,72,128]{2,1,0:T(8,128)(2,1)S(1)}, u32[]{:S(2)}) copy-start(bf16[24,72,128]{2,1,0:T(8,128)(2,1)S(1)} %collective-permute-done.left_ref) | copy-start | bytes 1327108
  32.3 16.6 %copy-start.3 = (bf16[24,72,128]{2,1,0:T(8,128)(2,1)}, bf16[24,72,128]{2,1,0:T(8,128)(2,1)S(1)}, u32[]{:S(2)}) copy-start(bf16[24,72,128]{2,1,0:T(8,128)(2,1)S(1)} %collective-permute-done.1.right_ref) | copy-start | bytes 1327108
  33.0 15.9 %copy-start.5 = (bf16[18,24,512]{2,1,0:T(8,128)(2,1)}, bf16[18,24,512]{2,1,0:T(8,128)(2,1)S(1)}, u32[]{:S(2)}) copy-start(bf16[18,24,512]{2,1,0:T(8,128)(2,1)S(1)} %collective-permute-done.3.refs_0_.top_ref) | copy-start | bytes 1327108
  33.6 15.2 %collective-permute-start.8 = (bf16[36,72,128]{2,1,0:T(8,128)(2,1)S(1)}, bf16[36,72,128]{2,1,0:T(8,128)(2,1)S(1)}, u32[]{:S(2)}, u32[]{:S(2)}) collective-permute-start(bf16[36,72,128]{2,1,0:T(8,128)(2,1)S(1)} %get-tuple-element.82), channel_id=1, source_target_pairs={{0,4},{4,0},{8,12},{12,8},{1,5},{5,1},{9,13},{13,9},{2,6},{6,2},{1... | collective-permute-start | bytes 1990664 | tf_op jit(solution)/shard_map/ppermute | solution.py:1142
  34.0 14.8 %collective-permute-start.9 = (bf16[36,72,128]{2,1,0:T(8,128)(2,1)S(1)}, bf16[36,72,128]{2,1,0:T(8,128)(2,1)S(1)}, u32[]{:S(2)}, u32[]{:S(2)}) collective-permute-start(bf16[36,72,128]{2,1,0:T(8,128)(2,1)S(1)} %get-tuple-element.83), channel_id=1, source_target_pairs={{4,8},{8,4},{5,9},{9,5},{6,10},{10,6},{7,11},{11,7},{20,24},{24,20... | collective-permute-start | bytes 1990664 | tf_op jit(solution)/shard_map/ppermute | solution.py:1148
  38.1 3.6 %collective-permute-start.10 = (f32[4,128]{1,0:T(4,128)S(1)}, f32[4,128]{1,0:T(4,128)S(1)}, u32[]{:S(2)}, u32[]{:S(2)}) collective-permute-start(f32[4,128]{1,0:T(4,128)S(1)} %get-tuple-element.84), channel_id=1, source_target_pairs={{0,64},{4,68},{8,72},{12,76},{16,80},{20,84},{24,88},{28,92},{32,9... | collective-permute-start | bytes 6152 | tf_op jit(solution)/shard_map/ppermute | solution.py:1157
  41.7 4.0 %collective-permute-start.11 = (f32[4,128]{1,0:T(4,128)S(1)}, f32[4,128]{1,0:T(4,128)S(1)}, u32[]{:S(2)}, u32[]{:S(2)}) collective-permute-start(f32[4,128]{1,0:T(4,128)S(1)} %add.63), channel_id=1, source_target_pairs={{0,8},{4,12},{8,0},{12,4},{16,24},{20,28},{24,16},{28,20},{32,40},... | collective-permute-start | bytes 6152 | tf_op jit(solution)/shard_map/ppermute | solution.py:1157
  41.7 17.7 %collective-permute-start.13 = (bf16[5,64,256]{2,1,0:T(8,128)(2,1)S(1)}, bf16[5,64,256]{2,1,0:T(8,128)(2,1)S(1)}, u32[]{:S(2)}, u32[]{:S(2)}) collective-permute-start(bf16[5,64,256]{2,1,0:T(8,128)(2,1)S(1)} %copy-done.10), channel_id=1, source_target_pairs={{0,2},{1,3},{2,0},{3,1},{4,6},{5,7},{6,4},{7,5},{8,10},{9,11},{10,... | collective-permute-start | bytes 491528 | tf_op jit(solution)/shard_map/ppermute | solution.py:1137
  44.6 14.9 %collective-permute-start.12 = (bf16[5,64,256]{2,1,0:T(8,128)(2,1)S(1)}, bf16[5,64,256]{2,1,0:T(8,128)(2,1)S(1)}, u32[]{:S(2)}, u32[]{:S(2)}) collective-permute-start(bf16[5,64,256]{2,1,0:T(8,128)(2,1)S(1)} %copy-done.10), channel_id=1, source_target_pairs={{0,1},{1,2},{2,3},{3,0},{4,5},{5,6},{6,7},{7,4},{8,9},{9,10},{10,1... | collective-permute-start | bytes 491528 | tf_op jit(solution)/shard_map/ppermute | solution.py:1137
  45.8 13.7 %collective-permute-start.14 = (bf16[5,64,256]{2,1,0:T(8,128)(2,1)S(1)}, bf16[5,64,256]{2,1,0:T(8,128)(2,1)S(1)}, u32[]{:S(2)}, u32[]{:S(2)}) collective-permute-start(bf16[5,64,256]{2,1,0:T(8,128)(2,1)S(1)} %copy-done.10), channel_id=1, source_target_pairs={{0,3},{1,0},{2,1},{3,2},{4,7},{5,4},{6,5},{7,6},{8,11},{9,8},{10,9... | collective-permute-start | bytes 491528 | tf_op jit(solution)/shard_map/ppermute | solution.py:1137
  59.5 11.4 %collective-permute-start.15 = (bf16[160,1024]{1,0:T(8,128)(2,1)}, bf16[160,1024]{1,0:T(8,128)(2,1)S(1)}, u32[]{:S(2)}, u32[]{:S(2)}) collective-permute-start(bf16[160,1024]{1,0:T(8,128)(2,1)} %get-tuple-element.89), channel_id=1, source_target_pairs={{0,1},{1,2},{2,3},{3,0},{4,5},{5,6},{6,7},{7,4},{8,9},{9,10},{10,1... | collective-permute-start | bytes 983048 | tf_op jit(solution)/shard_map/ppermute | solution.py:1137
  59.5 14.8 %collective-permute-start.16 = (bf16[160,1024]{1,0:T(8,128)(2,1)}, bf16[160,1024]{1,0:T(8,128)(2,1)S(1)}, u32[]{:S(2)}, u32[]{:S(2)}) collective-permute-start(bf16[160,1024]{1,0:T(8,128)(2,1)} %get-tuple-element.90), channel_id=1, source_target_pairs={{0,2},{1,3},{2,0},{3,1},{4,6},{5,7},{6,4},{7,5},{8,10},{9,11},{10,... | collective-permute-start | bytes 983048 | tf_op jit(solution)/shard_map/ppermute | solution.py:1137
  61.7 15.6 %collective-permute-start.17 = (bf16[160,1024]{1,0:T(8,128)(2,1)}, bf16[160,1024]{1,0:T(8,128)(2,1)S(1)}, u32[]{:S(2)}, u32[]{:S(2)}) collective-permute-start(bf16[160,1024]{1,0:T(8,128)(2,1)} %get-tuple-element.91), channel_id=1, source_target_pairs={{0,3},{1,0},{2,1},{3,2},{4,7},{5,4},{6,5},{7,6},{8,11},{9,8},{10,9... | collective-permute-start | bytes 983048 | tf_op jit(solution)/shard_map/ppermute | solution.py:1137
  80.1 13.1 %collective-permute-start.18 = (bf16[224,1024]{1,0:T(8,128)(2,1)S(1)}, bf16[224,1024]{1,0:T(8,128)(2,1)S(1)}, u32[]{:S(2)}, u32[]{:S(2)}) collective-permute-start(bf16[224,1024]{1,0:T(8,128)(2,1)S(1)} %get-tuple-element.101), channel_id=1, source_target_pairs={{0,1},{1,2},{2,3},{3,0},{4,5},{5,6},{6,7},{7,4},{8,9},{9,10},{10,1... | collective-permute-start | bytes 1376264 | tf_op jit(solution)/shard_map/ppermute | solution.py:1137
  81.5 23.0 %collective-permute-start.19 = (bf16[224,1024]{1,0:T(8,128)(2,1)S(1)}, bf16[224,1024]{1,0:T(8,128)(2,1)S(1)}, u32[]{:S(2)}, u32[]{:S(2)}) collective-permute-start(bf16[224,1024]{1,0:T(8,128)(2,1)S(1)} %get-tuple-element.102), channel_id=1, source_target_pairs={{0,2},{1,3},{2,0},{3,1},{4,6},{5,7},{6,4},{7,5},{8,10},{9,11},{10,... | collective-permute-start | bytes 1376264 | tf_op jit(solution)/shard_map/ppermute | solution.py:1137
  84.5 20.0 %collective-permute-start.20 = (bf16[224,1024]{1,0:T(8,128)(2,1)S(1)}, bf16[224,1024]{1,0:T(8,128)(2,1)S(1)}, u32[]{:S(2)}, u32[]{:S(2)}) collective-permute-start(bf16[224,1024]{1,0:T(8,128)(2,1)S(1)} %get-tuple-element.103), channel_id=1, source_target_pairs={{0,3},{1,0},{2,1},{3,2},{4,7},{5,4},{6,5},{7,6},{8,11},{9,8},{10,9... | collective-permute-start | bytes 1376264 | tf_op jit(solution)/shard_map/ppermute | solution.py:1137
  107.7 3.0 %collective-permute-start.21 = (bf16[1024,256]{1,0:T(8,128)(2,1)S(1)}, bf16[1024,256]{1,0:T(8,128)(2,1)S(1)}, u32[]{:S(2)}, u32[]{:S(2)}) collective-permute-start(bf16[1024,256]{1,0:T(8,128)(2,1)S(1)} %bitcast.14), channel_id=1, source_target_pairs={{0,4},{4,0},{8,12},{12,8},{16,20},{20,16},{24,28},{28,24},{32,36},... | collective-permute-start | bytes 1572872 | tf_op jit(solution)/shard_map/ppermute | solution.py:1157
  111.3 12.9 %collective-permute-start.22 = (bf16[320,256]{1,0:T(8,128)(2,1)S(1)}, bf16[320,256]{1,0:T(8,128)(2,1)S(1)}, u32[]{:S(2)}, u32[]{:S(2)}) collective-permute-start(bf16[320,256]{1,0:T(8,128)(2,1)S(1)} %get-tuple-element.109), channel_id=1, source_target_pairs={{0,16},{4,20},{8,24},{12,28},{16,0},{20,4},{24,8},{28,12},{32,48},... | collective-permute-start | bytes 491528 | tf_op jit(solution)/shard_map/ppermute | solution.py:1157
  111.4 12.8 %collective-permute-start.23 = (bf16[320,256]{1,0:T(8,128)(2,1)S(1)}, bf16[320,256]{1,0:T(8,128)(2,1)S(1)}, u32[]{:S(2)}, u32[]{:S(2)}) collective-permute-start(bf16[320,256]{1,0:T(8,128)(2,1)S(1)} %get-tuple-element.110), channel_id=1, source_target_pairs={{0,8},{4,12},{8,0},{12,4},{16,24},{20,28},{24,16},{28,20},{32,40},... | collective-permute-start | bytes 491528 | tf_op jit(solution)/shard_map/ppermute | solution.py:1157
  115.0 10.2 %collective-permute-start.24 = (bf16[320,256]{1,0:T(8,128)(2,1)S(1)}, bf16[320,256]{1,0:T(8,128)(2,1)S(1)}, u32[]{:S(2)}, u32[]{:S(2)}) collective-permute-start(bf16[320,256]{1,0:T(8,128)(2,1)S(1)} %get-tuple-element.111), channel_id=1, source_target_pairs={{0,24},{4,28},{8,16},{12,20},{16,8},{20,12},{24,0},{28,4},{32,56},... | collective-permute-start | bytes 491528 | tf_op jit(solution)/shard_map/ppermute | solution.py:1157
  124.2 19.1 %copy-start.13 = (s32[4]{0:T(128)S(1)}, s32[4]{0:T(128)}, u32[]{:S(2)}) copy-start(s32[4]{0:T(128)} %copy-done.11) | copy-start | bytes 52
  126.4 16.9 %collective-permute-start.27 = (bf16[18,60,512]{2,1,0:T(8,128)(2,1)}, bf16[18,60,512]{2,1,0:T(8,128)(2,1)S(1)}, u32[]{:S(2)}, u32[]{:S(2)}) collective-permute-start(bf16[18,60,512]{2,1,0:T(8,128)(2,1)} %get-tuple-element.123), channel_id=1, source_target_pairs={{0,4},{4,0},{8,12},{12,8},{1,5},{5,1},{9,13},{13,9},{2,6},{6,2},{1... | collective-permute-start | bytes 3317768 | tf_op jit(solution)/shard_map/ppermute | solution.py:1142
  127.6 4.4 %collective-permute-start.25 = (bf16[160,256]{1,0:T(8,128)(2,1)}, bf16[160,256]{1,0:T(8,128)(2,1)}, u32[]{:S(2)}, u32[]{:S(2)}) collective-permute-start(bf16[160,256]{1,0:T(8,128)(2,1)} %get-tuple-element.120), channel_id=1, source_target_pairs={{0,32},{4,36},{8,40},{12,44},{16,48},{20,52},{24,56},{28,60},{32,0... | collective-permute-start | bytes 245768 | tf_op jit(solution)/shard_map/ppermute | solution.py:1157
  128.8 14.5 %collective-permute-start.28 = (bf16[18,36,512]{2,1,0:T(8,128)(2,1)}, bf16[18,36,512]{2,1,0:T(8,128)(2,1)S(1)}, u32[]{:S(2)}, u32[]{:S(2)}) collective-permute-start(bf16[18,36,512]{2,1,0:T(8,128)(2,1)} %copy-done.19), channel_id=1, source_target_pairs={{4,8},{8,4},{5,9},{9,5},{6,10},{10,6},{7,11},{11,7},{20,24},{24,20... | collective-permute-start | bytes 1990664 | tf_op jit(solution)/shard_map/ppermute | solution.py:1148
  133.6 7.3 %collective-permute-start.26 = (bf16[80,256]{1,0:T(8,128)(2,1)S(1)}, bf16[80,256]{1,0:T(8,128)(2,1)S(1)}, u32[]{:S(2)}, u32[]{:S(2)}) collective-permute-start(bf16[80,256]{1,0:T(8,128)(2,1)S(1)} %select_convert_fusion), channel_id=1, source_target_pairs={{0,64},{4,68},{8,72},{12,76},{16,80},{20,84},{24,88},{28,92},{32,9... | collective-permute-start | bytes 122888 | tf_op jit(solution)/shard_map/ppermute | solution.py:1157
  136.6 27.9 %collective-permute-start.32 = (bf16[18,24,512]{2,1,0:T(8,128)(2,1)}, bf16[18,24,512]{2,1,0:T(8,128)(2,1)S(1)}, u32[]{:S(2)}, u32[]{:S(2)}) collective-permute-start(bf16[18,24,512]{2,1,0:T(8,128)(2,1)} %copy-done.20), channel_id=1, source_target_pairs={{4,8},{8,4},{5,9},{9,5},{6,10},{10,6},{7,11},{11,7},{20,24},{24,20... | collective-permute-start | bytes 1327112 | tf_op jit(solution)/shard_map/ppermute | solution.py:1148
  145.7 23.1 %collective-permute-start.30 = (bf16[24,72,128]{2,1,0:T(8,128)(2,1)S(1)}, bf16[24,72,128]{2,1,0:T(8,128)(2,1)S(1)}, u32[]{:S(2)}, u32[]{:S(2)}) collective-permute-start(bf16[24,72,128]{2,1,0:T(8,128)(2,1)S(1)} %get-tuple-element.128), channel_id=1, source_target_pairs={{0,16},{16,32},{32,48},{48,64},{64,80},{80,96},{96,112},{112,128},... | collective-permute-start | bytes 1327112 | tf_op jit(solution)/shard_map/ppermute | solution.py:1137
  145.8 23.1 %collective-permute-start.31 = (bf16[24,72,128]{2,1,0:T(8,128)(2,1)S(1)}, bf16[24,72,128]{2,1,0:T(8,128)(2,1)S(1)}, u32[]{:S(2)}, u32[]{:S(2)}) collective-permute-start(bf16[24,72,128]{2,1,0:T(8,128)(2,1)S(1)} %get-tuple-element.129), channel_id=1, source_target_pairs={{0,240},{16,0},{32,16},{48,32},{64,48},{80,64},{96,80},{112,96},{1... | collective-permute-start | bytes 1327112 | tf_op jit(solution)/shard_map/ppermute | solution.py:1137
  149.7 19.1 %collective-permute-start.29 = (bf16[40,256]{1,0:T(8,128)(2,1)S(1)}, bf16[40,256]{1,0:T(8,128)(2,1)S(1)}, u32[]{:S(2)}, u32[]{:S(2)}) collective-permute-start(bf16[40,256]{1,0:T(8,128)(2,1)S(1)} %select_convert_fusion.1), channel_id=1, source_target_pairs={{0,128},{4,132},{8,136},{12,140},{16,144},{20,148},{24,152},{28,15... | collective-permute-start | bytes 61448 | tf_op jit(solution)/shard_map/ppermute | solution.py:1157
  168.9 7.3 %collective-permute-start.33 = (bf16[104,256]{1,0:T(8,128)(2,1)S(1)}, bf16[104,256]{1,0:T(8,128)(2,1)S(1)}, u32[]{:S(2)}, u32[]{:S(2)}) collective-permute-start(bf16[104,256]{1,0:T(8,128)(2,1)S(1)} %pad_maximum_fusion.3), channel_id=1, source_target_pairs={{0,128},{4,132},{8,136},{12,140},{16,144},{20,148},{24,152},{28,15... | collective-permute-start | bytes 159752 | tf_op jit(solution)/shard_map/ppermute | solution.py:1157
  176.2 26.8 %copy-start.17 = (f32[4,128]{1,0:T(4,128)S(1)}, f32[4,128]{1,0:T(4,128)}, u32[]{:S(2)}) copy-start(f32[4,128]{1,0:T(4,128)} %add_multiply_fusion) | copy-start | bytes 6148
  176.2 6.4 %collective-permute-start.34 = (bf16[144,256]{1,0:T(8,128)(2,1)S(1)}, bf16[144,256]{1,0:T(8,128)(2,1)S(1)}, u32[]{:S(2)}, u32[]{:S(2)}) collective-permute-start(bf16[144,256]{1,0:T(8,128)(2,1)S(1)} %pad_maximum_fusion.2), channel_id=1, source_target_pairs={{0,64},{4,68},{8,72},{12,76},{16,80},{20,84},{24,88},{28,92},{32,9... | collective-permute-start | bytes 221192 | tf_op jit(solution)/shard_map/ppermute | solution.py:1157
  182.6 4.3 %collective-permute-start.35 = (bf16[224,256]{1,0:T(8,128)(2,1)S(1)}, bf16[224,256]{1,0:T(8,128)(2,1)S(1)}, u32[]{:S(2)}, u32[]{:S(2)}) collective-permute-start(bf16[224,256]{1,0:T(8,128)(2,1)S(1)} %pad_maximum_fusion.1), channel_id=1, source_target_pairs={{0,32},{4,36},{8,40},{12,44},{16,48},{20,52},{24,56},{28,60},{32,0... | collective-permute-start | bytes 344072 | tf_op jit(solution)/shard_map/ppermute | solution.py:1157
  187.1 11.9 %collective-permute-start.38 = (bf16[384,256]{1,0:T(8,128)(2,1)S(1)}, bf16[384,256]{1,0:T(8,128)(2,1)S(1)}, u32[]{:S(2)}, u32[]{:S(2)}) collective-permute-start(bf16[384,256]{1,0:T(8,128)(2,1)S(1)} %pad_maximum_fusion), channel_id=1, source_target_pairs={{0,24},{4,28},{8,16},{12,20},{16,8},{20,12},{24,0},{28,4},{32,56},... | collective-permute-start | bytes 589832 | tf_op jit(solution)/shard_map/ppermute | solution.py:1157
  187.2 11.8 %collective-permute-start.37 = (bf16[384,256]{1,0:T(8,128)(2,1)S(1)}, bf16[384,256]{1,0:T(8,128)(2,1)S(1)}, u32[]{:S(2)}, u32[]{:S(2)}) collective-permute-start(bf16[384,256]{1,0:T(8,128)(2,1)S(1)} %pad_maximum_fusion), channel_id=1, source_target_pairs={{0,8},{4,12},{8,0},{12,4},{16,24},{20,28},{24,16},{28,20},{32,40},... | collective-permute-start | bytes 589832 | tf_op jit(solution)/shard_map/ppermute | solution.py:1157
  188.2 10.7 %collective-permute-start.36 = (bf16[384,256]{1,0:T(8,128)(2,1)S(1)}, bf16[384,256]{1,0:T(8,128)(2,1)S(1)}, u32[]{:S(2)}, u32[]{:S(2)}) collective-permute-start(bf16[384,256]{1,0:T(8,128)(2,1)S(1)} %pad_maximum_fusion), channel_id=1, source_target_pairs={{0,16},{4,20},{8,24},{12,28},{16,0},{20,4},{24,8},{28,12},{32,48},... | collective-permute-start | bytes 589832 | tf_op jit(solution)/shard_map/ppermute | solution.py:1157
  199.5 3.4 %collective-permute-start.39 = (bf16[1344,256]{1,0:T(8,128)(2,1)S(1)}, bf16[1344,256]{1,0:T(8,128)(2,1)S(1)}, u32[]{:S(2)}, u32[]{:S(2)}) collective-permute-start(bf16[1344,256]{1,0:T(8,128)(2,1)S(1)} %get-tuple-element.141.refs_1_), channel_id=1, source_target_pairs={{0,4},{4,0},{8,12},{12,8},{16,20},{20,16},{24,28},{28,24},{32,36},... | collective-permute-start | bytes 2064392 | tf_op jit(solution)/shard_map/ppermute | solution.py:1157
  (18 other events, 87.8 us)
where the time goes:
time: 210 us; the launch traced here: 209 us
  starting transfers between devices  74.7 us (36%)
  waiting for transfers between devices  66.6 us (32%)
  Pallas kernels  55.2 us (26%)
  local copies, waits for them, and re-layouts  8.55 us (4%)
  other arithmetic  2.69 us (1%)
    ppermute x20, waiting for transfers between devices, swap(): return lax.ppermute(value, GRID, [(i, i ^ mask) for i in range(count)])  38 us
    ppermute x20, starting transfers between devices, swap(): return lax.ppermute(value, GRID, [(i, i ^ mask) for i in range(count)])  34.4 us
    ppermute x13, waiting for transfers between devices, shift(): return lax.ppermute(value, axis, pairs)  26.4 us
    ppermute x13, starting transfers between devices, shift(): return lax.ppermute(value, axis, pairs)  22.3 us
    ppermute x4, starting transfers between devices, to_other_chip(): return lax.ppermute(value, 'lat', pairs + [(j, i) for i, j in pairs])  16.4 us
    pallas_call x1, Pallas kernels, conv_forward(): pl.pallas_call(conv_body, grid=(chan // lanes,), in_specs=[smem()] + halo...  9.54 us
    pallas_call x1, Pallas kernels, scatter_grads(): pl.pallas_call(scatter_body, grid=(chan // lanes,), in_specs=[smem(), who...  8.13 us
    pallas_call x1, Pallas kernels, tap_sums(): pl.pallas_call(taps_body, grid=(chan // lanes,), in_specs=[by_lanes(3, ce...  7.5 us
  transfers between devices with their start and end apart: 40, of which 19 were waited for; matrix products, arithmetic and copies ran while one was open for 2% of the time, Pallas kernels for 19%

commit v1 on v0

--- a/solution.py
+++ b/solution.py
@@ -80,18 +80,43 @@
     return [line[:, 128 * n : 128 * (n + 1)] for n in range(line.shape[1] // 128)]
 
 
+main = margin // 8 * 8
+rest = margin - main
+
+
+def put_packed(packed, number, main_value, rest_value, blocks):
+    packed[main * number : main * (number + 1), :] = main_value
+    first = main * blocks + rest * number
+    packed[first : first + rest, :] = rest_value
+
+
+def packed_main(line, number):
+    return line[main * number : main * (number + 1)]
+
+
+def packed_rest(line, number, blocks):
+    first = main * blocks + rest * number
+    return line[first : first + rest]
+
+
 def edges_body(tile_ref, right_ref, left_ref, sum_ref, packed):
     rows, cols, chan = tile_ref.shape
 
     def row_step(row, carry):
         line = tile_ref[row].astype(f32)
-        for number, block in enumerate(split_lanes(line)):
-            place = slice(margin * number, margin * (number + 1))
-            packed[0, row, place, :] = block[:margin]
-            packed[1, row, place, :] = roll_rows(block, cols - margin, margin)
+        blocks = split_lanes(line)
+        for number, block in enumerate(blocks):
+            put_packed(packed.at[0, row], number, block[:main], block[main:margin], len(blocks))
+            put_packed(
+                packed.at[1, row],
+                number,
+                block[cols - main :],
+                roll_rows(block, cols - margin, rest),
+                len(blocks),
+            )
         return carry + line
 
-    total = lax.fori_loop(0, rows, row_step, jnp.zeros((cols, chan), f32))
+    total = lax.fori_loop(0, rows, row_step, jnp.zeros((cols, chan), f32), unroll=2)
     left_ref[...] = packed[0].astype(bf16)
     right_ref[...] = packed[1].astype(bf16)
 
@@ -155,12 +180,14 @@
 
     def put(at, row, middle, before, behind, skip=0):
         before, behind = before[row].astype(f32), behind[row + skip].astype(f32)
+        count = before.shape[0] // margin
         for number, block in blocks:
-            place = slice(margin * number, margin * (number + 1))
             line = ext(block, at)
             line[lead:after, :] = middle[row, :, 128 * block : 128 * (block + 1)].astype(f32)
-            line[off:lead, :] = before[place]
-            line[after : after + margin, :] = behind[place]
+            line[lead - main : lead, :] = packed_main(before, number)
+            line[off : off + rest, :] = packed_rest(before, number, count)
+            line[after : after + main, :] = packed_main(behind, number)
+            line[after + main : after + margin, :] = packed_rest(behind, number, count)
 
     def tile_row(row, carry):
         put(margin + row, row, tile, left, right)
@@ -174,8 +201,8 @@
         put(cross_first + row, row, cross, cross_corner, cross_corner, margin)
         return carry
 
-    lax.fori_loop(0, rows, tile_row, 0)
-    lax.fori_loop(0, margin, strip_row, 0)
+    lax.fori_loop(0, rows, tile_row, 0, unroll=2)
+    lax.fori_loop(0, margin, strip_row, 0, unroll=2)
 
 
 def halo_specs(halos, lanes):
@@ -270,7 +297,7 @@
                     cells[member + 1, places[n], across] = summed[n]
             return carry
 
-        lax.fori_loop(0, rows // 2, conv_rows, 0)
+        lax.fori_loop(0, rows // 2, conv_rows, 0, unroll=2)
     for member in range(4):
         block = cells[member].astype(bf16)
         inputs_ref[member] = block
@@ -550,7 +577,7 @@
                 shifted[number, row] = pltpu.roll(wide, shift, 0) if shift else wide
         return carry
 
-    lax.fori_loop(0, rows, row_step, 0)
+    lax.fori_loop(0, rows, row_step, 0, unroll=4)
 
 
 def scatter_body(
@@ -625,7 +652,10 @@
                 for n in (0, 1):
                     parts = [jnp.zeros((8, lanes), f32) if s is None else s for s in sums[n]]
                     center = jnp.concatenate(parts[lead // 8 : (lead + cols) // 8], axis=0)
-                    left = roll_rows(jnp.concatenate(parts[: lead // 8], axis=0), off, margin)
+                    left = jnp.concatenate(
+                        parts[(lead - main) // 8 : lead // 8] + [roll_rows(parts[off // 8], off % 8, 8)],
+                        axis=0,
+                    )[:margin]
                     right = jnp.concatenate(parts[(lead + cols) // 8 :], axis=0)[:margin]
                     if inside:
                         row = at[n] - margin
@@ -645,7 +675,7 @@
                     ext_rows((begin + 2 * step, begin + 2 * step + 1))
                     return carry
 
-                lax.fori_loop(0, 3, step_rows, 0)
+                lax.fori_loop(0, 3, step_rows, 0, unroll=3)
             else:
                 for step in range(3):
                     ext_rows((begin + 2 * step, begin + 2 * step + 1))
@@ -726,7 +756,7 @@
             ext_ref[row, :, 128 * block : 128 * (block + 1)] = ext[block, row].astype(bf16)
         return carry
 
-    lax.fori_loop(0, ext.shape[1], copy_rows, 0)
+    lax.fori_loop(0, ext.shape[1], copy_rows, 0, unroll=4)
 
 
 def extend(ids, halos, before):
@@ -775,7 +805,7 @@
                     sums[tap] = sums[tap] + jnp.sum(grad * window, axis=0)
         return tuple(sums)
 
-    sums = lax.fori_loop(0, rows, tap_row, (jnp.zeros((8, lanes), f32),) * 27)
+    sums = lax.fori_loop(0, rows, tap_row, (jnp.zeros((8, lanes), f32),) * 27, unroll=2)
     rows_of = [jnp.sum(value, axis=0, keepdims=True) for value in sums]
     rows_of.append(sum_ref[:, place])
     rows_of += [jnp.zeros((1, lanes), f32)] * 4
@@ -819,10 +849,10 @@
             line[number, cols - ref.shape[1] + 2 * margin :, :] = ref[row - first].astype(f32)
             left = left + line[number, cols : cols + margin, :]
             right = right + line[number, cols + margin :, :]
-        for number, (one, two) in enumerate(zip(split_lanes(left), split_lanes(right))):
-            place = slice(margin * number, margin * (number + 1))
-            packed[0, row, place, :] = one
-            packed[1, row, place, :] = two
+        pairs = list(zip(split_lanes(left), split_lanes(right)))
+        for number, pair in enumerate(pairs):
+            for side, value in enumerate(pair):
+                put_packed(packed.at[side, row], number, value[:main], value[main:], len(pairs))
 
     for upper in (0, 1):
         pieces = [(chip_ref, shifted * (1 - upper), 0), (corner_ref, shifted * upper, 1)]
@@ -837,7 +867,7 @@
                     one_row(first + number, refs)
                     return carry
 
-                lax.fori_loop(0, last - first, step, 0)
+                lax.fori_loop(0, last - first, step, 0, unroll=3)
 
     left_out[...] = packed[0].astype(bf16)
     right_out[...] = packed[1].astype(bf16)
@@ -864,23 +894,16 @@
 def middle_body(id_ref, center_ref, chip_ref, cross_ref, out_ref):
     rows, cols, _ = center_ref.shape
     shifted = rows - margin
-    upper = id_ref[1]
-
-    def copy_row(row, carry):
-        out_ref[row] = center_ref[row].astype(f32)
-        return carry
-
-    def chip_row(row, carry):
-        out_ref[shifted * (1 - upper) + row] += chip_ref[row].astype(f32)[:cols]
-        return carry
-
-    def cross_row(row, carry):
-        out_ref[shifted * upper + row] += cross_ref[row].astype(f32)
-        return carry
-
-    lax.fori_loop(0, rows, copy_row, 0)
-    lax.fori_loop(0, margin, chip_row, 0)
-    lax.fori_loop(0, margin, cross_row, 0)
+    out_ref[...] = center_ref[...].astype(f32)
+    for upper in (0, 1):
+        chip_first, cross_first = shifted * (1 - upper), shifted * upper
+
+        @pl.when(id_ref[1] == upper)
+        def _(chip_first=chip_first, cross_first=cross_first):
+            for row in range(margin):
+                out_ref[chip_first + row] += chip_ref[row].astype(f32)[:cols]
+            for row in range(margin):
+                out_ref[cross_first + row] += cross_ref[row].astype(f32)
 
 
 def middle(ids, center, chip, cross):
@@ -912,20 +935,22 @@
 
     def row_step(row, carry):
         left, right = left_ref[row].astype(f32), right_ref[row].astype(f32)
-        for number in range(chan // 128):
-            place = slice(margin * number, margin * (number + 1))
+        count = chan // 128
+        for number in range(count):
             across = slice(128 * number, 128 * (number + 1))
-            pads[0, row, :margin, across] = left[place]
-            pads[1, row, cols - margin :, across] = right[place]
+            pads[0, row, :main, across] = packed_main(left, number)
+            pads[0, row, main:margin, across] = packed_rest(left, number, count)
+            pads[1, row, cols - main :, across] = packed_main(right, number)
+            pads[1, row, cols - margin : cols - main, across] = packed_rest(right, number, count)
         return carry
 
-    lax.fori_loop(0, rows, row_step, 0)
+    lax.fori_loop(0, rows, row_step, 0, unroll=4)
 
     def add_row(row, carry):
         out_ref[row] = (center_ref[row] + pads[0, row] + pads[1, row] + base).astype(bf16)
         return carry
 
-    lax.fori_loop(0, rows, add_row, 0)
+    lax.fori_loop(0, rows, add_row, 0, unroll=4)
 
 
 def finish(center, left, right, pooled):

time: 210 us -> 207 us (0.986)
  Pallas kernels: 55.2 us -> 52 us
    ppermute x20, starting transfers between devices: 34.4 us -> 37 us  [swap(): return lax.ppermute(value, GRID, [(i, i ^ mask) for i in range(count)])]
  transfers between devices with their start and end apart: 40 -> 40, of which waited for: 19 -> 19; matrix products, arithmetic and copies ran while one was open for 2% -> 3% of each run, Pallas kernels for 19% -> 18%
where the time goes in v1:
time: 207 us; the launch traced here: 206 us
  starting transfers between devices  76.2 us (37%)
  waiting for transfers between devices  65.9 us (32%)
  Pallas kernels  52 us (25%)
  local copies, waits for them, and re-layouts  8.55 us (4%)
  other arithmetic  2.69 us (1%)
    ppermute x20, waiting for transfers between devices, swap(): return lax.ppermute(value, GRID, [(i, i ^ mask) for i in range(count)])  37 us
    ppermute x20, starting transfers between devices, swap(): return lax.ppermute(value, GRID, [(i, i ^ mask) for i in range(count)])  37 us
    ppermute x13, waiting for transfers between devices, shift(): return lax.ppermute(value, axis, pairs)  26.7 us
    ppermute x13, starting transfers between devices, shift(): return lax.ppermute(value, axis, pairs)  22.1 us
    ppermute x4, starting transfers between devices, to_other_chip(): return lax.ppermute(value, 'lat', pairs + [(j, i) for i, j in pairs])  15.4 us
    pallas_call x1, Pallas kernels, conv_forward(): pl.pallas_call(conv_body, grid=(chan // lanes,), in_specs=[smem()] + halo...  9.48 us
    pallas_call x1, Pallas kernels, scatter_grads(): pl.pallas_call(scatter_body, grid=(chan // lanes,), in_specs=[smem(), who...  7.07 us
    pallas_call x1, Pallas kernels, tap_sums(): pl.pallas_call(taps_body, grid=(chan // lanes,), in_specs=[by_lanes(3, ce...  6.74 us
  transfers between devices with their start and end apart: 40, of which 19 were waited for; matrix products, arithmetic and copies ran while one was open for 3% of the time, Pallas kernels for 18%

profile of v1, /device:TPU:1, one launch (start us, length us, event | category | flops | bytes accessed | tf_op | source)
XLA Modules:
  0.0 206.4 jit_solution(16612067685938715868)
XLA Ops:
  0.6 2.1 %edges.1 = (bf16[24,72,128]{2,1,0:T(8,128)(2,1)S(1)}, bf16[24,72,128]{2,1,0:T(8,128)(2,1)S(1)}, f32[1,512]{1,0:T(1,128)S(1)}) custom-call(bf16[24,24,512]{2,1,0:T(8,128)(2,1)} %tile_ref.5), custom_call_target="tpu_custom_call" | custom-call | flops 294912 | bytes 2000000 | tf_op jit(solution)/shard_map/edges/pallas_call | solution.py:135
  2.7 3.3 %collective-permute-start.2 = (f32[4,128]{1,0:T(4,128)S(1)}, f32[4,128]{1,0:T(4,128)S(1)}, u32[]{:S(2)}, u32[]{:S(2)}) collective-permute-start(f32[4,128]{1,0:T(4,128)S(1)} %bitcast.12), channel_id=1, source_target_pairs={{0,4},{4,0},{8,12},{12,8},{16,20},{20,16},{24,28},{28,24},{32,36},... | collective-permute-start | bytes 6152 | tf_op jit(solution)/shard_map/ppermute | solution.py:1182
  6.1 4.9 %collective-permute-start.1 = (bf16[24,72,128]{2,1,0:T(8,128)(2,1)S(1)}, bf16[24,72,128]{2,1,0:T(8,128)(2,1)S(1)}, u32[]{:S(2)}, u32[]{:S(2)}) collective-permute-start(bf16[24,72,128]{2,1,0:T(8,128)(2,1)S(1)} %get-tuple-element.78), channel_id=1, source_target_pairs={{0,240},{16,0},{32,16},{48,32},{64,48},{80,64},{96,80},{112,96},{1... | collective-permute-start | bytes 1327112 | tf_op jit(solution)/shard_map/ppermute | solution.py:1162
  10.9 2.0 constant_dynamic-slice_fusion
  12.9 5.0 %collective-permute-start.4 = (bf16[18,24,512]{2,1,0:T(8,128)(2,1)}, bf16[18,24,512]{2,1,0:T(8,128)(2,1)S(1)}, u32[]{:S(2)}, u32[]{:S(2)}) collective-permute-start(bf16[18,24,512]{2,1,0:T(8,128)(2,1)} %get-tuple-element.156), channel_id=1, source_target_pairs={{4,8},{8,4},{5,9},{9,5},{6,10},{10,6},{7,11},{11,7},{20,24},{24,20... | collective-permute-start | bytes 1327112 | tf_op jit(solution)/shard_map/ppermute | solution.py:1173
  18.1 2.7 %collective-permute-done.5 = f32[4,128]{1,0:T(4,128)S(1)} collective-permute-done((f32[4,128]{1,0:T(4,128)S(1)}, f32[4,128]{1,0:T(4,128)S(1)}, u32[]{:S(2)}, u32[]{:S(2)}) %collective-permute-start.5) | collective-permute-done | bytes 2080 | tf_op jit(solution)/shard_map/ppermute | solution.py:1182
  20.8 4.4 %collective-permute-start.6 = (f32[4,128]{1,0:T(4,128)S(1)}, f32[4,128]{1,0:T(4,128)S(1)}, u32[]{:S(2)}, u32[]{:S(2)}) collective-permute-start(f32[4,128]{1,0:T(4,128)S(1)} %add.60), channel_id=1, source_target_pairs={{0,128},{4,132},{8,136},{12,140},{16,144},{20,148},{24,152},{28,15... | collective-permute-start | bytes 6152 | tf_op jit(solution)/shard_map/ppermute | solution.py:1182
  25.2 2.0 collective-permute-done.6
  27.3 4.9 %collective-permute-done.7 = f32[4,128]{1,0:T(4,128)S(1)} collective-permute-done((f32[4,128]{1,0:T(4,128)S(1)}, f32[4,128]{1,0:T(4,128)S(1)}, u32[]{:S(2)}, u32[]{:S(2)}) %collective-permute-start.7) | collective-permute-done | bytes 2080 | tf_op jit(solution)/shard_map/ppermute | solution.py:1182
  34.0 4.1 %collective-permute-start.9 = (bf16[36,72,128]{2,1,0:T(8,128)(2,1)S(1)}, bf16[36,72,128]{2,1,0:T(8,128)(2,1)S(1)}, u32[]{:S(2)}, u32[]{:S(2)}) collective-permute-start(bf16[36,72,128]{2,1,0:T(8,128)(2,1)S(1)} %get-tuple-element.83), channel_id=1, source_target_pairs={{4,8},{8,4},{5,9},{9,5},{6,10},{10,6},{7,11},{11,7},{20,24},{24,20... | collective-permute-start | bytes 1990664 | tf_op jit(solution)/shard_map/ppermute | solution.py:1173
  38.1 2.6 %collective-permute-start.10 = (f32[4,128]{1,0:T(4,128)S(1)}, f32[4,128]{1,0:T(4,128)S(1)}, u32[]{:S(2)}, u32[]{:S(2)}) collective-permute-start(f32[4,128]{1,0:T(4,128)S(1)} %get-tuple-element.84), channel_id=1, source_target_pairs={{0,64},{4,68},{8,72},{12,76},{16,80},{20,84},{24,88},{28,92},{32,9... | collective-permute-start | bytes 6152 | tf_op jit(solution)/shard_map/ppermute | solution.py:1182
  41.7 2.8 %collective-permute-start.13 = (bf16[5,64,256]{2,1,0:T(8,128)(2,1)S(1)}, bf16[5,64,256]{2,1,0:T(8,128)(2,1)S(1)}, u32[]{:S(2)}, u32[]{:S(2)}) collective-permute-start(bf16[5,64,256]{2,1,0:T(8,128)(2,1)S(1)} %copy-done.10), channel_id=1, source_target_pairs={{0,2},{1,3},{2,0},{3,1},{4,6},{5,7},{6,4},{7,5},{8,10},{9,11},{10,... | collective-permute-start | bytes 491528 | tf_op jit(solution)/shard_map/ppermute | solution.py:1162
  45.7 2.5 %collective-permute-start.14 = (bf16[5,64,256]{2,1,0:T(8,128)(2,1)S(1)}, bf16[5,64,256]{2,1,0:T(8,128)(2,1)S(1)}, u32[]{:S(2)}, u32[]{:S(2)}) collective-permute-start(bf16[5,64,256]{2,1,0:T(8,128)(2,1)S(1)} %copy-done.10), channel_id=1, source_target_pairs={{0,3},{1,0},{2,1},{3,2},{4,7},{5,4},{6,5},{7,6},{8,11},{9,8},{10,9... | collective-permute-start | bytes 491528 | tf_op jit(solution)/shard_map/ppermute | solution.py:1162
  49.8 9.5 %conv_forward.1 = (bf16[4,576,512]{2,1,0:T(8,128)(2,1)}, f32[144,1024]{1,0:T(8,128)}, bf16[160,1024]{1,0:T(8,128)(2,1)}, bf16[160,1024]{1,0:T(8,128)(2,1)}, bf16...) custom-call(s32[4]{0:T(128)} %copy-done.11, bf16[24,24,512]{2,1,0:T(8,128)(2,1)} %tile_ref.5, ...), custom_call_target="tpu_custom_call" | custom-call | flops 619905024 | bytes 20000000 | tf_op jit(solution)/shard_map/conv_forward/pallas_call | solution.py:344
  59.4 2.2 %collective-permute-start.16 = (bf16[160,1024]{1,0:T(8,128)(2,1)}, bf16[160,1024]{1,0:T(8,128)(2,1)S(1)}, u32[]{:S(2)}, u32[]{:S(2)}) collective-permute-start(bf16[160,1024]{1,0:T(8,128)(2,1)} %get-tuple-element.90), channel_id=1, source_target_pairs={{0,2},{1,3},{2,0},{3,1},{4,6},{5,7},{6,4},{7,5},{8,10},{9,11},{10,... | collective-permute-start | bytes 983048 | tf_op jit(solution)/shard_map/ppermute | solution.py:1162
  64.1 6.3 %extend.1 = (bf16[60,80,512]{2,1,0:T(8,128)(2,1)}, f32[8,128]{1,0:T(8,128)S(1)}) custom-call(s32[4]{0:T(128)S(1)} %copy-done.12, bf16[24,24,512]{2,1,0:T(8,128)(2,1)} %tile_ref.5, bf16[24,72,128]{2,1,0:T(8,128)(2,1)} %copy-done.2, bf16[24,72,128]{2,1,0:T(8,128)(2,1)} %copy-done.3, bf16[18,24,512]{2,1,0:T(8,128)(2,1)} %copy-done.5, ...), custom_call_target="tpu_custom_call" | custom-call | flops 1000000 | bytes 10000000 | tf_op jit(solution)/shard_map/extend/pallas_call | solution.py:765
  70.4 3.9 %collective-permute-done.16.two_ref = bf16[160,1024]{1,0:T(8,128)(2,1)S(1)} collective-permute-done((bf16[160,1024]{1,0:T(8,128)(2,1)}, bf16[160,1024]{1,0:T(8,128)(2,1)S(1)}, u32[]{:S(2)}, u32[]{:S(2)}) %collective-permute-start.16) | collective-permute-done | bytes 327712 | tf_op jit(solution)/shard_map/ppermute | solution.py:1162
  74.3 2.9 %collective-permute-done.17.three_ref = bf16[160,1024]{1,0:T(8,128)(2,1)S(1)} collective-permute-done((bf16[160,1024]{1,0:T(8,128)(2,1)}, bf16[160,1024]{1,0:T(8,128)(2,1)S(1)}, u32[]{:S(2)}, u32[]{:S(2)}) %collective-permute-start.17) | collective-permute-done | bytes 327712 | tf_op jit(solution)/shard_map/ppermute | solution.py:1162
  77.2 2.1 %project.1 = (bf16[256,256]{1,0:T(8,128)(2,1)S(1)}, bf16[144,1024]{1,0:T(8,128)(2,1)S(1)}, bf16[224,1024]{1,0:T(8,128)(2,1)S(1)}, bf16[224,1024]{1,0:T(8,128)(2,...) custom-call(s32[4]{0:T(128)S(1)} %copy-done.12, ...), custom_call_target="tpu_custom_call" | custom-call | flops 226492416 | bytes 4000000 | tf_op jit(solution)/shard_map/project/pallas_call | solution.py:451
  81.3 3.1 %collective-permute-start.19 = (bf16[224,1024]{1,0:T(8,128)(2,1)S(1)}, bf16[224,1024]{1,0:T(8,128)(2,1)S(1)}, u32[]{:S(2)}, u32[]{:S(2)}) collective-permute-start(bf16[224,1024]{1,0:T(8,128)(2,1)S(1)} %get-tuple-element.102), channel_id=1, source_target_pairs={{0,2},{1,3},{2,0},{3,1},{4,6},{5,7},{6,4},{7,5},{8,10},{9,11},{10,... | collective-permute-start | bytes 1376264 | tf_op jit(solution)/shard_map/ppermute | solution.py:1162
  84.4 8.6 %collective-permute-done.18.one_ref = bf16[224,1024]{1,0:T(8,128)(2,1)S(1)} collective-permute-done((bf16[224,1024]{1,0:T(8,128)(2,1)S(1)}, bf16[224,1024]{1,0:T(8,128)(2,1)S(1)}, u32[]{:S(2)}, u32[]{:S(2)}) %collective-permute-start.18) | collective-permute-done | bytes 458784 | tf_op jit(solution)/shard_map/ppermute | solution.py:1162
  93.0 11.4 %collective-permute-done.19.two_ref = bf16[224,1024]{1,0:T(8,128)(2,1)S(1)} collective-permute-done((bf16[224,1024]{1,0:T(8,128)(2,1)S(1)}, bf16[224,1024]{1,0:T(8,128)(2,1)S(1)}, u32[]{:S(2)}, u32[]{:S(2)}) %collective-permute-start.19) | collective-permute-done | bytes 458784 | tf_op jit(solution)/shard_map/ppermute | solution.py:1162
  104.4 3.1 %weight_grads.1 = (f32[2,512,256]{2,1,0:T(8,128)S(1)}, bf16[2,512,256]{2,1,0:T(8,128)(2,1)S(1)}, bf16[576,1024]{1,0:T(8,128)(2,1)S(1)}, f32[4,64,256]{2,1,0:T(8,128)S(1)}, f32[1,256]{1,0:T(1,128)S(1)}) custom-call(s32[4]{0:T(128)S(1)} %copy-done.12, bf16[144,1024]{1,0:T(8,128)(2,1)S(1)} %get-tuple-element.98.own_ref, ...), custom_call_target="tpu_custom_call" | custom-call | flops 603979776 | bytes 6000000 | tf_op jit(solution)/shard_map/weight_grads/pallas_call | solution.py:514
  107.6 1.4 collective-permute-start.21
  109.0 1.5 collective-permute-done.21.got_ref
  111.3 3.6 %collective-permute-start.23 = (bf16[320,256]{1,0:T(8,128)(2,1)S(1)}, bf16[320,256]{1,0:T(8,128)(2,1)S(1)}, u32[]{:S(2)}, u32[]{:S(2)}) collective-permute-start(bf16[320,256]{1,0:T(8,128)(2,1)S(1)} %get-tuple-element.110), channel_id=1, source_target_pairs={{0,8},{4,12},{8,0},{12,4},{16,24},{20,28},{24,16},{28,20},{32,40},... | collective-permute-start | bytes 491528 | tf_op jit(solution)/shard_map/ppermute | solution.py:1182
  115.1 7.1 %scatter_grads.1 = (bf16[3,576,512]{2,1,0:T(8,128)(2,1)}, bf16[24,24,512]{2,1,0:T(8,128)(2,1)}, bf16[24,18,512]{2,1,0:T(8,128)(2,1)}, bf16[24,18,512]{2,1,0:T(8,...) custom-call(s32[4]{0:T(128)S(1)} %copy-done.12, ...), custom_call_target="tpu_custom_call" | custom-call | flops 619905024 | bytes 15000000 | tf_op jit(solution)/shard_map/scatter_grads/pallas_call | solution.py:699
  123.0 2.0 collective-permute-done.24.three_ref
  128.7 2.0 collective-permute-start.28
  133.5 2.9 %collective-permute-start.26 = (bf16[80,256]{1,0:T(8,128)(2,1)S(1)}, bf16[80,256]{1,0:T(8,128)(2,1)S(1)}, u32[]{:S(2)}, u32[]{:S(2)}) collective-permute-start(bf16[80,256]{1,0:T(8,128)(2,1)S(1)} %select_convert_fusion), channel_id=1, source_target_pairs={{0,64},{4,68},{8,72},{12,76},{16,80},{20,84},{24,88},{28,92},{32,9... | collective-permute-start | bytes 122888 | tf_op jit(solution)/shard_map/ppermute | solution.py:1182
  136.4 4.3 %collective-permute-start.32 = (bf16[18,24,512]{2,1,0:T(8,128)(2,1)}, bf16[18,24,512]{2,1,0:T(8,128)(2,1)S(1)}, u32[]{:S(2)}, u32[]{:S(2)}) collective-permute-start(bf16[18,24,512]{2,1,0:T(8,128)(2,1)} %copy-done.20), channel_id=1, source_target_pairs={{4,8},{8,4},{5,9},{9,5},{6,10},{10,6},{7,11},{11,7},{20,24},{24,20... | collective-permute-start | bytes 1327112 | tf_op jit(solution)/shard_map/ppermute | solution.py:1173
  141.7 1.5 collective-permute-done.28.corner_ref
  143.2 2.5 %home.1 = (bf16[24,72,128]{2,1,0:T(8,128)(2,1)S(1)}, bf16[24,72,128]{2,1,0:T(8,128)(2,1)S(1)}) custom-call(s32[4]{0:T(128)S(1)} %copy-done.13, bf16[24,18,512]{2,1,0:T(8,128)(2,1)} %get-tuple-element.121.left_ref, bf16[24,18,512]{2,1,0:T(8,128)(2,1)} %get-tuple-element.122.right_ref, bf16[18,60,512]{2,1,0:T(8,128)(2,1)S(1)} %collective-permute-done.27.chip_ref, ...), custom_call_target="tpu_custom_call" | custom-call | flops 221184 | bytes 5000000 | tf_op jit(solution)/shard_map/home/pallas_call | solution.py:879
  145.8 3.7 %collective-permute-start.31 = (bf16[24,72,128]{2,1,0:T(8,128)(2,1)S(1)}, bf16[24,72,128]{2,1,0:T(8,128)(2,1)S(1)}, u32[]{:S(2)}, u32[]{:S(2)}) collective-permute-start(bf16[24,72,128]{2,1,0:T(8,128)(2,1)S(1)} %get-tuple-element.129), channel_id=1, source_target_pairs={{0,240},{16,0},{32,16},{48,32},{64,48},{80,64},{96,80},{112,96},{1... | collective-permute-start | bytes 1327112 | tf_op jit(solution)/shard_map/ppermute | solution.py:1162
  149.5 5.9 %collective-permute-start.29 = (bf16[40,256]{1,0:T(8,128)(2,1)S(1)}, bf16[40,256]{1,0:T(8,128)(2,1)S(1)}, u32[]{:S(2)}, u32[]{:S(2)}) collective-permute-start(bf16[40,256]{1,0:T(8,128)(2,1)S(1)} %select_convert_fusion.1), channel_id=1, source_target_pairs={{0,128},{4,132},{8,136},{12,140},{16,144},{20,148},{24,152},{28,15... | collective-permute-start | bytes 61448 | tf_op jit(solution)/shard_map/ppermute | solution.py:1182
  155.4 1.6 unpack_mixed.1
  157.0 6.7 %tap_sums.1 = f32[64,256]{1,0:T(8,128)S(1)} custom-call(bf16[3,576,512]{2,1,0:T(8,128)(2,1)} %get-tuple-element.138.grad_ref, bf16[60,80,512]{2,1,0:T(8,128)(2,1)} %get-tuple-element.139.ext_ref, f32[1,256]{1,0:T(1,128)S(1)} %get-tuple-element.140.sum_ref), custom_call_target="tpu_custom_call" | custom-call | flops 15925248 | bytes 15000000 | tf_op jit(solution)/shard_map/tap_sums/pallas_call | solution.py:821
  164.5 2.6 %middle.1.center_ref = f32[24,24,512]{2,1,0:T(8,128)S(1)} custom-call(s32[4]{0:T(128)S(1)} %copy-done.13, bf16[24,24,512]{2,1,0:T(8,128)(2,1)} %get-tuple-element.130.center_ref, bf16[18,60,512]{2,1,0:T(8,128)(2,1)} %copy-done.1, bf16[18,24,512]{2,1,0:T(8,128)(2,1)} %copy-done.24), custom_call_target="tpu_custom_call" | custom-call | flops 294912 | bytes 4000000 | tf_op jit(solution)/shard_map/middle/pallas_call | solution.py:911
  167.1 5.0 %collective-permute-start.33 = (bf16[104,256]{1,0:T(8,128)(2,1)S(1)}, bf16[104,256]{1,0:T(8,128)(2,1)S(1)}, u32[]{:S(2)}, u32[]{:S(2)}) collective-permute-start(bf16[104,256]{1,0:T(8,128)(2,1)S(1)} %pad_maximum_fusion.3), channel_id=1, source_target_pairs={{0,128},{4,132},{8,136},{12,140},{16,144},{20,148},{24,152},{28,15... | collective-permute-start | bytes 159752 | tf_op jit(solution)/shard_map/ppermute | solution.py:1182
  172.2 2.3 %collective-permute-done.33 = bf16[104,256]{1,0:T(8,128)(2,1)S(1)} collective-permute-done((bf16[104,256]{1,0:T(8,128)(2,1)S(1)}, bf16[104,256]{1,0:T(8,128)(2,1)S(1)}, u32[]{:S(2)}, u32[]{:S(2)}) %collective-permute-start.33) | collective-permute-done | bytes 53280 | tf_op jit(solution)/shard_map/ppermute | solution.py:1182
  175.7 5.1 %collective-permute-done.34 = bf16[144,256]{1,0:T(8,128)(2,1)S(1)} collective-permute-done((bf16[144,256]{1,0:T(8,128)(2,1)S(1)}, bf16[144,256]{1,0:T(8,128)(2,1)S(1)}, u32[]{:S(2)}, u32[]{:S(2)}) %collective-permute-start.34) | collective-permute-done | bytes 73760 | tf_op jit(solution)/shard_map/ppermute | solution.py:1182
  181.0 3.6 %collective-permute-done.35 = bf16[224,256]{1,0:T(8,128)(2,1)S(1)} collective-permute-done((bf16[224,256]{1,0:T(8,128)(2,1)S(1)}, bf16[224,256]{1,0:T(8,128)(2,1)S(1)}, u32[]{:S(2)}, u32[]{:S(2)}) %collective-permute-start.35) | collective-permute-done | bytes 114720 | tf_op jit(solution)/shard_map/ppermute | solution.py:1182
  184.8 2.1 %collective-permute-start.37 = (bf16[384,256]{1,0:T(8,128)(2,1)S(1)}, bf16[384,256]{1,0:T(8,128)(2,1)S(1)}, u32[]{:S(2)}, u32[]{:S(2)}) collective-permute-start(bf16[384,256]{1,0:T(8,128)(2,1)S(1)} %pad_maximum_fusion), channel_id=1, source_target_pairs={{0,8},{4,12},{8,0},{12,4},{16,24},{20,28},{24,16},{28,20},{32,40},... | collective-permute-start | bytes 589832 | tf_op jit(solution)/shard_map/ppermute | solution.py:1182
  188.1 8.5 %collective-permute-done.38.three_ref = bf16[384,256]{1,0:T(8,128)(2,1)S(1)} collective-permute-done((bf16[384,256]{1,0:T(8,128)(2,1)S(1)}, bf16[384,256]{1,0:T(8,128)(2,1)S(1)}, u32[]{:S(2)}, u32[]{:S(2)}) %collective-permute-start.38) | collective-permute-done | bytes 196640 | tf_op jit(solution)/shard_map/ppermute | solution.py:1182
  197.2 1.6 collective-permute-start.39
  198.8 1.8 collective-permute-done.39.refs_2_.refs_4_
  200.6 3.5 %last_stage.1 = (f32[5,512,256]{2,1,0:T(8,128)}, f32[5,64,256]{2,1,0:T(8,128)}, f32[3,9,512]{2,1,0:T(8,128)S(1)}, f32[1,512]{1,0:T(1,128)S(1)}) custom-call(s32[4]{0:T(128)S(1)} %copy-done.13, bf16[1344,256]{1,0:T(8,128)(2,1)S(1)} %get-tuple-element.141.refs_1_, bf16[1344,256]{1,0:T(8,128)(2,1)S(1)} %collective-permute-done.39.refs_2_.refs_4_, ...), custom_call_target="tpu_custom_call" | custom-call | flops 1048576 | bytes 5000000 | tf_op jit(solution)/shard_map/last_stage/pallas_call | solution.py:1126
  204.8 1.6 finish.1
  (129 shorter events, 24.4 us)
Async XLA Ops:
  2.7 8.2 %collective-permute-start.2 = (f32[4,128]{1,0:T(4,128)S(1)}, f32[4,128]{1,0:T(4,128)S(1)}, u32[]{:S(2)}, u32[]{:S(2)}) collective-permute-start(f32[4,128]{1,0:T(4,128)S(1)} %bitcast.12), channel_id=1, source_target_pairs={{0,4},{4,0},{8,12},{12,8},{16,20},{20,16},{24,28},{28,24},{32,36},... | collective-permute-start | bytes 6152 | tf_op jit(solution)/shard_map/ppermute | solution.py:1182
  6.1 26.1 %collective-permute-start = (bf16[24,72,128]{2,1,0:T(8,128)(2,1)S(1)}, bf16[24,72,128]{2,1,0:T(8,128)(2,1)S(1)}, u32[]{:S(2)}, u32[]{:S(2)}) collective-permute-start(bf16[24,72,128]{2,1,0:T(8,128)(2,1)S(1)} %get-tuple-element.77), channel_id=1, source_target_pairs={{0,16},{16,32},{32,48},{48,64},{64,80},{80,96},{96,112},{112,128},... | collective-permute-start | bytes 1327112 | tf_op jit(solution)/shard_map/ppermute | solution.py:1162
  6.1 26.1 %collective-permute-start.1 = (bf16[24,72,128]{2,1,0:T(8,128)(2,1)S(1)}, bf16[24,72,128]{2,1,0:T(8,128)(2,1)S(1)}, u32[]{:S(2)}, u32[]{:S(2)}) collective-permute-start(bf16[24,72,128]{2,1,0:T(8,128)(2,1)S(1)} %get-tuple-element.78), channel_id=1, source_target_pairs={{0,240},{16,0},{32,16},{48,32},{64,48},{80,64},{96,80},{112,96},{1... | collective-permute-start | bytes 1327112 | tf_op jit(solution)/shard_map/ppermute | solution.py:1162
  12.9 28.8 %copy-start.10 = (bf16[5,64,256]{2,1,0:T(8,128)(2,1)S(1)}, bf16[5,64,256]{2,1,0:T(8,128)(2,1)}, u32[]{:S(2)}) copy-start(bf16[5,64,256]{2,1,0:T(8,128)(2,1)} %weight_own.1) | copy-start | bytes 491524
  12.9 31.9 %copy-start.25 = (f32[3,9,512]{2,0,1:T(4,128)S(1)}, f32[3,9,512]{2,0,1:T(4,128)}, u32[]{:S(2)}) copy-start(f32[3,9,512]{2,0,1:T(4,128)} %param.6) | copy-start | bytes 165892
  12.9 20.0 %collective-permute-start.4 = (bf16[18,24,512]{2,1,0:T(8,128)(2,1)}, bf16[18,24,512]{2,1,0:T(8,128)(2,1)S(1)}, u32[]{:S(2)}, u32[]{:S(2)}) collective-permute-start(bf16[18,24,512]{2,1,0:T(8,128)(2,1)} %get-tuple-element.156), channel_id=1, source_target_pairs={{4,8},{8,4},{5,9},{9,5},{6,10},{10,6},{7,11},{11,7},{20,24},{24,20... | collective-permute-start | bytes 1327112 | tf_op jit(solution)/shard_map/ppermute | solution.py:1173
  17.9 15.0 %collective-permute-start.3 = (bf16[18,24,512]{2,1,0:T(8,128)(2,1)S(1)}, bf16[18,24,512]{2,1,0:T(8,128)(2,1)S(1)}, u32[]{:S(2)}, u32[]{:S(2)}) collective-permute-start(bf16[18,24,512]{2,1,0:T(8,128)(2,1)S(1)} %get-tuple-element.157), channel_id=1, source_target_pairs={{0,4},{4,0},{8,12},{12,8},{1,5},{5,1},{9,13},{13,9},{2,6},{6,2},{1... | collective-permute-start | bytes 1327112 | tf_op jit(solution)/shard_map/ppermute | solution.py:1167
  18.0 2.8 %collective-permute-start.5 = (f32[4,128]{1,0:T(4,128)S(1)}, f32[4,128]{1,0:T(4,128)S(1)}, u32[]{:S(2)}, u32[]{:S(2)}) collective-permute-start(f32[4,128]{1,0:T(4,128)S(1)} %add.58), channel_id=1, source_target_pairs={{0,32},{4,36},{8,40},{12,44},{16,48},{20,52},{24,56},{28,60},{32,0... | collective-permute-start | bytes 6152 | tf_op jit(solution)/shard_map/ppermute | solution.py:1182
  20.8 6.3 %collective-permute-start.6 = (f32[4,128]{1,0:T(4,128)S(1)}, f32[4,128]{1,0:T(4,128)S(1)}, u32[]{:S(2)}, u32[]{:S(2)}) collective-permute-start(f32[4,128]{1,0:T(4,128)S(1)} %add.60), channel_id=1, source_target_pairs={{0,128},{4,132},{8,136},{12,140},{16,144},{20,148},{24,152},{28,15... | collective-permute-start | bytes 6152 | tf_op jit(solution)/shard_map/ppermute | solution.py:1182
  27.2 5.0 %collective-permute-start.7 = (f32[4,128]{1,0:T(4,128)S(1)}, f32[4,128]{1,0:T(4,128)S(1)}, u32[]{:S(2)}, u32[]{:S(2)}) collective-permute-start(f32[4,128]{1,0:T(4,128)S(1)} %add.61), channel_id=1, source_target_pairs={{0,16},{4,20},{8,24},{12,28},{16,0},{20,4},{24,8},{28,12},{32,48},... | collective-permute-start | bytes 6152 | tf_op jit(solution)/shard_map/ppermute | solution.py:1182
  27.3 21.5 %copy-start.11 = (s32[4]{0:T(128)}, s32[4]{0:T(128)S(1)}, u32[]{:S(2)}) copy-start(s32[4]{0:T(128)S(1)} %pad_add_fusion.id_ref.refs_0_) | copy-start | bytes 52
  32.2 16.6 %copy-start.2 = (bf16[24,72,128]{2,1,0:T(8,128)(2,1)}, bf16[24,72,128]{2,1,0:T(8,128)(2,1)S(1)}, u32[]{:S(2)}) copy-start(bf16[24,72,128]{2,1,0:T(8,128)(2,1)S(1)} %collective-permute-done.left_ref) | copy-start | bytes 1327108
  32.2 16.6 %copy-start.3 = (bf16[24,72,128]{2,1,0:T(8,128)(2,1)}, bf16[24,72,128]{2,1,0:T(8,128)(2,1)S(1)}, u32[]{:S(2)}) copy-start(bf16[24,72,128]{2,1,0:T(8,128)(2,1)S(1)} %collective-permute-done.1.right_ref) | copy-start | bytes 1327108
  32.9 15.9 %copy-start.5 = (bf16[18,24,512]{2,1,0:T(8,128)(2,1)}, bf16[18,24,512]{2,1,0:T(8,128)(2,1)S(1)}, u32[]{:S(2)}) copy-start(bf16[18,24,512]{2,1,0:T(8,128)(2,1)S(1)} %collective-permute-done.3.refs_0_.top_ref) | copy-start | bytes 1327108
  33.6 15.2 %collective-permute-start.8 = (bf16[36,72,128]{2,1,0:T(8,128)(2,1)S(1)}, bf16[36,72,128]{2,1,0:T(8,128)(2,1)S(1)}, u32[]{:S(2)}, u32[]{:S(2)}) collective-permute-start(bf16[36,72,128]{2,1,0:T(8,128)(2,1)S(1)} %get-tuple-element.82), channel_id=1, source_target_pairs={{0,4},{4,0},{8,12},{12,8},{1,5},{5,1},{9,13},{13,9},{2,6},{6,2},{1... | collective-permute-start | bytes 1990664 | tf_op jit(solution)/shard_map/ppermute | solution.py:1167
  34.0 14.8 %collective-permute-start.9 = (bf16[36,72,128]{2,1,0:T(8,128)(2,1)S(1)}, bf16[36,72,128]{2,1,0:T(8,128)(2,1)S(1)}, u32[]{:S(2)}, u32[]{:S(2)}) collective-permute-start(bf16[36,72,128]{2,1,0:T(8,128)(2,1)S(1)} %get-tuple-element.83), channel_id=1, source_target_pairs={{4,8},{8,4},{5,9},{9,5},{6,10},{10,6},{7,11},{11,7},{20,24},{24,20... | collective-permute-start | bytes 1990664 | tf_op jit(solution)/shard_map/ppermute | solution.py:1173
  38.1 3.6 %collective-permute-start.10 = (f32[4,128]{1,0:T(4,128)S(1)}, f32[4,128]{1,0:T(4,128)S(1)}, u32[]{:S(2)}, u32[]{:S(2)}) collective-permute-start(f32[4,128]{1,0:T(4,128)S(1)} %get-tuple-element.84), channel_id=1, source_target_pairs={{0,64},{4,68},{8,72},{12,76},{16,80},{20,84},{24,88},{28,92},{32,9... | collective-permute-start | bytes 6152 | tf_op jit(solution)/shard_map/ppermute | solution.py:1182
  41.7 4.0 %collective-permute-start.11 = (f32[4,128]{1,0:T(4,128)S(1)}, f32[4,128]{1,0:T(4,128)S(1)}, u32[]{:S(2)}, u32[]{:S(2)}) collective-permute-start(f32[4,128]{1,0:T(4,128)S(1)} %add.63), channel_id=1, source_target_pairs={{0,8},{4,12},{8,0},{12,4},{16,24},{20,28},{24,16},{28,20},{32,40},... | collective-permute-start | bytes 6152 | tf_op jit(solution)/shard_map/ppermute | solution.py:1182
  41.7 17.6 %collective-permute-start.13 = (bf16[5,64,256]{2,1,0:T(8,128)(2,1)S(1)}, bf16[5,64,256]{2,1,0:T(8,128)(2,1)S(1)}, u32[]{:S(2)}, u32[]{:S(2)}) collective-permute-start(bf16[5,64,256]{2,1,0:T(8,128)(2,1)S(1)} %copy-done.10), channel_id=1, source_target_pairs={{0,2},{1,3},{2,0},{3,1},{4,6},{5,7},{6,4},{7,5},{8,10},{9,11},{10,... | collective-permute-start | bytes 491528 | tf_op jit(solution)/shard_map/ppermute | solution.py:1162
  44.5 14.8 %collective-permute-start.12 = (bf16[5,64,256]{2,1,0:T(8,128)(2,1)S(1)}, bf16[5,64,256]{2,1,0:T(8,128)(2,1)S(1)}, u32[]{:S(2)}, u32[]{:S(2)}) collective-permute-start(bf16[5,64,256]{2,1,0:T(8,128)(2,1)S(1)} %copy-done.10), channel_id=1, source_target_pairs={{0,1},{1,2},{2,3},{3,0},{4,5},{5,6},{6,7},{7,4},{8,9},{9,10},{10,1... | collective-permute-start | bytes 491528 | tf_op jit(solution)/shard_map/ppermute | solution.py:1162
  45.7 13.6 %collective-permute-start.14 = (bf16[5,64,256]{2,1,0:T(8,128)(2,1)S(1)}, bf16[5,64,256]{2,1,0:T(8,128)(2,1)S(1)}, u32[]{:S(2)}, u32[]{:S(2)}) collective-permute-start(bf16[5,64,256]{2,1,0:T(8,128)(2,1)S(1)} %copy-done.10), channel_id=1, source_target_pairs={{0,3},{1,0},{2,1},{3,2},{4,7},{5,4},{6,5},{7,6},{8,11},{9,8},{10,9... | collective-permute-start | bytes 491528 | tf_op jit(solution)/shard_map/ppermute | solution.py:1162
  59.3 11.1 %collective-permute-start.15 = (bf16[160,1024]{1,0:T(8,128)(2,1)}, bf16[160,1024]{1,0:T(8,128)(2,1)S(1)}, u32[]{:S(2)}, u32[]{:S(2)}) collective-permute-start(bf16[160,1024]{1,0:T(8,128)(2,1)} %get-tuple-element.89), channel_id=1, source_target_pairs={{0,1},{1,2},{2,3},{3,0},{4,5},{5,6},{6,7},{7,4},{8,9},{9,10},{10,1... | collective-permute-start | bytes 983048 | tf_op jit(solution)/shard_map/ppermute | solution.py:1162
  59.4 14.9 %collective-permute-start.16 = (bf16[160,1024]{1,0:T(8,128)(2,1)}, bf16[160,1024]{1,0:T(8,128)(2,1)S(1)}, u32[]{:S(2)}, u32[]{:S(2)}) collective-permute-start(bf16[160,1024]{1,0:T(8,128)(2,1)} %get-tuple-element.90), channel_id=1, source_target_pairs={{0,2},{1,3},{2,0},{3,1},{4,6},{5,7},{6,4},{7,5},{8,10},{9,11},{10,... | collective-permute-start | bytes 983048 | tf_op jit(solution)/shard_map/ppermute | solution.py:1162
  61.6 15.6 %collective-permute-start.17 = (bf16[160,1024]{1,0:T(8,128)(2,1)}, bf16[160,1024]{1,0:T(8,128)(2,1)S(1)}, u32[]{:S(2)}, u32[]{:S(2)}) collective-permute-start(bf16[160,1024]{1,0:T(8,128)(2,1)} %get-tuple-element.91), channel_id=1, source_target_pairs={{0,3},{1,0},{2,1},{3,2},{4,7},{5,4},{6,5},{7,6},{8,11},{9,8},{10,9... | collective-permute-start | bytes 983048 | tf_op jit(solution)/shard_map/ppermute | solution.py:1162
  79.9 13.1 %collective-permute-start.18 = (bf16[224,1024]{1,0:T(8,128)(2,1)S(1)}, bf16[224,1024]{1,0:T(8,128)(2,1)S(1)}, u32[]{:S(2)}, u32[]{:S(2)}) collective-permute-start(bf16[224,1024]{1,0:T(8,128)(2,1)S(1)} %get-tuple-element.101), channel_id=1, source_target_pairs={{0,1},{1,2},{2,3},{3,0},{4,5},{5,6},{6,7},{7,4},{8,9},{9,10},{10,1... | collective-permute-start | bytes 1376264 | tf_op jit(solution)/shard_map/ppermute | solution.py:1162
  81.3 23.1 %collective-permute-start.19 = (bf16[224,1024]{1,0:T(8,128)(2,1)S(1)}, bf16[224,1024]{1,0:T(8,128)(2,1)S(1)}, u32[]{:S(2)}, u32[]{:S(2)}) collective-permute-start(bf16[224,1024]{1,0:T(8,128)(2,1)S(1)} %get-tuple-element.102), channel_id=1, source_target_pairs={{0,2},{1,3},{2,0},{3,1},{4,6},{5,7},{6,4},{7,5},{8,10},{9,11},{10,... | collective-permute-start | bytes 1376264 | tf_op jit(solution)/shard_map/ppermute | solution.py:1162
  84.4 20.0 %collective-permute-start.20 = (bf16[224,1024]{1,0:T(8,128)(2,1)S(1)}, bf16[224,1024]{1,0:T(8,128)(2,1)S(1)}, u32[]{:S(2)}, u32[]{:S(2)}) collective-permute-start(bf16[224,1024]{1,0:T(8,128)(2,1)S(1)} %get-tuple-element.103), channel_id=1, source_target_pairs={{0,3},{1,0},{2,1},{3,2},{4,7},{5,4},{6,5},{7,6},{8,11},{9,8},{10,9... | collective-permute-start | bytes 1376264 | tf_op jit(solution)/shard_map/ppermute | solution.py:1162
  107.6 3.0 %collective-permute-start.21 = (bf16[1024,256]{1,0:T(8,128)(2,1)S(1)}, bf16[1024,256]{1,0:T(8,128)(2,1)S(1)}, u32[]{:S(2)}, u32[]{:S(2)}) collective-permute-start(bf16[1024,256]{1,0:T(8,128)(2,1)S(1)} %bitcast.14), channel_id=1, source_target_pairs={{0,4},{4,0},{8,12},{12,8},{16,20},{20,16},{24,28},{28,24},{32,36},... | collective-permute-start | bytes 1572872 | tf_op jit(solution)/shard_map/ppermute | solution.py:1182
  111.2 11.8 %collective-permute-start.22 = (bf16[320,256]{1,0:T(8,128)(2,1)S(1)}, bf16[320,256]{1,0:T(8,128)(2,1)S(1)}, u32[]{:S(2)}, u32[]{:S(2)}) collective-permute-start(bf16[320,256]{1,0:T(8,128)(2,1)S(1)} %get-tuple-element.109), channel_id=1, source_target_pairs={{0,16},{4,20},{8,24},{12,28},{16,0},{20,4},{24,8},{28,12},{32,48},... | collective-permute-start | bytes 491528 | tf_op jit(solution)/shard_map/ppermute | solution.py:1182
  111.3 11.7 %collective-permute-start.23 = (bf16[320,256]{1,0:T(8,128)(2,1)S(1)}, bf16[320,256]{1,0:T(8,128)(2,1)S(1)}, u32[]{:S(2)}, u32[]{:S(2)}) collective-permute-start(bf16[320,256]{1,0:T(8,128)(2,1)S(1)} %get-tuple-element.110), channel_id=1, source_target_pairs={{0,8},{4,12},{8,0},{12,4},{16,24},{20,28},{24,16},{28,20},{32,40},... | collective-permute-start | bytes 491528 | tf_op jit(solution)/shard_map/ppermute | solution.py:1182
  114.8 10.2 %collective-permute-start.24 = (bf16[320,256]{1,0:T(8,128)(2,1)S(1)}, bf16[320,256]{1,0:T(8,128)(2,1)S(1)}, u32[]{:S(2)}, u32[]{:S(2)}) collective-permute-start(bf16[320,256]{1,0:T(8,128)(2,1)S(1)} %get-tuple-element.111), channel_id=1, source_target_pairs={{0,24},{4,28},{8,16},{12,20},{16,8},{20,12},{24,0},{28,4},{32,56},... | collective-permute-start | bytes 491528 | tf_op jit(solution)/shard_map/ppermute | solution.py:1182
  123.0 20.1 %copy-start.13 = (s32[4]{0:T(128)S(1)}, s32[4]{0:T(128)}, u32[]{:S(2)}) copy-start(s32[4]{0:T(128)} %copy-done.11) | copy-start | bytes 52
  126.3 16.8 %collective-permute-start.27 = (bf16[18,60,512]{2,1,0:T(8,128)(2,1)}, bf16[18,60,512]{2,1,0:T(8,128)(2,1)S(1)}, u32[]{:S(2)}, u32[]{:S(2)}) collective-permute-start(bf16[18,60,512]{2,1,0:T(8,128)(2,1)} %get-tuple-element.123), channel_id=1, source_target_pairs={{0,4},{4,0},{8,12},{12,8},{1,5},{5,1},{9,13},{13,9},{2,6},{6,2},{1... | collective-permute-start | bytes 3317768 | tf_op jit(solution)/shard_map/ppermute | solution.py:1167
  127.5 4.4 %collective-permute-start.25 = (bf16[160,256]{1,0:T(8,128)(2,1)}, bf16[160,256]{1,0:T(8,128)(2,1)}, u32[]{:S(2)}, u32[]{:S(2)}) collective-permute-start(bf16[160,256]{1,0:T(8,128)(2,1)} %get-tuple-element.120), channel_id=1, source_target_pairs={{0,32},{4,36},{8,40},{12,44},{16,48},{20,52},{24,56},{28,60},{32,0... | collective-permute-start | bytes 245768 | tf_op jit(solution)/shard_map/ppermute | solution.py:1182
  128.7 14.5 %collective-permute-start.28 = (bf16[18,36,512]{2,1,0:T(8,128)(2,1)}, bf16[18,36,512]{2,1,0:T(8,128)(2,1)S(1)}, u32[]{:S(2)}, u32[]{:S(2)}) collective-permute-start(bf16[18,36,512]{2,1,0:T(8,128)(2,1)} %copy-done.19), channel_id=1, source_target_pairs={{4,8},{8,4},{5,9},{9,5},{6,10},{10,6},{7,11},{11,7},{20,24},{24,20... | collective-permute-start | bytes 1990664 | tf_op jit(solution)/shard_map/ppermute | solution.py:1173
  133.5 7.2 %collective-permute-start.26 = (bf16[80,256]{1,0:T(8,128)(2,1)S(1)}, bf16[80,256]{1,0:T(8,128)(2,1)S(1)}, u32[]{:S(2)}, u32[]{:S(2)}) collective-permute-start(bf16[80,256]{1,0:T(8,128)(2,1)S(1)} %select_convert_fusion), channel_id=1, source_target_pairs={{0,64},{4,68},{8,72},{12,76},{16,80},{20,84},{24,88},{28,92},{32,9... | collective-permute-start | bytes 122888 | tf_op jit(solution)/shard_map/ppermute | solution.py:1182
  136.4 27.3 %collective-permute-start.32 = (bf16[18,24,512]{2,1,0:T(8,128)(2,1)}, bf16[18,24,512]{2,1,0:T(8,128)(2,1)S(1)}, u32[]{:S(2)}, u32[]{:S(2)}) collective-permute-start(bf16[18,24,512]{2,1,0:T(8,128)(2,1)} %copy-done.20), channel_id=1, source_target_pairs={{4,8},{8,4},{5,9},{9,5},{6,10},{10,6},{7,11},{11,7},{20,24},{24,20... | collective-permute-start | bytes 1327112 | tf_op jit(solution)/shard_map/ppermute | solution.py:1173
  145.7 21.4 %collective-permute-start.30 = (bf16[24,72,128]{2,1,0:T(8,128)(2,1)S(1)}, bf16[24,72,128]{2,1,0:T(8,128)(2,1)S(1)}, u32[]{:S(2)}, u32[]{:S(2)}) collective-permute-start(bf16[24,72,128]{2,1,0:T(8,128)(2,1)S(1)} %get-tuple-element.128), channel_id=1, source_target_pairs={{0,16},{16,32},{32,48},{48,64},{64,80},{80,96},{96,112},{112,128},... | collective-permute-start | bytes 1327112 | tf_op jit(solution)/shard_map/ppermute | solution.py:1162
  145.8 21.3 %collective-permute-start.31 = (bf16[24,72,128]{2,1,0:T(8,128)(2,1)S(1)}, bf16[24,72,128]{2,1,0:T(8,128)(2,1)S(1)}, u32[]{:S(2)}, u32[]{:S(2)}) collective-permute-start(bf16[24,72,128]{2,1,0:T(8,128)(2,1)S(1)} %get-tuple-element.129), channel_id=1, source_target_pairs={{0,240},{16,0},{32,16},{48,32},{64,48},{80,64},{96,80},{112,96},{1... | collective-permute-start | bytes 1327112 | tf_op jit(solution)/shard_map/ppermute | solution.py:1162
  149.5 17.6 %collective-permute-start.29 = (bf16[40,256]{1,0:T(8,128)(2,1)S(1)}, bf16[40,256]{1,0:T(8,128)(2,1)S(1)}, u32[]{:S(2)}, u32[]{:S(2)}) collective-permute-start(bf16[40,256]{1,0:T(8,128)(2,1)S(1)} %select_convert_fusion.1), channel_id=1, source_target_pairs={{0,128},{4,132},{8,136},{12,140},{16,144},{20,148},{24,152},{28,15... | collective-permute-start | bytes 61448 | tf_op jit(solution)/shard_map/ppermute | solution.py:1182
  167.1 7.4 %collective-permute-start.33 = (bf16[104,256]{1,0:T(8,128)(2,1)S(1)}, bf16[104,256]{1,0:T(8,128)(2,1)S(1)}, u32[]{:S(2)}, u32[]{:S(2)}) collective-permute-start(bf16[104,256]{1,0:T(8,128)(2,1)S(1)} %pad_maximum_fusion.3), channel_id=1, source_target_pairs={{0,128},{4,132},{8,136},{12,140},{16,144},{20,148},{24,152},{28,15... | collective-permute-start | bytes 159752 | tf_op jit(solution)/shard_map/ppermute | solution.py:1182
  174.6 26.1 %copy-start.17 = (f32[4,128]{1,0:T(4,128)S(1)}, f32[4,128]{1,0:T(4,128)}, u32[]{:S(2)}) copy-start(f32[4,128]{1,0:T(4,128)} %add_multiply_fusion) | copy-start | bytes 6148
  174.6 6.3 %collective-permute-start.34 = (bf16[144,256]{1,0:T(8,128)(2,1)S(1)}, bf16[144,256]{1,0:T(8,128)(2,1)S(1)}, u32[]{:S(2)}, u32[]{:S(2)}) collective-permute-start(bf16[144,256]{1,0:T(8,128)(2,1)S(1)} %pad_maximum_fusion.2), channel_id=1, source_target_pairs={{0,64},{4,68},{8,72},{12,76},{16,80},{20,84},{24,88},{28,92},{32,9... | collective-permute-start | bytes 221192 | tf_op jit(solution)/shard_map/ppermute | solution.py:1182
  180.9 3.7 %collective-permute-start.35 = (bf16[224,256]{1,0:T(8,128)(2,1)S(1)}, bf16[224,256]{1,0:T(8,128)(2,1)S(1)}, u32[]{:S(2)}, u32[]{:S(2)}) collective-permute-start(bf16[224,256]{1,0:T(8,128)(2,1)S(1)} %pad_maximum_fusion.1), channel_id=1, source_target_pairs={{0,32},{4,36},{8,40},{12,44},{16,48},{20,52},{24,56},{28,60},{32,0... | collective-permute-start | bytes 344072 | tf_op jit(solution)/shard_map/ppermute | solution.py:1182
  184.7 11.9 %collective-permute-start.38 = (bf16[384,256]{1,0:T(8,128)(2,1)S(1)}, bf16[384,256]{1,0:T(8,128)(2,1)S(1)}, u32[]{:S(2)}, u32[]{:S(2)}) collective-permute-start(bf16[384,256]{1,0:T(8,128)(2,1)S(1)} %pad_maximum_fusion), channel_id=1, source_target_pairs={{0,24},{4,28},{8,16},{12,20},{16,8},{20,12},{24,0},{28,4},{32,56},... | collective-permute-start | bytes 589832 | tf_op jit(solution)/shard_map/ppermute | solution.py:1182
  184.8 11.8 %collective-permute-start.37 = (bf16[384,256]{1,0:T(8,128)(2,1)S(1)}, bf16[384,256]{1,0:T(8,128)(2,1)S(1)}, u32[]{:S(2)}, u32[]{:S(2)}) collective-permute-start(bf16[384,256]{1,0:T(8,128)(2,1)S(1)} %pad_maximum_fusion), channel_id=1, source_target_pairs={{0,8},{4,12},{8,0},{12,4},{16,24},{20,28},{24,16},{28,20},{32,40},... | collective-permute-start | bytes 589832 | tf_op jit(solution)/shard_map/ppermute | solution.py:1182
  186.9 9.7 %collective-permute-start.36 = (bf16[384,256]{1,0:T(8,128)(2,1)S(1)}, bf16[384,256]{1,0:T(8,128)(2,1)S(1)}, u32[]{:S(2)}, u32[]{:S(2)}) collective-permute-start(bf16[384,256]{1,0:T(8,128)(2,1)S(1)} %pad_maximum_fusion), channel_id=1, source_target_pairs={{0,16},{4,20},{8,24},{12,28},{16,0},{20,4},{24,8},{28,12},{32,48},... | collective-permute-start | bytes 589832 | tf_op jit(solution)/shard_map/ppermute | solution.py:1182
  197.2 3.4 %collective-permute-start.39 = (bf16[1344,256]{1,0:T(8,128)(2,1)S(1)}, bf16[1344,256]{1,0:T(8,128)(2,1)S(1)}, u32[]{:S(2)}, u32[]{:S(2)}) collective-permute-start(bf16[1344,256]{1,0:T(8,128)(2,1)S(1)} %get-tuple-element.141.refs_1_), channel_id=1, source_target_pairs={{0,4},{4,0},{8,12},{12,8},{16,20},{20,16},{24,28},{28,24},{32,36},... | collective-permute-start | bytes 2064392 | tf_op jit(solution)/shard_map/ppermute | solution.py:1182
  (18 other events, 89.2 us)

commit v2 on v1

--- a/solution.py
+++ b/solution.py
@@ -207,7 +207,7 @@
 
 def halo_specs(halos, lanes):
     return [
-        by_lanes(*halo.shape[:2], lanes=lanes) if number in (0, 3, 4) else whole(*halo.shape)
+        by_lanes(*halo.shape[:2], lanes=lanes) if number in (0, 3, 4) else vmem()
         for number, halo in enumerate(halos)
     ]
 
@@ -369,7 +369,7 @@
             pltpu.VMEM((8, fan), f32),
             pltpu.VMEM((16, 4 * fan), f32),
         ],
-        compiler_params=params(58),
+        compiler_params=params(40),
         cost_estimate=cost(2 * cells * chan * (4 * fan + 27), 20_000_000),
         name="conv_forward",
     )(ids, stay(halos[0]), *halos[1:], kernel, weight, pooled, cotangent)

time: 207 us -> 205 us (level)
  local copies, waits for them, and re-layouts: 8.55 us -> 5.79 us
    unnamed x54 -> x42, local copies, waits for them, and re-layouts: 6.56 us -> 3.59 us
  transfers between devices with their start and end apart: 40 -> 40, of which waited for: 19 -> 19; matrix products, arithmetic and copies ran while one was open for 3% -> 2% of each run, Pallas kernels for 18% -> 17%
where the time goes in v2:
time: 205 us; the launch traced here: 204 us
  starting transfers between devices  77 us (38%)
  waiting for transfers between devices  66.9 us (33%)
  Pallas kernels  51.2 us (25%)
  local copies, waits for them, and re-layouts  5.79 us (3%)
  other arithmetic  2.15 us (1%)
    ppermute x20, waiting for transfers between devices, swap(): return lax.ppermute(value, GRID, [(i, i ^ mask) for i in range(count)])  37.7 us
    ppermute x20, starting transfers between devices, swap(): return lax.ppermute(value, GRID, [(i, i ^ mask) for i in range(count)])  36.9 us
    ppermute x13, waiting for transfers between devices, shift(): return lax.ppermute(value, axis, pairs)  26.9 us
    ppermute x13, starting transfers between devices, shift(): return lax.ppermute(value, axis, pairs)  23.2 us
    ppermute x4, starting transfers between devices, to_other_chip(): return lax.ppermute(value, 'lat', pairs + [(j, i) for i, j in pairs])  15.4 us
    pallas_call x1, Pallas kernels, conv_forward(): pl.pallas_call(conv_body, grid=(chan // lanes,), in_specs=[smem()] + halo...  8.12 us
    pallas_call x1, Pallas kernels, scatter_grads(): pl.pallas_call(scatter_body, grid=(chan // lanes,), in_specs=[smem(), who...  7.05 us
    pallas_call x1, Pallas kernels, tap_sums(): pl.pallas_call(taps_body, grid=(chan // lanes,), in_specs=[by_lanes(3, ce...  6.74 us
  transfers between devices with their start and end apart: 40, of which 19 were waited for; matrix products, arithmetic and copies ran while one was open for 2% of the time, Pallas kernels for 17%

profile of v2, /device:TPU:1, one launch (start us, length us, event | category | flops | bytes accessed | tf_op | source)
XLA Modules:
  0.0 204.2 jit_solution(2155818234274973662)
XLA Ops:
  0.6 3.0 %edges.1 = (bf16[24,72,128]{2,1,0:T(8,128)(2,1)}, bf16[24,72,128]{2,1,0:T(8,128)(2,1)}, f32[1,512]{1,0:T(1,128)S(1)}) custom-call(bf16[24,24,512]{2,1,0:T(8,128)(2,1)} %tile_ref.5), custom_call_target="tpu_custom_call" | custom-call | flops 294912 | bytes 2000000 | tf_op jit(solution)/shard_map/edges/pallas_call | solution.py:135
  3.6 3.2 %collective-permute-start.2 = (f32[4,128]{1,0:T(4,128)S(1)}, f32[4,128]{1,0:T(4,128)S(1)}, u32[]{:S(2)}, u32[]{:S(2)}) collective-permute-start(f32[4,128]{1,0:T(4,128)S(1)} %bitcast.12), channel_id=1, source_target_pairs={{0,4},{4,0},{8,12},{12,8},{16,20},{20,16},{24,28},{28,24},{32,36},... | collective-permute-start | bytes 6152 | tf_op jit(solution)/shard_map/ppermute | solution.py:1182
  6.9 4.9 %collective-permute-start.1 = (bf16[24,72,128]{2,1,0:T(8,128)(2,1)}, bf16[24,72,128]{2,1,0:T(8,128)(2,1)S(1)}, u32[]{:S(2)}, u32[]{:S(2)}) collective-permute-start(bf16[24,72,128]{2,1,0:T(8,128)(2,1)} %get-tuple-element.78), channel_id=1, source_target_pairs={{0,240},{16,0},{32,16},{48,32},{64,48},{80,64},{96,80},{112,96},{1... | collective-permute-start | bytes 1327112 | tf_op jit(solution)/shard_map/ppermute | solution.py:1162
  11.7 2.2 %constant_dynamic-slice_fusion = (bf16[18,24,512]{2,1,0:T(8,128)(2,1)}, bf16[18,24,512]{2,1,0:T(8,128)(2,1)}) fusion(bf16[24,24,512]{2,1,0:T(8,128)(2,1)} %tile_ref.5, s32[]{:T(128)S(6)} %select_n.58, s32[]{:T(128)S(6)} %select_n.59), kind=kLoop, calls=%fused_computation.19 | loop fusion | bytes 1769480 | tf_op jit(solution)/shard_map/dynamic_slice | solution.py:1239
  13.9 4.9 %collective-permute-start.4 = (bf16[18,24,512]{2,1,0:T(8,128)(2,1)}, bf16[18,24,512]{2,1,0:T(8,128)(2,1)S(1)}, u32[]{:S(2)}, u32[]{:S(2)}) collective-permute-start(bf16[18,24,512]{2,1,0:T(8,128)(2,1)} %get-tuple-element.156), channel_id=1, source_target_pairs={{4,8},{8,4},{5,9},{9,5},{6,10},{10,6},{7,11},{11,7},{20,24},{24,20... | collective-permute-start | bytes 1327112 | tf_op jit(solution)/shard_map/ppermute | solution.py:1173
  19.0 2.7 %collective-permute-done.5 = f32[4,128]{1,0:T(4,128)S(1)} collective-permute-done((f32[4,128]{1,0:T(4,128)S(1)}, f32[4,128]{1,0:T(4,128)S(1)}, u32[]{:S(2)}, u32[]{:S(2)}) %collective-permute-start.5) | collective-permute-done | bytes 2080 | tf_op jit(solution)/shard_map/ppermute | solution.py:1182
  21.8 4.4 %collective-permute-start.6 = (f32[4,128]{1,0:T(4,128)S(1)}, f32[4,128]{1,0:T(4,128)S(1)}, u32[]{:S(2)}, u32[]{:S(2)}) collective-permute-start(f32[4,128]{1,0:T(4,128)S(1)} %add.60), channel_id=1, source_target_pairs={{0,128},{4,132},{8,136},{12,140},{16,144},{20,148},{24,152},{28,15... | collective-permute-start | bytes 6152 | tf_op jit(solution)/shard_map/ppermute | solution.py:1182
  26.2 2.0 collective-permute-done.6
  28.2 5.0 %collective-permute-done.7 = f32[4,128]{1,0:T(4,128)S(1)} collective-permute-done((f32[4,128]{1,0:T(4,128)S(1)}, f32[4,128]{1,0:T(4,128)S(1)}, u32[]{:S(2)}, u32[]{:S(2)}) %collective-permute-start.7) | collective-permute-done | bytes 2080 | tf_op jit(solution)/shard_map/ppermute | solution.py:1182
  34.9 4.1 %collective-permute-start.9 = (bf16[36,72,128]{2,1,0:T(8,128)(2,1)S(1)}, bf16[36,72,128]{2,1,0:T(8,128)(2,1)S(1)}, u32[]{:S(2)}, u32[]{:S(2)}) collective-permute-start(bf16[36,72,128]{2,1,0:T(8,128)(2,1)S(1)} %get-tuple-element.83), channel_id=1, source_target_pairs={{4,8},{8,4},{5,9},{9,5},{6,10},{10,6},{7,11},{11,7},{20,24},{24,20... | collective-permute-start | bytes 1990664 | tf_op jit(solution)/shard_map/ppermute | solution.py:1173
  39.1 2.6 %collective-permute-start.10 = (f32[4,128]{1,0:T(4,128)S(1)}, f32[4,128]{1,0:T(4,128)S(1)}, u32[]{:S(2)}, u32[]{:S(2)}) collective-permute-start(f32[4,128]{1,0:T(4,128)S(1)} %get-tuple-element.84), channel_id=1, source_target_pairs={{0,64},{4,68},{8,72},{12,76},{16,80},{20,84},{24,88},{28,92},{32,9... | collective-permute-start | bytes 6152 | tf_op jit(solution)/shard_map/ppermute | solution.py:1182
  42.7 2.8 %collective-permute-start.13 = (bf16[5,64,256]{2,1,0:T(8,128)(2,1)S(1)}, bf16[5,64,256]{2,1,0:T(8,128)(2,1)S(1)}, u32[]{:S(2)}, u32[]{:S(2)}) collective-permute-start(bf16[5,64,256]{2,1,0:T(8,128)(2,1)S(1)} %copy-done.11), channel_id=1, source_target_pairs={{0,2},{1,3},{2,0},{3,1},{4,6},{5,7},{6,4},{7,5},{8,10},{9,11},{10,... | collective-permute-start | bytes 491528 | tf_op jit(solution)/shard_map/ppermute | solution.py:1162
  46.7 2.5 %collective-permute-start.14 = (bf16[5,64,256]{2,1,0:T(8,128)(2,1)S(1)}, bf16[5,64,256]{2,1,0:T(8,128)(2,1)S(1)}, u32[]{:S(2)}, u32[]{:S(2)}) collective-permute-start(bf16[5,64,256]{2,1,0:T(8,128)(2,1)S(1)} %copy-done.11), channel_id=1, source_target_pairs={{0,3},{1,0},{2,1},{3,2},{4,7},{5,4},{6,5},{7,6},{8,11},{9,8},{10,9... | collective-permute-start | bytes 491528 | tf_op jit(solution)/shard_map/ppermute | solution.py:1162
  49.2 8.1 %conv_forward.1 = (bf16[4,576,512]{2,1,0:T(8,128)(2,1)}, f32[144,1024]{1,0:T(8,128)}, bf16[160,1024]{1,0:T(8,128)(2,1)S(1)}, bf16[160,1024]{1,0:T(8,128)(2,1)S(1...) custom-call(s32[4]{0:T(128)S(1)} %pad_add_fusion.id_ref.refs_0_, ...), custom_call_target="tpu_custom_call" | custom-call | flops 619905024 | bytes 20000000 | tf_op jit(solution)/shard_map/conv_forward/pallas_call | solution.py:344
  57.9 2.5 %collective-permute-start.16 = (bf16[160,1024]{1,0:T(8,128)(2,1)S(1)}, bf16[160,1024]{1,0:T(8,128)(2,1)S(1)}, u32[]{:S(2)}, u32[]{:S(2)}) collective-permute-start(bf16[160,1024]{1,0:T(8,128)(2,1)S(1)} %get-tuple-element.90), channel_id=1, source_target_pairs={{0,2},{1,3},{2,0},{3,1},{4,6},{5,7},{6,4},{7,5},{8,10},{9,11},{10,... | collective-permute-start | bytes 983048 | tf_op jit(solution)/shard_map/ppermute | solution.py:1162
  61.5 6.3 %extend.1 = (bf16[60,80,512]{2,1,0:T(8,128)(2,1)}, f32[8,128]{1,0:T(8,128)S(1)}) custom-call(s32[4]{0:T(128)S(1)} %pad_add_fusion.id_ref.refs_0_, bf16[24,24,512]{2,1,0:T(8,128)(2,1)} %tile_ref.5, bf16[24,72,128]{2,1,0:T(8,128)(2,1)} %copy-done.2, bf16[24,72,128]{2,1,0:T(8,128)(2,1)} %copy-done.3, bf16[18,24,512]{2,1,0:T(8,128)(2,1)} %copy-done.5, ...), custom_call_target="tpu_custom_call" | custom-call | flops 1000000 | bytes 10000000 | tf_op jit(solution)/shard_map/extend/pallas_call | solution.py:765
  67.8 5.7 %collective-permute-done.16.two_ref = bf16[160,1024]{1,0:T(8,128)(2,1)S(1)} collective-permute-done((bf16[160,1024]{1,0:T(8,128)(2,1)S(1)}, bf16[160,1024]{1,0:T(8,128)(2,1)S(1)}, u32[]{:S(2)}, u32[]{:S(2)}) %collective-permute-start.16) | collective-permute-done | bytes 327712 | tf_op jit(solution)/shard_map/ppermute | solution.py:1162
  75.0 2.1 %project.1 = (bf16[256,256]{1,0:T(8,128)(2,1)S(1)}, bf16[144,1024]{1,0:T(8,128)(2,1)S(1)}, bf16[224,1024]{1,0:T(8,128)(2,1)S(1)}, bf16[224,1024]{1,0:T(8,128)(2,...) custom-call(s32[4]{0:T(128)S(1)} %pad_add_fusion.id_ref.refs_0_, ...), custom_call_target="tpu_custom_call" | custom-call | flops 226492416 | bytes 4000000 | tf_op jit(solution)/shard_map/project/pallas_call | solution.py:451
  77.7 2.3 %collective-permute-start.18 = (bf16[224,1024]{1,0:T(8,128)(2,1)S(1)}, bf16[224,1024]{1,0:T(8,128)(2,1)S(1)}, u32[]{:S(2)}, u32[]{:S(2)}) collective-permute-start(bf16[224,1024]{1,0:T(8,128)(2,1)S(1)} %get-tuple-element.101), channel_id=1, source_target_pairs={{0,1},{1,2},{2,3},{3,0},{4,5},{5,6},{6,7},{7,4},{8,9},{9,10},{10,1... | collective-permute-start | bytes 1376264 | tf_op jit(solution)/shard_map/ppermute | solution.py:1162
  80.1 2.3 %collective-permute-start.19 = (bf16[224,1024]{1,0:T(8,128)(2,1)S(1)}, bf16[224,1024]{1,0:T(8,128)(2,1)S(1)}, u32[]{:S(2)}, u32[]{:S(2)}) collective-permute-start(bf16[224,1024]{1,0:T(8,128)(2,1)S(1)} %get-tuple-element.102), channel_id=1, source_target_pairs={{0,2},{1,3},{2,0},{3,1},{4,6},{5,7},{6,4},{7,5},{8,10},{9,11},{10,... | collective-permute-start | bytes 1376264 | tf_op jit(solution)/shard_map/ppermute | solution.py:1162
  82.5 8.4 %collective-permute-done.18.one_ref = bf16[224,1024]{1,0:T(8,128)(2,1)S(1)} collective-permute-done((bf16[224,1024]{1,0:T(8,128)(2,1)S(1)}, bf16[224,1024]{1,0:T(8,128)(2,1)S(1)}, u32[]{:S(2)}, u32[]{:S(2)}) %collective-permute-start.18) | collective-permute-done | bytes 458784 | tf_op jit(solution)/shard_map/ppermute | solution.py:1162
  90.9 11.4 %collective-permute-done.19.two_ref = bf16[224,1024]{1,0:T(8,128)(2,1)S(1)} collective-permute-done((bf16[224,1024]{1,0:T(8,128)(2,1)S(1)}, bf16[224,1024]{1,0:T(8,128)(2,1)S(1)}, u32[]{:S(2)}, u32[]{:S(2)}) %collective-permute-start.19) | collective-permute-done | bytes 458784 | tf_op jit(solution)/shard_map/ppermute | solution.py:1162
  102.3 3.1 %weight_grads.1 = (f32[2,512,256]{2,1,0:T(8,128)S(1)}, bf16[2,512,256]{2,1,0:T(8,128)(2,1)S(1)}, bf16[576,1024]{1,0:T(8,128)(2,1)S(1)}, f32[4,64,256]{2,1,0:T(8,128)S(1)}, f32[1,256]{1,0:T(1,128)S(1)}) custom-call(s32[4]{0:T(128)S(1)} %pad_add_fusion.id_ref.refs_0_, bf16[144,1024]{1,0:T(8,128)(2,1)S(1)} %get-tuple-element.98.own_ref, ...), custom_call_target="tpu_custom_call" | custom-call | flops 603979776 | bytes 6000000 | tf_op jit(solution)/shard_map/weight_grads/pallas_call | solution.py:514
  105.5 1.4 collective-permute-start.21
  106.9 1.5 collective-permute-done.21.got_ref
  109.2 3.6 %collective-permute-start.23 = (bf16[320,256]{1,0:T(8,128)(2,1)S(1)}, bf16[320,256]{1,0:T(8,128)(2,1)S(1)}, u32[]{:S(2)}, u32[]{:S(2)}) collective-permute-start(bf16[320,256]{1,0:T(8,128)(2,1)S(1)} %get-tuple-element.110), channel_id=1, source_target_pairs={{0,8},{4,12},{8,0},{12,4},{16,24},{20,28},{24,16},{28,20},{32,40},... | collective-permute-start | bytes 491528 | tf_op jit(solution)/shard_map/ppermute | solution.py:1182
  113.0 7.0 %scatter_grads.1 = (bf16[3,576,512]{2,1,0:T(8,128)(2,1)}, bf16[24,24,512]{2,1,0:T(8,128)(2,1)}, bf16[24,18,512]{2,1,0:T(8,128)(2,1)}, bf16[24,18,512]{2,1,0:T(8,...) custom-call(s32[4]{0:T(128)S(1)} %pad_add_fusion.id_ref.refs_0_, ...), custom_call_target="tpu_custom_call" | custom-call | flops 619905024 | bytes 15000000 | tf_op jit(solution)/shard_map/scatter_grads/pallas_call | solution.py:699
  120.9 2.0 collective-permute-done.24.three_ref
  126.6 2.0 collective-permute-start.28
  131.3 2.8 %collective-permute-start.26 = (bf16[80,256]{1,0:T(8,128)(2,1)S(1)}, bf16[80,256]{1,0:T(8,128)(2,1)S(1)}, u32[]{:S(2)}, u32[]{:S(2)}) collective-permute-start(bf16[80,256]{1,0:T(8,128)(2,1)S(1)} %select_convert_fusion), channel_id=1, source_target_pairs={{0,64},{4,68},{8,72},{12,76},{16,80},{20,84},{24,88},{28,92},{32,9... | collective-permute-start | bytes 122888 | tf_op jit(solution)/shard_map/ppermute | solution.py:1182
  134.2 4.4 %collective-permute-start.32 = (bf16[18,24,512]{2,1,0:T(8,128)(2,1)}, bf16[18,24,512]{2,1,0:T(8,128)(2,1)S(1)}, u32[]{:S(2)}, u32[]{:S(2)}) collective-permute-start(bf16[18,24,512]{2,1,0:T(8,128)(2,1)} %copy-done.16), channel_id=1, source_target_pairs={{4,8},{8,4},{5,9},{9,5},{6,10},{10,6},{7,11},{11,7},{20,24},{24,20... | collective-permute-start | bytes 1327112 | tf_op jit(solution)/shard_map/ppermute | solution.py:1173
  139.5 1.5 collective-permute-done.28.corner_ref
  141.1 2.3 %home.1 = (bf16[24,72,128]{2,1,0:T(8,128)(2,1)S(1)}, bf16[24,72,128]{2,1,0:T(8,128)(2,1)S(1)}) custom-call(s32[4]{0:T(128)S(1)} %pad_add_fusion.id_ref.refs_0_, bf16[24,18,512]{2,1,0:T(8,128)(2,1)} %get-tuple-element.121.left_ref, bf16[24,18,512]{2,1,0:T(8,128)(2,1)} %get-tuple-element.122.right_ref, ...), custom_call_target="tpu_custom_call" | custom-call | flops 221184 | bytes 5000000 | tf_op jit(solution)/shard_map/home/pallas_call | solution.py:879
  143.7 3.6 %collective-permute-start.31 = (bf16[24,72,128]{2,1,0:T(8,128)(2,1)S(1)}, bf16[24,72,128]{2,1,0:T(8,128)(2,1)S(1)}, u32[]{:S(2)}, u32[]{:S(2)}) collective-permute-start(bf16[24,72,128]{2,1,0:T(8,128)(2,1)S(1)} %get-tuple-element.129), channel_id=1, source_target_pairs={{0,240},{16,0},{32,16},{48,32},{64,48},{80,64},{96,80},{112,96},{1... | collective-permute-start | bytes 1327112 | tf_op jit(solution)/shard_map/ppermute | solution.py:1162
  147.3 5.9 %collective-permute-start.29 = (bf16[40,256]{1,0:T(8,128)(2,1)S(1)}, bf16[40,256]{1,0:T(8,128)(2,1)S(1)}, u32[]{:S(2)}, u32[]{:S(2)}) collective-permute-start(bf16[40,256]{1,0:T(8,128)(2,1)S(1)} %select_convert_fusion.1), channel_id=1, source_target_pairs={{0,128},{4,132},{8,136},{12,140},{16,144},{20,148},{24,152},{28,15... | collective-permute-start | bytes 61448 | tf_op jit(solution)/shard_map/ppermute | solution.py:1182
  153.2 1.6 unpack_mixed.1
  154.8 6.7 %tap_sums.1 = f32[64,256]{1,0:T(8,128)S(1)} custom-call(bf16[3,576,512]{2,1,0:T(8,128)(2,1)} %get-tuple-element.138.grad_ref, bf16[60,80,512]{2,1,0:T(8,128)(2,1)} %get-tuple-element.139.ext_ref, f32[1,256]{1,0:T(1,128)S(1)} %get-tuple-element.140.sum_ref), custom_call_target="tpu_custom_call" | custom-call | flops 15925248 | bytes 15000000 | tf_op jit(solution)/shard_map/tap_sums/pallas_call | solution.py:821
  162.3 2.6 %middle.1.center_ref = f32[24,24,512]{2,1,0:T(8,128)S(1)} custom-call(s32[4]{0:T(128)S(1)} %pad_add_fusion.id_ref.refs_0_, bf16[24,24,512]{2,1,0:T(8,128)(2,1)} %get-tuple-element.130.center_ref, bf16[18,60,512]{2,1,0:T(8,128)(2,1)} %copy-done.1, bf16[18,24,512]{2,1,0:T(8,128)(2,1)} %copy-done.18), custom_call_target="tpu_custom_call" | custom-call | flops 294912 | bytes 4000000 | tf_op jit(solution)/shard_map/middle/pallas_call | solution.py:911
  165.0 5.0 %collective-permute-start.33 = (bf16[104,256]{1,0:T(8,128)(2,1)S(1)}, bf16[104,256]{1,0:T(8,128)(2,1)S(1)}, u32[]{:S(2)}, u32[]{:S(2)}) collective-permute-start(bf16[104,256]{1,0:T(8,128)(2,1)S(1)} %pad_maximum_fusion.3), channel_id=1, source_target_pairs={{0,128},{4,132},{8,136},{12,140},{16,144},{20,148},{24,152},{28,15... | collective-permute-start | bytes 159752 | tf_op jit(solution)/shard_map/ppermute | solution.py:1182
  170.0 2.3 %collective-permute-done.33 = bf16[104,256]{1,0:T(8,128)(2,1)S(1)} collective-permute-done((bf16[104,256]{1,0:T(8,128)(2,1)S(1)}, bf16[104,256]{1,0:T(8,128)(2,1)S(1)}, u32[]{:S(2)}, u32[]{:S(2)}) %collective-permute-start.33) | collective-permute-done | bytes 53280 | tf_op jit(solution)/shard_map/ppermute | solution.py:1182
  173.5 5.2 %collective-permute-done.34 = bf16[144,256]{1,0:T(8,128)(2,1)S(1)} collective-permute-done((bf16[144,256]{1,0:T(8,128)(2,1)S(1)}, bf16[144,256]{1,0:T(8,128)(2,1)S(1)}, u32[]{:S(2)}, u32[]{:S(2)}) %collective-permute-start.34) | collective-permute-done | bytes 73760 | tf_op jit(solution)/shard_map/ppermute | solution.py:1182
  178.8 3.6 %collective-permute-done.35 = bf16[224,256]{1,0:T(8,128)(2,1)S(1)} collective-permute-done((bf16[224,256]{1,0:T(8,128)(2,1)S(1)}, bf16[224,256]{1,0:T(8,128)(2,1)S(1)}, u32[]{:S(2)}, u32[]{:S(2)}) %collective-permute-start.35) | collective-permute-done | bytes 114720 | tf_op jit(solution)/shard_map/ppermute | solution.py:1182
  182.7 2.2 %collective-permute-start.37 = (bf16[384,256]{1,0:T(8,128)(2,1)S(1)}, bf16[384,256]{1,0:T(8,128)(2,1)S(1)}, u32[]{:S(2)}, u32[]{:S(2)}) collective-permute-start(bf16[384,256]{1,0:T(8,128)(2,1)S(1)} %pad_maximum_fusion), channel_id=1, source_target_pairs={{0,8},{4,12},{8,0},{12,4},{16,24},{20,28},{24,16},{28,20},{32,40},... | collective-permute-start | bytes 589832 | tf_op jit(solution)/shard_map/ppermute | solution.py:1182
  185.9 8.5 %collective-permute-done.38.three_ref = bf16[384,256]{1,0:T(8,128)(2,1)S(1)} collective-permute-done((bf16[384,256]{1,0:T(8,128)(2,1)S(1)}, bf16[384,256]{1,0:T(8,128)(2,1)S(1)}, u32[]{:S(2)}, u32[]{:S(2)}) %collective-permute-start.38) | collective-permute-done | bytes 196640 | tf_op jit(solution)/shard_map/ppermute | solution.py:1182
  195.1 1.6 collective-permute-start.39
  196.7 1.8 collective-permute-done.39.refs_2_.refs_4_
  198.4 3.5 %last_stage.1 = (f32[5,512,256]{2,1,0:T(8,128)}, f32[5,64,256]{2,1,0:T(8,128)}, f32[3,9,512]{2,1,0:T(8,128)S(1)}, f32[1,512]{1,0:T(1,128)S(1)}) custom-call(s32[4]{0:T(128)S(1)} %pad_add_fusion.id_ref.refs_0_, bf16[1344,256]{1,0:T(8,128)(2,1)S(1)} %get-tuple-element.141.refs_1_, bf16[1344,256]{1,0:T(8,128)(2,1)S(1)} %collective-permute-done.39.refs_2_.refs_4_, ...), custom_call_target="tpu_custom_call" | custom-call | flops 1048576 | bytes 5000000 | tf_op jit(solution)/shard_map/last_stage/pallas_call | solution.py:1126
  202.6 1.6 finish.1
  (117 shorter events, 22.1 us)
Async XLA Ops:
  3.6 8.1 %collective-permute-start.2 = (f32[4,128]{1,0:T(4,128)S(1)}, f32[4,128]{1,0:T(4,128)S(1)}, u32[]{:S(2)}, u32[]{:S(2)}) collective-permute-start(f32[4,128]{1,0:T(4,128)S(1)} %bitcast.12), channel_id=1, source_target_pairs={{0,4},{4,0},{8,12},{12,8},{16,20},{20,16},{24,28},{28,24},{32,36},... | collective-permute-start | bytes 6152 | tf_op jit(solution)/shard_map/ppermute | solution.py:1182
  6.9 26.4 %collective-permute-start = (bf16[24,72,128]{2,1,0:T(8,128)(2,1)}, bf16[24,72,128]{2,1,0:T(8,128)(2,1)S(1)}, u32[]{:S(2)}, u32[]{:S(2)}) collective-permute-start(bf16[24,72,128]{2,1,0:T(8,128)(2,1)} %get-tuple-element.77), channel_id=1, source_target_pairs={{0,16},{16,32},{32,48},{48,64},{64,80},{80,96},{96,112},{112,128},... | collective-permute-start | bytes 1327112 | tf_op jit(solution)/shard_map/ppermute | solution.py:1162
  6.9 26.4 %collective-permute-start.1 = (bf16[24,72,128]{2,1,0:T(8,128)(2,1)}, bf16[24,72,128]{2,1,0:T(8,128)(2,1)S(1)}, u32[]{:S(2)}, u32[]{:S(2)}) collective-permute-start(bf16[24,72,128]{2,1,0:T(8,128)(2,1)} %get-tuple-element.78), channel_id=1, source_target_pairs={{0,240},{16,0},{32,16},{48,32},{64,48},{80,64},{96,80},{112,96},{1... | collective-permute-start | bytes 1327112 | tf_op jit(solution)/shard_map/ppermute | solution.py:1162
  13.9 28.7 %copy-start.11 = (bf16[5,64,256]{2,1,0:T(8,128)(2,1)S(1)}, bf16[5,64,256]{2,1,0:T(8,128)(2,1)}, u32[]{:S(2)}) copy-start(bf16[5,64,256]{2,1,0:T(8,128)(2,1)} %weight_own.1) | copy-start | bytes 491524
  13.9 31.9 %copy-start.19 = (f32[3,9,512]{2,0,1:T(4,128)S(1)}, f32[3,9,512]{2,0,1:T(4,128)}, u32[]{:S(2)}) copy-start(f32[3,9,512]{2,0,1:T(4,128)} %param.6) | copy-start | bytes 165892
  13.9 35.3 %copy-start = (bf16[5,512,256]{2,1,0:T(8,128)(2,1)S(1)}, bf16[5,512,256]{2,1,0:T(8,128)(2,1)}, u32[]{:S(2)}) copy-start(bf16[5,512,256]{2,1,0:T(8,128)(2,1)} %refs_5_.1) | copy-start | bytes 3932164
  13.9 35.3 %copy-start.12 = (bf16[24,24,64]{2,1,0:T(8,128)(2,1)S(1)}, bf16[24,24,64]{2,1,0:T(8,128)(2,1)}, u32[]{:S(2)}) copy-start(bf16[24,24,64]{2,1,0:T(8,128)(2,1)} %cot_ref.1) | copy-start | bytes 221188
  13.9 20.0 %collective-permute-start.4 = (bf16[18,24,512]{2,1,0:T(8,128)(2,1)}, bf16[18,24,512]{2,1,0:T(8,128)(2,1)S(1)}, u32[]{:S(2)}, u32[]{:S(2)}) collective-permute-start(bf16[18,24,512]{2,1,0:T(8,128)(2,1)} %get-tuple-element.156), channel_id=1, source_target_pairs={{4,8},{8,4},{5,9},{9,5},{6,10},{10,6},{7,11},{11,7},{20,24},{24,20... | collective-permute-start | bytes 1327112 | tf_op jit(solution)/shard_map/ppermute | solution.py:1173
  18.8 15.1 %collective-permute-start.3 = (bf16[18,24,512]{2,1,0:T(8,128)(2,1)}, bf16[18,24,512]{2,1,0:T(8,128)(2,1)S(1)}, u32[]{:S(2)}, u32[]{:S(2)}) collective-permute-start(bf16[18,24,512]{2,1,0:T(8,128)(2,1)} %get-tuple-element.157), channel_id=1, source_target_pairs={{0,4},{4,0},{8,12},{12,8},{1,5},{5,1},{9,13},{13,9},{2,6},{6,2},{1... | collective-permute-start | bytes 1327112 | tf_op jit(solution)/shard_map/ppermute | solution.py:1167
  18.9 2.8 %collective-permute-start.5 = (f32[4,128]{1,0:T(4,128)S(1)}, f32[4,128]{1,0:T(4,128)S(1)}, u32[]{:S(2)}, u32[]{:S(2)}) collective-permute-start(f32[4,128]{1,0:T(4,128)S(1)} %add.58), channel_id=1, source_target_pairs={{0,32},{4,36},{8,40},{12,44},{16,48},{20,52},{24,56},{28,60},{32,0... | collective-permute-start | bytes 6152 | tf_op jit(solution)/shard_map/ppermute | solution.py:1182
  21.8 6.3 %collective-permute-start.6 = (f32[4,128]{1,0:T(4,128)S(1)}, f32[4,128]{1,0:T(4,128)S(1)}, u32[]{:S(2)}, u32[]{:S(2)}) collective-permute-start(f32[4,128]{1,0:T(4,128)S(1)} %add.60), channel_id=1, source_target_pairs={{0,128},{4,132},{8,136},{12,140},{16,144},{20,148},{24,152},{28,15... | collective-permute-start | bytes 6152 | tf_op jit(solution)/shard_map/ppermute | solution.py:1182
  28.1 5.1 %collective-permute-start.7 = (f32[4,128]{1,0:T(4,128)S(1)}, f32[4,128]{1,0:T(4,128)S(1)}, u32[]{:S(2)}, u32[]{:S(2)}) collective-permute-start(f32[4,128]{1,0:T(4,128)S(1)} %add.61), channel_id=1, source_target_pairs={{0,16},{4,20},{8,24},{12,28},{16,0},{20,4},{24,8},{28,12},{32,48},... | collective-permute-start | bytes 6152 | tf_op jit(solution)/shard_map/ppermute | solution.py:1182
  33.2 24.1 %copy-start.2 = (bf16[24,72,128]{2,1,0:T(8,128)(2,1)}, bf16[24,72,128]{2,1,0:T(8,128)(2,1)S(1)}, u32[]{:S(2)}) copy-start(bf16[24,72,128]{2,1,0:T(8,128)(2,1)S(1)} %collective-permute-done.left_ref) | copy-start | bytes 1327108
  33.2 24.1 %copy-start.3 = (bf16[24,72,128]{2,1,0:T(8,128)(2,1)}, bf16[24,72,128]{2,1,0:T(8,128)(2,1)S(1)}, u32[]{:S(2)}) copy-start(bf16[24,72,128]{2,1,0:T(8,128)(2,1)S(1)} %collective-permute-done.1.right_ref) | copy-start | bytes 1327108
  33.9 23.5 %copy-start.4 = (bf16[18,24,512]{2,1,0:T(8,128)(2,1)}, bf16[18,24,512]{2,1,0:T(8,128)(2,1)S(1)}, u32[]{:S(2)}) copy-start(bf16[18,24,512]{2,1,0:T(8,128)(2,1)S(1)} %collective-permute-done.4.refs_1_.bottom_ref) | copy-start | bytes 1327108
  33.9 23.5 %copy-start.5 = (bf16[18,24,512]{2,1,0:T(8,128)(2,1)}, bf16[18,24,512]{2,1,0:T(8,128)(2,1)S(1)}, u32[]{:S(2)}) copy-start(bf16[18,24,512]{2,1,0:T(8,128)(2,1)S(1)} %collective-permute-done.3.refs_0_.top_ref) | copy-start | bytes 1327108
  34.6 14.6 %collective-permute-start.8 = (bf16[36,72,128]{2,1,0:T(8,128)(2,1)S(1)}, bf16[36,72,128]{2,1,0:T(8,128)(2,1)S(1)}, u32[]{:S(2)}, u32[]{:S(2)}) collective-permute-start(bf16[36,72,128]{2,1,0:T(8,128)(2,1)S(1)} %get-tuple-element.82), channel_id=1, source_target_pairs={{0,4},{4,0},{8,12},{12,8},{1,5},{5,1},{9,13},{13,9},{2,6},{6,2},{1... | collective-permute-start | bytes 1990664 | tf_op jit(solution)/shard_map/ppermute | solution.py:1167
  34.9 14.3 %collective-permute-start.9 = (bf16[36,72,128]{2,1,0:T(8,128)(2,1)S(1)}, bf16[36,72,128]{2,1,0:T(8,128)(2,1)S(1)}, u32[]{:S(2)}, u32[]{:S(2)}) collective-permute-start(bf16[36,72,128]{2,1,0:T(8,128)(2,1)S(1)} %get-tuple-element.83), channel_id=1, source_target_pairs={{4,8},{8,4},{5,9},{9,5},{6,10},{10,6},{7,11},{11,7},{20,24},{24,20... | collective-permute-start | bytes 1990664 | tf_op jit(solution)/shard_map/ppermute | solution.py:1173
  39.1 3.6 %collective-permute-start.10 = (f32[4,128]{1,0:T(4,128)S(1)}, f32[4,128]{1,0:T(4,128)S(1)}, u32[]{:S(2)}, u32[]{:S(2)}) collective-permute-start(f32[4,128]{1,0:T(4,128)S(1)} %get-tuple-element.84), channel_id=1, source_target_pairs={{0,64},{4,68},{8,72},{12,76},{16,80},{20,84},{24,88},{28,92},{32,9... | collective-permute-start | bytes 6152 | tf_op jit(solution)/shard_map/ppermute | solution.py:1182
  42.7 4.0 %collective-permute-start.11 = (f32[4,128]{1,0:T(4,128)S(1)}, f32[4,128]{1,0:T(4,128)S(1)}, u32[]{:S(2)}, u32[]{:S(2)}) collective-permute-start(f32[4,128]{1,0:T(4,128)S(1)} %add.63), channel_id=1, source_target_pairs={{0,8},{4,12},{8,0},{12,4},{16,24},{20,28},{24,16},{28,20},{32,40},... | collective-permute-start | bytes 6152 | tf_op jit(solution)/shard_map/ppermute | solution.py:1182
  42.7 14.7 %collective-permute-start.13 = (bf16[5,64,256]{2,1,0:T(8,128)(2,1)S(1)}, bf16[5,64,256]{2,1,0:T(8,128)(2,1)S(1)}, u32[]{:S(2)}, u32[]{:S(2)}) collective-permute-start(bf16[5,64,256]{2,1,0:T(8,128)(2,1)S(1)} %copy-done.11), channel_id=1, source_target_pairs={{0,2},{1,3},{2,0},{3,1},{4,6},{5,7},{6,4},{7,5},{8,10},{9,11},{10,... | collective-permute-start | bytes 491528 | tf_op jit(solution)/shard_map/ppermute | solution.py:1162
  45.5 11.9 %collective-permute-start.12 = (bf16[5,64,256]{2,1,0:T(8,128)(2,1)S(1)}, bf16[5,64,256]{2,1,0:T(8,128)(2,1)S(1)}, u32[]{:S(2)}, u32[]{:S(2)}) collective-permute-start(bf16[5,64,256]{2,1,0:T(8,128)(2,1)S(1)} %copy-done.11), channel_id=1, source_target_pairs={{0,1},{1,2},{2,3},{3,0},{4,5},{5,6},{6,7},{7,4},{8,9},{9,10},{10,1... | collective-permute-start | bytes 491528 | tf_op jit(solution)/shard_map/ppermute | solution.py:1162
  46.7 10.7 %collective-permute-start.14 = (bf16[5,64,256]{2,1,0:T(8,128)(2,1)S(1)}, bf16[5,64,256]{2,1,0:T(8,128)(2,1)S(1)}, u32[]{:S(2)}, u32[]{:S(2)}) collective-permute-start(bf16[5,64,256]{2,1,0:T(8,128)(2,1)S(1)} %copy-done.11), channel_id=1, source_target_pairs={{0,3},{1,0},{2,1},{3,2},{4,7},{5,4},{6,5},{7,6},{8,11},{9,8},{10,9... | collective-permute-start | bytes 491528 | tf_op jit(solution)/shard_map/ppermute | solution.py:1162
  57.4 10.4 %collective-permute-start.15 = (bf16[160,1024]{1,0:T(8,128)(2,1)S(1)}, bf16[160,1024]{1,0:T(8,128)(2,1)S(1)}, u32[]{:S(2)}, u32[]{:S(2)}) collective-permute-start(bf16[160,1024]{1,0:T(8,128)(2,1)S(1)} %get-tuple-element.89), channel_id=1, source_target_pairs={{0,1},{1,2},{2,3},{3,0},{4,5},{5,6},{6,7},{7,4},{8,9},{9,10},{10,1... | collective-permute-start | bytes 983048 | tf_op jit(solution)/shard_map/ppermute | solution.py:1162
  57.9 15.6 %collective-permute-start.16 = (bf16[160,1024]{1,0:T(8,128)(2,1)S(1)}, bf16[160,1024]{1,0:T(8,128)(2,1)S(1)}, u32[]{:S(2)}, u32[]{:S(2)}) collective-permute-start(bf16[160,1024]{1,0:T(8,128)(2,1)S(1)} %get-tuple-element.90), channel_id=1, source_target_pairs={{0,2},{1,3},{2,0},{3,1},{4,6},{5,7},{6,4},{7,5},{8,10},{9,11},{10,... | collective-permute-start | bytes 983048 | tf_op jit(solution)/shard_map/ppermute | solution.py:1162
  60.4 14.6 %collective-permute-start.17 = (bf16[160,1024]{1,0:T(8,128)(2,1)S(1)}, bf16[160,1024]{1,0:T(8,128)(2,1)S(1)}, u32[]{:S(2)}, u32[]{:S(2)}) collective-permute-start(bf16[160,1024]{1,0:T(8,128)(2,1)S(1)} %get-tuple-element.91), channel_id=1, source_target_pairs={{0,3},{1,0},{2,1},{3,2},{4,7},{5,4},{6,5},{7,6},{8,11},{9,8},{10,9... | collective-permute-start | bytes 983048 | tf_op jit(solution)/shard_map/ppermute | solution.py:1162
  77.7 13.2 %collective-permute-start.18 = (bf16[224,1024]{1,0:T(8,128)(2,1)S(1)}, bf16[224,1024]{1,0:T(8,128)(2,1)S(1)}, u32[]{:S(2)}, u32[]{:S(2)}) collective-permute-start(bf16[224,1024]{1,0:T(8,128)(2,1)S(1)} %get-tuple-element.101), channel_id=1, source_target_pairs={{0,1},{1,2},{2,3},{3,0},{4,5},{5,6},{6,7},{7,4},{8,9},{9,10},{10,1... | collective-permute-start | bytes 1376264 | tf_op jit(solution)/shard_map/ppermute | solution.py:1162
  80.1 22.2 %collective-permute-start.19 = (bf16[224,1024]{1,0:T(8,128)(2,1)S(1)}, bf16[224,1024]{1,0:T(8,128)(2,1)S(1)}, u32[]{:S(2)}, u32[]{:S(2)}) collective-permute-start(bf16[224,1024]{1,0:T(8,128)(2,1)S(1)} %get-tuple-element.102), channel_id=1, source_target_pairs={{0,2},{1,3},{2,0},{3,1},{4,6},{5,7},{6,4},{7,5},{8,10},{9,11},{10,... | collective-permute-start | bytes 1376264 | tf_op jit(solution)/shard_map/ppermute | solution.py:1162
  82.3 20.0 %collective-permute-start.20 = (bf16[224,1024]{1,0:T(8,128)(2,1)S(1)}, bf16[224,1024]{1,0:T(8,128)(2,1)S(1)}, u32[]{:S(2)}, u32[]{:S(2)}) collective-permute-start(bf16[224,1024]{1,0:T(8,128)(2,1)S(1)} %get-tuple-element.103), channel_id=1, source_target_pairs={{0,3},{1,0},{2,1},{3,2},{4,7},{5,4},{6,5},{7,6},{8,11},{9,8},{10,9... | collective-permute-start | bytes 1376264 | tf_op jit(solution)/shard_map/ppermute | solution.py:1162
  105.5 3.0 %collective-permute-start.21 = (bf16[1024,256]{1,0:T(8,128)(2,1)S(1)}, bf16[1024,256]{1,0:T(8,128)(2,1)S(1)}, u32[]{:S(2)}, u32[]{:S(2)}) collective-permute-start(bf16[1024,256]{1,0:T(8,128)(2,1)S(1)} %bitcast.14), channel_id=1, source_target_pairs={{0,4},{4,0},{8,12},{12,8},{16,20},{20,16},{24,28},{28,24},{32,36},... | collective-permute-start | bytes 1572872 | tf_op jit(solution)/shard_map/ppermute | solution.py:1182
  109.1 11.8 %collective-permute-start.22 = (bf16[320,256]{1,0:T(8,128)(2,1)S(1)}, bf16[320,256]{1,0:T(8,128)(2,1)S(1)}, u32[]{:S(2)}, u32[]{:S(2)}) collective-permute-start(bf16[320,256]{1,0:T(8,128)(2,1)S(1)} %get-tuple-element.109), channel_id=1, source_target_pairs={{0,16},{4,20},{8,24},{12,28},{16,0},{20,4},{24,8},{28,12},{32,48},... | collective-permute-start | bytes 491528 | tf_op jit(solution)/shard_map/ppermute | solution.py:1182
  109.2 11.7 %collective-permute-start.23 = (bf16[320,256]{1,0:T(8,128)(2,1)S(1)}, bf16[320,256]{1,0:T(8,128)(2,1)S(1)}, u32[]{:S(2)}, u32[]{:S(2)}) collective-permute-start(bf16[320,256]{1,0:T(8,128)(2,1)S(1)} %get-tuple-element.110), channel_id=1, source_target_pairs={{0,8},{4,12},{8,0},{12,4},{16,24},{20,28},{24,16},{28,20},{32,40},... | collective-permute-start | bytes 491528 | tf_op jit(solution)/shard_map/ppermute | solution.py:1182
  112.7 10.2 %collective-permute-start.24 = (bf16[320,256]{1,0:T(8,128)(2,1)S(1)}, bf16[320,256]{1,0:T(8,128)(2,1)S(1)}, u32[]{:S(2)}, u32[]{:S(2)}) collective-permute-start(bf16[320,256]{1,0:T(8,128)(2,1)S(1)} %get-tuple-element.111), channel_id=1, source_target_pairs={{0,24},{4,28},{8,16},{12,20},{16,8},{20,12},{24,0},{28,4},{32,56},... | collective-permute-start | bytes 491528 | tf_op jit(solution)/shard_map/ppermute | solution.py:1182
  124.2 16.9 %collective-permute-start.27 = (bf16[18,60,512]{2,1,0:T(8,128)(2,1)}, bf16[18,60,512]{2,1,0:T(8,128)(2,1)S(1)}, u32[]{:S(2)}, u32[]{:S(2)}) collective-permute-start(bf16[18,60,512]{2,1,0:T(8,128)(2,1)} %get-tuple-element.123), channel_id=1, source_target_pairs={{0,4},{4,0},{8,12},{12,8},{1,5},{5,1},{9,13},{13,9},{2,6},{6,2},{1... | collective-permute-start | bytes 3317768 | tf_op jit(solution)/shard_map/ppermute | solution.py:1167
  125.4 4.4 %collective-permute-start.25 = (bf16[160,256]{1,0:T(8,128)(2,1)}, bf16[160,256]{1,0:T(8,128)(2,1)}, u32[]{:S(2)}, u32[]{:S(2)}) collective-permute-start(bf16[160,256]{1,0:T(8,128)(2,1)} %get-tuple-element.120), channel_id=1, source_target_pairs={{0,32},{4,36},{8,40},{12,44},{16,48},{20,52},{24,56},{28,60},{32,0... | collective-permute-start | bytes 245768 | tf_op jit(solution)/shard_map/ppermute | solution.py:1182
  126.6 14.5 %collective-permute-start.28 = (bf16[18,36,512]{2,1,0:T(8,128)(2,1)}, bf16[18,36,512]{2,1,0:T(8,128)(2,1)S(1)}, u32[]{:S(2)}, u32[]{:S(2)}) collective-permute-start(bf16[18,36,512]{2,1,0:T(8,128)(2,1)} %copy-done.15), channel_id=1, source_target_pairs={{4,8},{8,4},{5,9},{9,5},{6,10},{10,6},{7,11},{11,7},{20,24},{24,20... | collective-permute-start | bytes 1990664 | tf_op jit(solution)/shard_map/ppermute | solution.py:1173
  131.3 7.2 %collective-permute-start.26 = (bf16[80,256]{1,0:T(8,128)(2,1)S(1)}, bf16[80,256]{1,0:T(8,128)(2,1)S(1)}, u32[]{:S(2)}, u32[]{:S(2)}) collective-permute-start(bf16[80,256]{1,0:T(8,128)(2,1)S(1)} %select_convert_fusion), channel_id=1, source_target_pairs={{0,64},{4,68},{8,72},{12,76},{16,80},{20,84},{24,88},{28,92},{32,9... | collective-permute-start | bytes 122888 | tf_op jit(solution)/shard_map/ppermute | solution.py:1182
  134.2 27.4 %collective-permute-start.32 = (bf16[18,24,512]{2,1,0:T(8,128)(2,1)}, bf16[18,24,512]{2,1,0:T(8,128)(2,1)S(1)}, u32[]{:S(2)}, u32[]{:S(2)}) collective-permute-start(bf16[18,24,512]{2,1,0:T(8,128)(2,1)} %copy-done.16), channel_id=1, source_target_pairs={{4,8},{8,4},{5,9},{9,5},{6,10},{10,6},{7,11},{11,7},{20,24},{24,20... | collective-permute-start | bytes 1327112 | tf_op jit(solution)/shard_map/ppermute | solution.py:1173
  143.4 21.6 %collective-permute-start.30 = (bf16[24,72,128]{2,1,0:T(8,128)(2,1)S(1)}, bf16[24,72,128]{2,1,0:T(8,128)(2,1)S(1)}, u32[]{:S(2)}, u32[]{:S(2)}) collective-permute-start(bf16[24,72,128]{2,1,0:T(8,128)(2,1)S(1)} %get-tuple-element.128), channel_id=1, source_target_pairs={{0,16},{16,32},{32,48},{48,64},{64,80},{80,96},{96,112},{112,128},... | collective-permute-start | bytes 1327112 | tf_op jit(solution)/shard_map/ppermute | solution.py:1162
  143.7 21.3 %collective-permute-start.31 = (bf16[24,72,128]{2,1,0:T(8,128)(2,1)S(1)}, bf16[24,72,128]{2,1,0:T(8,128)(2,1)S(1)}, u32[]{:S(2)}, u32[]{:S(2)}) collective-permute-start(bf16[24,72,128]{2,1,0:T(8,128)(2,1)S(1)} %get-tuple-element.129), channel_id=1, source_target_pairs={{0,240},{16,0},{32,16},{48,32},{64,48},{80,64},{96,80},{112,96},{1... | collective-permute-start | bytes 1327112 | tf_op jit(solution)/shard_map/ppermute | solution.py:1162
  147.3 17.6 %collective-permute-start.29 = (bf16[40,256]{1,0:T(8,128)(2,1)S(1)}, bf16[40,256]{1,0:T(8,128)(2,1)S(1)}, u32[]{:S(2)}, u32[]{:S(2)}) collective-permute-start(bf16[40,256]{1,0:T(8,128)(2,1)S(1)} %select_convert_fusion.1), channel_id=1, source_target_pairs={{0,128},{4,132},{8,136},{12,140},{16,144},{20,148},{24,152},{28,15... | collective-permute-start | bytes 61448 | tf_op jit(solution)/shard_map/ppermute | solution.py:1182
  165.0 7.4 %collective-permute-start.33 = (bf16[104,256]{1,0:T(8,128)(2,1)S(1)}, bf16[104,256]{1,0:T(8,128)(2,1)S(1)}, u32[]{:S(2)}, u32[]{:S(2)}) collective-permute-start(bf16[104,256]{1,0:T(8,128)(2,1)S(1)} %pad_maximum_fusion.3), channel_id=1, source_target_pairs={{0,128},{4,132},{8,136},{12,140},{16,144},{20,148},{24,152},{28,15... | collective-permute-start | bytes 159752 | tf_op jit(solution)/shard_map/ppermute | solution.py:1182
  172.4 6.3 %collective-permute-start.34 = (bf16[144,256]{1,0:T(8,128)(2,1)S(1)}, bf16[144,256]{1,0:T(8,128)(2,1)S(1)}, u32[]{:S(2)}, u32[]{:S(2)}) collective-permute-start(bf16[144,256]{1,0:T(8,128)(2,1)S(1)} %pad_maximum_fusion.2), channel_id=1, source_target_pairs={{0,64},{4,68},{8,72},{12,76},{16,80},{20,84},{24,88},{28,92},{32,9... | collective-permute-start | bytes 221192 | tf_op jit(solution)/shard_map/ppermute | solution.py:1182
  178.7 3.7 %collective-permute-start.35 = (bf16[224,256]{1,0:T(8,128)(2,1)S(1)}, bf16[224,256]{1,0:T(8,128)(2,1)S(1)}, u32[]{:S(2)}, u32[]{:S(2)}) collective-permute-start(bf16[224,256]{1,0:T(8,128)(2,1)S(1)} %pad_maximum_fusion.1), channel_id=1, source_target_pairs={{0,32},{4,36},{8,40},{12,44},{16,48},{20,52},{24,56},{28,60},{32,0... | collective-permute-start | bytes 344072 | tf_op jit(solution)/shard_map/ppermute | solution.py:1182
  182.6 11.9 %collective-permute-start.38 = (bf16[384,256]{1,0:T(8,128)(2,1)S(1)}, bf16[384,256]{1,0:T(8,128)(2,1)S(1)}, u32[]{:S(2)}, u32[]{:S(2)}) collective-permute-start(bf16[384,256]{1,0:T(8,128)(2,1)S(1)} %pad_maximum_fusion), channel_id=1, source_target_pairs={{0,24},{4,28},{8,16},{12,20},{16,8},{20,12},{24,0},{28,4},{32,56},... | collective-permute-start | bytes 589832 | tf_op jit(solution)/shard_map/ppermute | solution.py:1182
  182.7 11.8 %collective-permute-start.37 = (bf16[384,256]{1,0:T(8,128)(2,1)S(1)}, bf16[384,256]{1,0:T(8,128)(2,1)S(1)}, u32[]{:S(2)}, u32[]{:S(2)}) collective-permute-start(bf16[384,256]{1,0:T(8,128)(2,1)S(1)} %pad_maximum_fusion), channel_id=1, source_target_pairs={{0,8},{4,12},{8,0},{12,4},{16,24},{20,28},{24,16},{28,20},{32,40},... | collective-permute-start | bytes 589832 | tf_op jit(solution)/shard_map/ppermute | solution.py:1182
  184.9 9.6 %collective-permute-start.36 = (bf16[384,256]{1,0:T(8,128)(2,1)S(1)}, bf16[384,256]{1,0:T(8,128)(2,1)S(1)}, u32[]{:S(2)}, u32[]{:S(2)}) collective-permute-start(bf16[384,256]{1,0:T(8,128)(2,1)S(1)} %pad_maximum_fusion), channel_id=1, source_target_pairs={{0,16},{4,20},{8,24},{12,28},{16,0},{20,4},{24,8},{28,12},{32,48},... | collective-permute-start | bytes 589832 | tf_op jit(solution)/shard_map/ppermute | solution.py:1182
  195.1 3.4 %collective-permute-start.39 = (bf16[1344,256]{1,0:T(8,128)(2,1)S(1)}, bf16[1344,256]{1,0:T(8,128)(2,1)S(1)}, u32[]{:S(2)}, u32[]{:S(2)}) collective-permute-start(bf16[1344,256]{1,0:T(8,128)(2,1)S(1)} %get-tuple-element.141.refs_1_), channel_id=1, source_target_pairs={{0,4},{4,0},{8,12},{12,8},{16,20},{20,16},{24,28},{28,24},{32,36},... | collective-permute-start | bytes 2064392 | tf_op jit(solution)/shard_map/ppermute | solution.py:1182
  (12 other events, 57.8 us)
